TPU v7x, 256 devices: a whole 4x4x8 slice. The times are simulated.
256 devices in a mesh: dp: 16 (over z, y_hi), seq: 16 (over y_lo, x, core).
Axes of the slice: x: 4, y: 4 (y_hi: 2, y_lo: 2; y = y_hi * 2 + y_lo), z: 8, core: 2. Of those that a mesh axis runs over, the one named last changes fastest.
Arguments:
- frames: bfloat16 [16, 4096, 1536], P('dp', 'seq'), may hold values from -6 to 6
- arrival: int32 [16, 16], replicated, may hold values from 0 to 15, as said below
- lengths: int32 [16], replicated, may hold values from 1024 to 4096, as said below
- attn_gain: float32 [1536], replicated, may hold values from 0.1 to 1.9
- w_qkv: bfloat16 [1536, 4608], P('dp'), may hold values from -8 to 8
- w_out: bfloat16 [1536, 1536], replicated, may hold values from -0.15625 to 0.15625
- conv_gain: float32 [1536], replicated, may hold values from 0.1 to 1.9
- conv_kernel: float32 [31, 1536], replicated, may hold values from -2 to 2
Outputs:
- encoded: bfloat16 [16, 4096, 1536], P('dp', 'seq')
Inputs may be any that keep to these rules, and one draw needn't show every extreme that they name: arrival[s] is a permutation of the 16 data groups for every s. `lengths`: at least one recording fills its whole slot.
All inputs are finite; a program needn't handle non-finite values.
Results may differ from a plain program's by a relative error of at most 0.0085.
Values may be sent and summed in bfloat16 or wider, within the bound.
No kernel may reach another device: no remote copies, remote signals or barrier semaphores. Data moves between devices by JAX's collectives and lax.ppermute only.
A program may use at most 128 MiB of HBM per device.

v0:
```python
import jax
import jax.numpy as jnp
from jax import lax
from jax.sharding import PartitionSpec as P

HEAD = 64
KERNEL = 31
ITERS = 2


def passed_along(value, axis, by):
    size = lax.axis_size(axis)
    pairs = [(i, i + by) for i in range(size) if 0 <= i + by < size]
    return lax.ppermute(value, axis, pairs)


def padded_2(block, sides, width):
    for axis, dim in sides:
        count = lax.axis_size(axis)
        forward = [(i, i + 1) for i in range(count - 1)]
        backward = [(target, source) for source, target in forward]
        low = lax.ppermute(
            lax.slice_in_dim(block, block.shape[dim] - width, None, axis=dim), axis, forward
        )
        high = lax.ppermute(lax.slice_in_dim(block, 0, width, axis=dim), axis, backward)
        block = jnp.concatenate([low, block, high], axis=dim)
    return block


def norm(v):
    mean = jnp.mean(v, axis=-1, keepdims=True)
    var = jnp.mean((v - mean) ** 2, axis=-1, keepdims=True)
    return (v - mean) / jnp.sqrt(var + 1e-05)


def on_device(frames, arrival, lengths, attn_gain, w_qkv, w_out, conv_gain, conv_kernel):
    span = frames.shape[1]
    width = w_out.shape[0]
    heads = width // HEAD
    half = (KERNEL - 1) // 2
    group = lax.axis_index("dp")
    place = lax.axis_index("seq")
    groups = lax.axis_size("dp")
    w_full = lax.all_gather(w_qkv, "dp", axis=0, tiled=True)
    row_here = lax.dynamic_index_in_dim(arrival, place, 0, keepdims=False)
    source = lax.dynamic_index_in_dim(row_here, group, 0, keepdims=False)
    slots = jnp.arange(groups)
    owner = jnp.sum(jnp.where(row_here == group, slots, 0))
    onehot = (slots == owner).astype(jnp.bfloat16)
    packed = onehot[:, None, None] * frames
    received = lax.all_to_all(packed, "dp", split_axis=0, concat_axis=0, tiled=True)
    x = lax.dynamic_index_in_dim(received, source, 0, keepdims=False)
    length = lax.dynamic_index_in_dim(lengths, group, 0, keepdims=False)
    position = place * span + jnp.arange(span)
    own_valid = position < length
    left_valid = jnp.logical_and(position - span < length, place > 0)
    key_valid = jnp.concatenate([left_valid, own_valid])
    valid = own_valid.astype(jnp.float32)
    for step in range(ITERS):
        h = (norm(x.astype(jnp.float32)) * attn_gain).astype(jnp.bfloat16)
        qkv = jnp.dot(h, w_full, preferred_element_type=jnp.float32).astype(jnp.bfloat16)
        query = qkv[:, :width].reshape(span, heads, HEAD)
        pairs = qkv[:, width:]
        left = passed_along(pairs, "seq", 1)
        joined = jnp.concatenate([left, pairs], axis=0)
        keys = joined[:, :width].reshape(2 * span, heads, HEAD)
        values = joined[:, width:].reshape(2 * span, heads, HEAD)
        scores = jnp.einsum(
            "chd,khd->hck", query, keys, preferred_element_type=jnp.float32
        ) * HEAD ** (-0.5)
        scores = jnp.where(key_valid[None, None, :], scores, -1e30)
        top = jnp.max(scores, axis=-1, keepdims=True)
        expo = jnp.exp(scores - top)
        probs = (expo / jnp.sum(expo, axis=-1, keepdims=True)).astype(jnp.bfloat16)
        ctx = jnp.einsum("hck,khd->chd", probs, values, preferred_element_type=jnp.float32)
        ctx = ctx.astype(jnp.bfloat16).reshape(span, width)
        x1 = x.astype(jnp.float32) + jnp.dot(ctx, w_out, preferred_element_type=jnp.float32)
        g = (norm(x1) * conv_gain * valid[:, None]).astype(jnp.bfloat16)
        padded = padded_2(g, (("seq", 0),), half).astype(jnp.float32)
        conv = jnp.zeros_like(x1)
        for tap in range(KERNEL):
            conv = conv + conv_kernel[tap] * padded[tap : tap + span]
        x = ((x1 + jax.nn.silu(conv)) * valid[:, None]).astype(jnp.bfloat16)
    return x[None]


def solution(mesh):
    placed = (P("dp", "seq", None), P(), P(), P(), P("dp", None), P(), P(), P())
    return jax.shard_map(
        on_device, mesh=mesh, in_specs=placed, out_specs=P("dp", "seq", None), check_vma=False
    )
```

profile of v0, /device:TPU:24, one launch (start us, length us, event | category | flops | bytes accessed | tf_op | source)
XLA Modules:
  0.0 592.4 jit_solution(13019606399275503283)
XLA Ops:
  9.2 6.8 %broadcast_multiply_fusion = bf16[16,256,1536]{2,1,0:T(8,128)(2,1)} fusion(bf16[256,1536]{1,0:T(8,128)(2,1)} %bitcast.66, bf16[16]{0:T(256)(128)(2,1)S(1)} %compare_convert_fusion), kind=kLoop, calls=%fused_computation.16 | loop fusion | flops 6291456 | bytes 13369376 | tf_op jit(solution)/shard_map/mul | solution.py:50
  16.1 11.4 %all-to-all-start = ((bf16[16,256,1536]{2,1,0:T(8,128)(2,1)}), bf16[16,256,1536]{2,1,0:T(8,128)(2,1)}, u32[]{:S(2)}, u32[]{:S(2)}) async-start(bf16[16,256,1536]{2,1,0:T(8,128)(2,1)} %broadcast_multiply_fusion), calls=%async_computation | async-start | bytes 25165824 | tf_op jit(solution)/shard_map/all_to_all | solution.py:51
  30.8 328.7 %all-to-all-done = bf16[16,256,1536]{2,1,0:T(8,128)(2,1)} async-done(((bf16[16,256,1536]{2,1,0:T(8,128)(2,1)}), bf16[16,256,1536]{2,1,0:T(8,128)(2,1)}, u32[]{:S(2)}, u32[]{:S(2)}) %all-to-all-start) | async-done | bytes 12582944 | tf_op jit(solution)/shard_map/all_to_all | solution.py:51
  362.3 66.1 %all-gather.2.cloned.1.call-done = bf16[1536,4608]{1,0:T(8,128)(2,1)} async-done(((bf16[96,4608]{1,0:T(8,128)(2,1)}), bf16[1536,4608]{1,0:T(8,128)(2,1)}) %all-gather.2.cloned.1.call-update) | async-done | bytes 14155792 | tf_op jit(solution)/shard_map/all_gather | solution.py:44
  428.4 9.3 %convolution_convert_fusion.1 = bf16[256,4608]{1,0:T(8,128)(2,1)S(1)} fusion(bf16[1536,4608]{1,0:T(8,128)(2,1)} %all-gather.2.cloned.1.call-done, f32[1536]{0:T(1024)S(1)} %copy-done.6, f32[256]{0:T(256)S(1)} %add_sqrt_fusion.3, f32[256]{0:T(256)S(1)} %broadcast_multiply_fusion.4, bf16[16,256,1536]{2,1,0:T(8,128)(2,1)} %all-to-all-done, s32[]{:T(128)S(6)} %select_n.33), kind=kOutput, calls=%fused_computation.11 | convolution fusion | flops 3627024384 | bytes 17309700 | tf_op jit(solution)/shard_map/dot_general | solution.py:61
  445.0 18.4 %collective-permute-done = bf16[256,3072]{1,0:T(8,128)(2,1)} collective-permute-done((bf16[256,3072]{1,0:T(8,128)(2,1)S(1)}, bf16[256,3072]{1,0:T(8,128)(2,1)}, u32[]{:S(2)}, u32[]{:S(2)}) %collective-permute-start) | collective-permute-done | bytes 1572896 | tf_op jit(solution)/shard_map/ppermute | solution.py:14
  463.4 2.7 pad_maximum_fusion.1
  466.1 2.6 copy.15
  470.4 10.4 %fusion.112 = (f32[24,256]{1,0:T(8,128)S(1)}, f32[24,256,512]{2,1,0:T(8,128)}) fusion(pred[512]{0:T(512)(128)(4,1)S(1)} %pad_add_fusion, bf16[256,24,64]{0,2,1:T(8,128)(2,1)} %bitcast.65, bf16[512,24,64]{0,2,1:T(8,128)(2,1)} %bitcast.63), kind=kOutput, calls=%fused_computation.242 | convolution fusion | flops 415236608 | bytes 14967296 | tf_op jit(solution)/shard_map/sub | solution.py:73
  480.8 5.9 %fusion.86 = bf16[24,64,256]{2,1,0:T(8,128)(2,1)S(1)} fusion(bf16[512,24,64]{0,2,1:T(8,128)(2,1)S(1)} %bitcast.61, f32[24,256,512]{2,1,0:T(8,128)} %get-tuple-element.49, f32[24,256]{1,0:T(8,128)S(1)} %get-tuple-element.48), kind=kOutput, calls=%fused_computation.175 | convolution fusion | flops 409337856 | bytes 14966784 | tf_op jit(solution)/shard_map/hck,khd->chd/dot_general | solution.py:75
  486.7 2.6 fusion.113
  492.3 2.6 collective-permute-start.1
  495.2 4.7 collective-permute-done.1
  500.1 8.6 %convert_reduce_fusion = (f32[256]{0:T(256)S(1)}, bf16[256,1536]{1,0:T(8,128)(2,1)S(1)}) fusion(f32[256]{0:T(256)S(1)} %get-tuple-element.38, f32[256,1536]{1,0:T(8,128)S(1)} %get-tuple-element.51, f32[286,1536]{1,0:T(8,128)S(1)} %maximum_convert_fusion, f32[1536]{0:T(1024)S(1)} %get-tuple-element.34, f32[1536]{0:T(1024)S(1)} %get-tuple-element.35, ...), kind=kLoop, calls=%fused_computation.28 | loop fusion | flops 27524864 | bytes 51310592 | tf_op jit(solution)/shard_map/reduce_sum | solution.py:31
  509.0 9.4 %convolution_convert_fusion = bf16[256,4608]{1,0:T(8,128)(2,1)S(1)} fusion(bf16[1536,4608]{1,0:T(8,128)(2,1)} %all-gather.2.cloned.1.call-done, bf16[256,1536]{1,0:T(8,128)(2,1)S(1)} %get-tuple-element.37, f32[256]{0:T(256)S(1)} %add_sqrt_fusion.1, f32[256]{0:T(256)S(1)} %broadcast_multiply_fusion.2, f32[1536]{0:T(1024)S(1)} %copy-done.6), kind=kOutput, calls=%fused_computation.10 | convolution fusion | flops 3627024384 | bytes 17309696 | tf_op jit(solution)/shard_map/dot_general | solution.py:61
  521.7 2.3 copy.19
  524.0 18.5 %collective-permute-done.3 = bf16[256,3072]{1,0:T(8,128)(2,1)} collective-permute-done((bf16[256,3072]{1,0:T(8,128)(2,1)S(1)}, bf16[256,3072]{1,0:T(8,128)(2,1)}, u32[]{:S(2)}, u32[]{:S(2)}) %collective-permute-start.3) | collective-permute-done | bytes 1572896 | tf_op jit(solution)/shard_map/ppermute | solution.py:14
  542.5 3.2 pad_maximum_fusion
  545.8 2.7 copy.18
  550.1 10.4 %fusion.114 = (f32[24,256]{1,0:T(8,128)S(1)}, f32[24,256,512]{2,1,0:T(8,128)}) fusion(pred[512]{0:T(512)(128)(4,1)S(1)} %pad_add_fusion, bf16[256,24,64]{0,2,1:T(8,128)(2,1)} %bitcast.64, bf16[512,24,64]{0,2,1:T(8,128)(2,1)} %bitcast.62), kind=kOutput, calls=%fused_computation.244 | convolution fusion | flops 415236608 | bytes 14967296 | tf_op jit(solution)/shard_map/sub | solution.py:73
  560.5 5.9 %fusion.85 = bf16[24,64,256]{2,1,0:T(8,128)(2,1)S(1)} fusion(bf16[512,24,64]{0,2,1:T(8,128)(2,1)S(1)} %bitcast.60, f32[24,256,512]{2,1,0:T(8,128)} %get-tuple-element.53, f32[24,256]{1,0:T(8,128)S(1)} %get-tuple-element.52), kind=kOutput, calls=%fused_computation.174 | convolution fusion | flops 409337856 | bytes 14966784 | tf_op jit(solution)/shard_map/hck,khd->chd/dot_general | solution.py:75
  570.6 2.4 collective-permute-start.4
  573.0 5.1 collective-permute-done.4
  578.3 7.2 %fusion.99 = bf16[1,256,1536]{2,1,0:T(8,128)(2,1)} fusion(f32[256]{0:T(256)S(1)} %get-tuple-element.38, f32[256,1536]{1,0:T(8,128)S(1)} %get-tuple-element.55, f32[286,1536]{1,0:T(8,128)S(1)} %maximum_convert_fusion.1, f32[1536]{0:T(1024)S(1)} %get-tuple-element.34, f32[1536]{0:T(1024)S(1)} %get-tuple-element.35, f32[1536]{0:T(1024)S(1)} %get-tuple-element.6, ...), kind=kLoop, calls=%fused_computation.186 | loop fusion | flops 26738688 | bytes 51309568 | tf_op jit(solution)/shard_map/broadcast_in_dim | solution.py:84
  (71 shorter events, 28.5 us)
Async XLA Ops:
  6.5 421.9 %all-gather.2.cloned.1.call-start = ((), (), s32[]{:S(2)}) async-start(), calls=%async_computation.1 | async-start | bytes 15040512 | tf_op jit(solution)/shard_map/all_gather | solution.py:44
  16.1 343.4 %all-to-all-start = ((bf16[16,256,1536]{2,1,0:T(8,128)(2,1)}), bf16[16,256,1536]{2,1,0:T(8,128)(2,1)}, u32[]{:S(2)}, u32[]{:S(2)}) async-start(bf16[16,256,1536]{2,1,0:T(8,128)(2,1)} %broadcast_multiply_fusion), calls=%async_computation | async-start | bytes 25165824 | tf_op jit(solution)/shard_map/all_to_all | solution.py:51
  27.5 400.9 %copy-start.6 = (f32[1536]{0:T(1024)S(1)}, f32[1536]{0:T(1024)}, u32[]{:S(2)}) copy-start(f32[1536]{0:T(1024)} %param.11) | copy-start | bytes 18436
  437.7 1.4 copy-start.1
  439.1 2.4 copy-start.7
  439.1 4.4 copy-start.4
  439.3 4.5 slice-start.4
  439.3 24.1 %collective-permute-start = (bf16[256,3072]{1,0:T(8,128)(2,1)S(1)}, bf16[256,3072]{1,0:T(8,128)(2,1)}, u32[]{:S(2)}, u32[]{:S(2)}) collective-permute-start(bf16[256,3072]{1,0:T(8,128)(2,1)S(1)} %slice.451), channel_id=1, source_target_pairs={{0,1},{1,2},{2,3},{3,4},{4,5},{5,6},{6,7},{7,8},{8,9},{9,10},{10,1... | collective-permute-start | bytes 4718600 | tf_op jit(solution)/shard_map/ppermute | solution.py:14
  470.4 10.4 %copy-start.3 = (bf16[512,1536]{0,1:T(8,128)(2,1)S(1)}, bf16[512,1536]{0,1:T(8,128)(2,1)}, u32[]{:S(2)}) copy-start(bf16[512,1536]{0,1:T(8,128)(2,1)} %copy.15) | copy-start | bytes 4718596
  470.4 16.3 %slice-start = ((s8[4718592]{0:T(1024)(128)(4,1)}), s8[524288]{0:T(1024)(128)(4,1)S(1)}, s32[]{:S(2)}) async-start(s8[4718592]{0:T(1024)(128)(4,1)} %bitcast.54), calls=%async_computation.2 | async-start | bytes 1048576
  480.8 6.0 %slice-start.1 = ((s8[4718592]{0:T(1024)(128)(4,1)}), s8[4194304]{0:T(1024)(128)(4,1)S(1)}, s32[]{:S(2)}) async-start(s8[4718592]{0:T(1024)(128)(4,1)} %bitcast.54), calls=%async_computation.3 | async-start | bytes 8388608
  489.3 0.7 copy-start.5
  490.4 4.8 collective-permute-start.2
  492.3 7.5 %collective-permute-start.1 = (bf16[15,1536]{1,0:T(8,128)(2,1)S(1)}, bf16[15,1536]{1,0:T(8,128)(2,1)S(1)}, u32[]{:S(2)}, u32[]{:S(2)}) collective-permute-start(bf16[15,1536]{1,0:T(8,128)(2,1)S(1)} %get-tuple-element.46), channel_id=1, source_target_pairs={{0,1},{1,2},{2,3},{3,4},{4,5},{5,6},{6,7},{7,8},{8,9},{9,10},{10,1... | collective-permute-start | bytes 138248 | tf_op jit(solution)/shard_map/ppermute | solution.py:22
  518.6 24.0 %collective-permute-start.3 = (bf16[256,3072]{1,0:T(8,128)(2,1)S(1)}, bf16[256,3072]{1,0:T(8,128)(2,1)}, u32[]{:S(2)}, u32[]{:S(2)}) collective-permute-start(bf16[256,3072]{1,0:T(8,128)(2,1)S(1)} %slice.488), channel_id=1, source_target_pairs={{0,1},{1,2},{2,3},{3,4},{4,5},{5,6},{6,7},{7,8},{8,9},{9,10},{10,1... | collective-permute-start | bytes 4718600 | tf_op jit(solution)/shard_map/ppermute | solution.py:14
  545.8 2.7 copy-start
  550.1 10.4 %copy-start.2 = (bf16[512,1536]{0,1:T(8,128)(2,1)S(1)}, bf16[512,1536]{0,1:T(8,128)(2,1)}, u32[]{:S(2)}) copy-start(bf16[512,1536]{0,1:T(8,128)(2,1)} %copy.18) | copy-start | bytes 4718596
  550.1 16.3 %slice-start.2 = ((s8[4718592]{0:T(1024)(128)(4,1)}), s8[524288]{0:T(1024)(128)(4,1)S(1)}, s32[]{:S(2)}) async-start(s8[4718592]{0:T(1024)(128)(4,1)} %bitcast.56), calls=%async_computation.4 | async-start | bytes 1048576
  560.5 6.0 %slice-start.3 = ((s8[4718592]{0:T(1024)(128)(4,1)}), s8[4194304]{0:T(1024)(128)(4,1)S(1)}, s32[]{:S(2)}) async-start(s8[4718592]{0:T(1024)(128)(4,1)} %bitcast.56), calls=%async_computation.5 | async-start | bytes 8388608
  568.6 4.3 collective-permute-start.5
  570.6 7.5 %collective-permute-start.4 = (bf16[15,1536]{1,0:T(8,128)(2,1)S(1)}, bf16[15,1536]{1,0:T(8,128)(2,1)S(1)}, u32[]{:S(2)}, u32[]{:S(2)}) collective-permute-start(bf16[15,1536]{1,0:T(8,128)(2,1)S(1)} %get-tuple-element.44), channel_id=1, source_target_pairs={{0,1},{1,2},{2,3},{3,4},{4,5},{5,6},{6,7},{7,8},{8,9},{9,10},{10,1... | collective-permute-start | bytes 138248 | tf_op jit(solution)/shard_map/ppermute | solution.py:22
Sparse Core Ops, SparseCore 0:
  10.0 418.4 all-gather.1
where the time goes:
time: 595 us; the launch traced here: 592 us
  waiting for transfers between devices  442 us (74%)
  matrix products  55.4 us (9%)
  other arithmetic  36.8 us (6%)
  starting transfers between devices  24.7 us (4%)
  local copies, waits for them, and re-layouts  17.5 us (3%)
  between operations  15.7 us (3%)
    all_to_all x1, waiting for transfers between devices, on_device(): lax.all_to_all(packed, 'dp', split_axis=0, concat_axis=0, tiled=True)  329 us
    all_gather x1, waiting for transfers between devices, on_device(): w_full = lax.all_gather(w_qkv, 'dp', axis=0, tiled=True)  66.1 us
    ppermute x2, waiting for transfers between devices, passed_along(): return lax.ppermute(value, axis, pairs)  36.9 us
    sub x2, matrix products, on_device(): expo = jnp.exp(scores - top)  20.8 us
    dot_general x2, matrix products, on_device(): jnp.dot(h, w_full, preferred_element_type=jnp.float32).astype(jnp.bfloat16)  18.7 us
  transfers between devices with their start and end apart: 8, of which 6 were waited for; matrix products, arithmetic and copies ran while one was open for 3% of the time, Pallas kernels for 0%

commit v1 on v0

v1 whole, which is shorter than its diff:
```python
import functools

import jax
import jax.numpy as jnp
from jax import lax
from jax.experimental import pallas as pl
from jax.experimental.pallas import tpu as pltpu
from jax.sharding import Mesh, PartitionSpec as P

HEAD = 64
KERNEL = 31
ITERS = 2
HALO = 16
EPS = 1e-05
DP = ("z", "yh")
SEQ = ("yl", "x", "core")
BF = jnp.bfloat16
F32 = jnp.float32
VMEM = 48 * 1024 * 1024


def params(**kw):
    return pltpu.CompilerParams(vmem_limit_bytes=VMEM, **kw)


def normed(v):
    mean = jnp.mean(v, axis=-1, keepdims=True)
    d = v - mean
    var = jnp.mean(d * d, axis=-1, keepdims=True)
    return d * lax.rsqrt(var + EPS)


def pick_kernel(row_ref, in_ref, out_ref):
    for r in range(in_ref.shape[0]):
        out_ref[r] = in_ref[row_ref[r]]


def pick(chunks, row):
    return pl.pallas_call(
        pick_kernel,
        out_shape=jax.ShapeDtypeStruct(chunks.shape, chunks.dtype),
        in_specs=[
            pl.BlockSpec(memory_space=pltpu.SMEM),
            pl.BlockSpec(memory_space=pltpu.VMEM),
        ],
        out_specs=pl.BlockSpec(memory_space=pltpu.VMEM),
        compiler_params=params(),
        name="pick",
    )(row, chunks)


def head_kernel(x_ref, gain_ref, perm_ref, out_ref):
    h = (normed(x_ref[...].astype(F32)) * gain_ref[...]).astype(BF)
    out_ref[...] = jnp.dot(h, perm_ref[...], preferred_element_type=F32).astype(BF)


def head(x, gain, perm):
    return pl.pallas_call(
        head_kernel,
        out_shape=jax.ShapeDtypeStruct(x.shape, BF),
        compiler_params=params(),
        name="head",
    )(x, gain, perm)


def project_kernel(h_ref, w_ref, out_ref):
    depth = w_ref.shape[0] * w_ref.shape[2]
    w = w_ref[...].reshape(depth, w_ref.shape[3])
    out_ref[0] = jnp.dot(h_ref[...], w, preferred_element_type=F32).astype(BF)


def project(h, w):
    parts, blocks, rows, cols = w.shape
    span, width = h.shape
    return pl.pallas_call(
        project_kernel,
        grid=(blocks,),
        out_shape=jax.ShapeDtypeStruct((blocks, span, cols), BF),
        in_specs=[
            pl.BlockSpec((span, width), lambda b: (0, 0)),
            pl.BlockSpec((parts, 1, rows, cols), lambda b: (0, b, 0, 0)),
        ],
        out_specs=pl.BlockSpec((1, span, cols), lambda b: (b, 0, 0)),
        compiler_params=params(),
        name="project",
    )(h, w)


def attend_kernel(
    left_ref, own_ref, w_ref, wout_ref, x_ref, bias_ref, gain_ref, valid_ref,
    x1_ref, g_ref, acc_ref,
):
    b = pl.program_id(0)
    span = left_ref.shape[0]
    group = wout_ref.shape[0]
    w = w_ref[...].reshape(w_ref.shape[0] * w_ref.shape[2], w_ref.shape[3])
    kv_left = jnp.dot(left_ref[...], w, preferred_element_type=F32).astype(BF)
    lane = lax.broadcasted_iota(jnp.int32, (span, 128), 1)
    low = lane < HEAD
    tag = jnp.where(lane == 0, 1.0, 0.0).astype(BF)
    ones = jnp.ones((2 * span, 128), BF)
    outs = []
    for p in range(group // 128):
        at = 128 * p
        k = jnp.concatenate([kv_left[:, at : at + 128], own_ref[0, :, at : at + 128]], axis=0)
        k = jnp.concatenate([k, bias_ref[...]], axis=1)
        at = group + 128 * p
        v = jnp.concatenate([kv_left[:, at : at + 128], own_ref[0, :, at : at + 128]], axis=0)
        v = jnp.concatenate([v, ones], axis=1)
        at = 2 * group + 128 * p
        q = own_ref[0, :, at : at + 128] * jnp.asarray(HEAD ** (-0.5), BF)
        halves = []
        for mask in (low, jnp.logical_not(low)):
            qh = jnp.where(mask, q, jnp.zeros_like(q))
            qh = jnp.concatenate([qh, tag], axis=1)
            s = lax.dot_general(qh, k, (((1,), (1,)), ((), ())), preferred_element_type=F32)
            top = jnp.max(s, axis=-1, keepdims=True)
            e = jnp.exp(s - top).astype(BF)
            o = jnp.dot(e, v, preferred_element_type=F32)
            halves.append(o[:, :128] / o[:, 128:])
        outs.append(jnp.where(low, halves[0], halves[1]).astype(BF))
    ctx = jnp.concatenate(outs, axis=1)
    part = jnp.dot(ctx, wout_ref[...], preferred_element_type=F32)

    @pl.when(b == 0)
    def _():
        acc_ref[...] = part

    @pl.when(b > 0)
    def _():
        acc_ref[...] += part

    @pl.when(b == pl.num_programs(0) - 1)
    def _():
        x1 = x_ref[...].astype(F32) + acc_ref[...]
        x1_ref[...] = x1
        g_ref[...] = (normed(x1) * gain_ref[...] * valid_ref[...]).astype(BF)


def attend(left, own, w, w_out, x, bias, gain, valid):
    parts, blocks, rows, cols = w.shape
    span, width = x.shape
    group = width // blocks
    whole = lambda *shape: pl.BlockSpec(shape, lambda b: (0,) * len(shape))
    return pl.pallas_call(
        attend_kernel,
        grid=(blocks,),
        out_shape=(
            jax.ShapeDtypeStruct((span, width), F32),
            jax.ShapeDtypeStruct((span, width), BF),
        ),
        in_specs=[
            whole(span, width),
            pl.BlockSpec((1, span, cols), lambda b: (b, 0, 0)),
            pl.BlockSpec((parts, 1, rows, 2 * group), lambda b: (0, b, 0, 0)),
            pl.BlockSpec((group, width), lambda b: (b, 0)),
            whole(span, width),
            whole(2 * span, 128),
            whole(1, width),
            whole(span, 1),
        ],
        out_specs=(whole(span, width), whole(span, width)),
        scratch_shapes=[pltpu.VMEM((span, width), F32)],
        compiler_params=params(),
        name="attend",
    )(left, own, w, w_out, x, bias, gain, valid)


def conv_kernel_body(last, g_ref, low_ref, high_ref, x1_ref, taps_ref, valid_ref, *rest):
    if last:
        x_ref, pad_ref = rest
    else:
        gain_ref, perm_ref, x_ref, h_ref, pad_ref = rest
    span, width = x1_ref.shape
    valid = valid_ref[...]
    for c in range(width // 128):
        cols = pl.ds(128 * c, 128)
        pad_ref[pl.ds(0, HALO), :] = low_ref[:, cols].astype(F32)
        pad_ref[pl.ds(HALO, span), :] = g_ref[:, cols].astype(F32)
        pad_ref[pl.ds(HALO + span, HALO), :] = high_ref[:, cols].astype(F32)
        taps = taps_ref[:, cols]
        y = jnp.zeros((span, 128), F32)
        for r in range(8):
            hits = [(j, (j + 1) // 8) for j in range(KERNEL) if (j + 1) % 8 == r]
            deep = max(m for _, m in hits)
            moved = pad_ref[pl.ds(r, span + 8 * deep), :]
            for j, m in hits:
                y = y + taps[j : j + 1, :] * moved[8 * m : 8 * m + span]
        silu = y / (1.0 + jnp.exp(-y))
        x_ref[:, cols] = ((x1_ref[:, cols] + silu) * valid).astype(BF)
    if not last:
        h = (normed(x_ref[...].astype(F32)) * gain_ref[...]).astype(BF)
        h_ref[...] = jnp.dot(h, perm_ref[...], preferred_element_type=F32).astype(BF)


def convolve(g, low, high, x1, taps, valid, gain, perm, last):
    span, width = x1.shape
    out = [jax.ShapeDtypeStruct((span, width), BF)]
    args = [g, low, high, x1, taps, valid]
    if not last:
        out.append(out[0])
        args += [gain, perm]
    return pl.pallas_call(
        functools.partial(conv_kernel_body, last),
        out_shape=tuple(out),
        scratch_shapes=[pltpu.VMEM((span + 2 * HALO, 128), F32)],
        compiler_params=params(),
        name="convolve",
    )(*args)


def along(value, by):
    size = lax.axis_size(SEQ)
    pairs = [(i, i + by) for i in range(size) if 0 <= i + by < size]
    return lax.ppermute(value, SEQ, pairs)


def weight_blocks(w, frames):
    rows, cols = w.shape
    zs, xs = lax.axis_size("z"), lax.axis_size("x")
    deep = rows // (lax.axis_size("yl") * lax.axis_size("core"))
    width = cols // 3
    group = width // xs
    at = (lax.axis_index("yl") * lax.axis_size("core") + lax.axis_index("core")) * deep
    col = lax.axis_index("x") * group
    own = jnp.concatenate(
        [lax.dynamic_slice(w, (at, part * width + col), (deep, group)) for part in (1, 2, 0)],
        axis=1,
    )
    pieces = {0: own}
    for step in range(1, zs // 2 + 1):
        for k in {step, zs - step}:
            pieces[k] = lax.ppermute(own, "z", [(i, (i + k) % zs) for i in range(zs)])
    stack = jnp.concatenate([pieces[k] for k in range(zs)], axis=0)
    stack, frames = lax.optimization_barrier((stack, frames))
    full = lax.all_gather(stack, ("yh",) + SEQ, axis=0, tiled=True)
    parts = lax.axis_size("yh") * lax.axis_size("yl")
    return full.reshape(parts, xs, -1, 3 * group), frames


def order(width, deep):
    zs = lax.axis_size("z")
    cores = lax.axis_size("core")
    yls = lax.axis_size("yl")
    place = jnp.arange(width)
    i = place % deep
    k = place // deep % zs
    core = place // (deep * zs) % cores
    yl = place // (deep * zs * cores) % yls
    yh = place // (deep * zs * cores * yls)
    z = (lax.axis_index("z") - k) % zs
    feature = (z * lax.axis_size("yh") + yh) * (yls * cores * deep) + (yl * cores + core) * deep + i
    return (jnp.arange(width)[:, None] == feature[None, :]).astype(BF)


def on_device(frames, arrival, lengths, attn_gain, w_qkv, w_out, conv_gain, conv_kernel):
    span = frames.shape[1]
    width = w_out.shape[0]
    group = lax.axis_index(DP)
    place = lax.axis_index(SEQ)
    groups = lax.axis_size(DP)
    w, frames = weight_blocks(w_qkv, frames)
    row_here = lax.dynamic_index_in_dim(arrival, place, 0, keepdims=False)
    chunks = frames.reshape(groups, span // groups, width)
    chunks = lax.all_to_all(chunks, DP, split_axis=0, concat_axis=0, tiled=True)
    chunks = pick(chunks, row_here)
    chunks = lax.all_to_all(chunks, DP, split_axis=0, concat_axis=0, tiled=True)
    x = chunks.reshape(span, width)

    perm = order(width, w_qkv.shape[0] // (lax.axis_size("yl") * lax.axis_size("core")))
    length = lax.dynamic_index_in_dim(lengths, group, 0, keepdims=False)
    position = place * span + jnp.arange(span)
    own_valid = position < length
    left_valid = jnp.logical_and(position - span < length, place > 0)
    key_valid = jnp.concatenate([left_valid, own_valid])
    bias = jnp.where(key_valid, 0.0, -1e30).astype(BF)
    bias = jnp.where(jnp.arange(128)[None, :] == 0, bias[:, None], jnp.zeros((), BF))
    valid = own_valid.astype(F32)[:, None]
    gain_a = attn_gain[None, :]
    gain_c = conv_gain[None, :]
    taps = jnp.pad(conv_kernel, ((0, 1), (0, 0)))

    h = head(x, gain_a, perm)
    for step in range(ITERS):
        last = step == ITERS - 1
        left = along(h, 1)
        own = project(h, w)
        x1, g = attend(left, own, w, w_out, x, bias, gain_c, valid)
        low = along(g[span - HALO :], 1)
        high = along(g[:HALO], -1)
        out = convolve(g, low, high, x1, taps, valid, gain_a, perm, last)
        x = out[0]
        if not last:
            h = out[1]
    return x[None]


def solution(mesh):
    fine = Mesh(mesh.devices.reshape(8, 2, 2, 4, 2), DP + SEQ)
    placed = (P(DP, SEQ, None), P(), P(), P(), P(DP, None), P(), P(), P())
    return jax.shard_map(
        on_device, mesh=fine, in_specs=placed, out_specs=P(DP, SEQ, None), check_vma=False
    )
```

time: 595 us -> 214 us (0.36)
  waiting for transfers between devices: 442 us -> 72.7 us
  Pallas kernels: 0 us -> 62.6 us
  matrix products: 55.4 us -> 0 us
  other arithmetic: 36.8 us -> 5.75 us
  starting transfers between devices: 24.7 us -> 51.7 us
  local copies, waits for them, and re-layouts: 17.5 us -> 5.1 us
    all_to_all x1 -> x2, waiting for transfers between devices: 329 us -> 36.5 us  [on_device(): chunks = lax.all_to_all(chunks, DP, split_axis=0, concat_axis=0, tiled=True)]
    pallas_call x0 -> x8, Pallas kernels: none -> 62.6 us  [the longest x2 26.5 us: attend(): pl.pallas_call(attend_kernel, grid=(blocks,), out_shape=(jax.ShapeDtypeSt...]
    all_gather x1, waiting for transfers between devices: 66.1 us -> 24.2 us  [weight_blocks(): full = lax.all_gather(stack, ('yh',) + SEQ, axis=0, tiled=True)]
    ppermute x6 -> x13, waiting for transfers between devices: 46.7 us -> 11.9 us  [the longest x6 7.51 us: along(): return lax.ppermute(value, SEQ, pairs)]
    dot_general x6 -> x0, matrix products: 34.6 us -> none  [the longest x2 18.7 us: on_device(): jnp.dot(h, w_full, preferred_element_type=jnp.float32).astype(jnp.bfloat16)]
    ppermute x6 -> x13, starting transfers between devices: 13.3 us -> 38.1 us  [the longest x6 19.6 us: along(): return lax.ppermute(value, SEQ, pairs)]
    sub x2 -> x0, matrix products: 20.8 us -> none  [on_device(): expo = jnp.exp(scores - top)]
    slice x15 -> x2, local copies, waits for them, and re-layouts: 13.8 us -> 0.02 us  [on_device(): high = along(g[:HALO], -1)]
  transfers between devices with their start and end apart: 8 -> 16, of which waited for: 6 -> 8; matrix products, arithmetic and copies ran while one was open for 3% -> 3% of each run, Pallas kernels for 0% -> 10%
where the time goes in v1:
time: 214 us; the launch traced here: 212 us
  waiting for transfers between devices  72.7 us (34%)
  Pallas kernels  62.6 us (29%)
  starting transfers between devices  51.7 us (24%)
  between operations  13.7 us (6%)
  other arithmetic  5.75 us (3%)
  local copies, waits for them, and re-layouts  5.1 us (2%)
    all_to_all x2, waiting for transfers between devices, on_device(): chunks = lax.all_to_all(chunks, DP, split_axis=0, concat_axis=0, tiled=True)  36.5 us
    pallas_call x2, Pallas kernels, attend(): pl.pallas_call(attend_kernel, grid=(blocks,), out_shape=(jax.ShapeDtypeSt...  26.5 us
    all_gather x1, waiting for transfers between devices, weight_blocks(): full = lax.all_gather(stack, ('yh',) + SEQ, axis=0, tiled=True)  24.2 us
    ppermute x6, starting transfers between devices, along(): return lax.ppermute(value, SEQ, pairs)  19.6 us
    ppermute x7, starting transfers between devices, weight_blocks(): pieces[k] = lax.ppermute(own, 'z', [(i, (i + k) % zs) for i in range(zs)])  18.5 us
    pallas_call x2, Pallas kernels, project(): pl.pallas_call(project_kernel, grid=(blocks,), out_shape=jax.ShapeDtypeSt...  15.6 us
    pallas_call x2, Pallas kernels, convolve(): pl.pallas_call(functools.partial(conv_kernel_body, last), out_shape=tuple...  14.9 us
    all_to_all x2, starting transfers between devices, on_device(): chunks = lax.all_to_all(chunks, DP, split_axis=0, concat_axis=0, tiled=True)  13.6 us
  transfers between devices with their start and end apart: 16, of which 8 were waited for; matrix products, arithmetic and copies ran while one was open for 3% of the time, Pallas kernels for 10%

profile of v1, /device:TPU:24, one launch (start us, length us, event | category | flops | bytes accessed | tf_op | source)
XLA Modules:
  0.0 211.5 jit_solution(10579778041705318882)
XLA Ops:
  9.3 3.3 %collective-permute-start.1 = (bf16[24,1152]{1,0:T(8,128)(2,1)S(1)}, bf16[24,1152]{1,0:T(8,128)(2,1)S(1)}, u32[]{:S(2)}, u32[]{:S(2)}) collective-permute-start(bf16[24,1152]{1,0:T(8,128)(2,1)S(1)} %get-tuple-element.28), channel_id=1, source_target_pairs={{0,64},{32,96},{64,128},{96,160},{128,192},{160,224},{192,0},{224,... | collective-permute-start | bytes 165896 | tf_op jit(solution)/shard_map/ppermute | solution.py:233
  12.6 4.0 %collective-permute-start.2 = (bf16[24,1152]{1,0:T(8,128)(2,1)S(1)}, bf16[24,1152]{1,0:T(8,128)(2,1)S(1)}, u32[]{:S(2)}, u32[]{:S(2)}) collective-permute-start(bf16[24,1152]{1,0:T(8,128)(2,1)S(1)} %get-tuple-element.28), channel_id=1, source_target_pairs={{0,96},{32,128},{64,160},{96,192},{128,224},{160,0},{192,32},{224,... | collective-permute-start | bytes 165896 | tf_op jit(solution)/shard_map/ppermute | solution.py:233
  17.2 4.9 %collective-permute-start.4 = (bf16[24,1152]{1,0:T(8,128)(2,1)S(1)}, bf16[24,1152]{1,0:T(8,128)(2,1)S(1)}, u32[]{:S(2)}, u32[]{:S(2)}) collective-permute-start(bf16[24,1152]{1,0:T(8,128)(2,1)S(1)} %get-tuple-element.28), channel_id=1, source_target_pairs={{0,160},{32,192},{64,224},{96,0},{128,32},{160,64},{192,96},{224,1... | collective-permute-start | bytes 165896 | tf_op jit(solution)/shard_map/ppermute | solution.py:233
  22.1 2.7 %collective-permute-start.5 = (bf16[24,1152]{1,0:T(8,128)(2,1)S(1)}, bf16[24,1152]{1,0:T(8,128)(2,1)S(1)}, u32[]{:S(2)}, u32[]{:S(2)}) collective-permute-start(bf16[24,1152]{1,0:T(8,128)(2,1)S(1)} %get-tuple-element.28), channel_id=1, source_target_pairs={{0,192},{32,224},{64,0},{96,32},{128,64},{160,96},{192,128},{224,1... | collective-permute-start | bytes 165896 | tf_op jit(solution)/shard_map/ppermute | solution.py:233
  26.0 3.6 %collective-permute-done.4 = bf16[24,1152]{1,0:T(8,128)(2,1)S(1)} collective-permute-done((bf16[24,1152]{1,0:T(8,128)(2,1)S(1)}, bf16[24,1152]{1,0:T(8,128)(2,1)S(1)}, u32[]{:S(2)}, u32[]{:S(2)}) %collective-permute-start.4) | collective-permute-done | bytes 55328 | tf_op jit(solution)/shard_map/ppermute | solution.py:233
  31.2 6.8 %all-to-all-start = ((bf16[16,16,1536]{2,1,0:T(8,128)(2,1)}), bf16[16,16,1536]{2,1,0:T(8,128)(2,1)S(1)}, u32[]{:S(2)}, u32[]{:S(2)}) async-start(bf16[16,16,1536]{2,1,0:T(8,128)(2,1)} %bitcast.13), calls=%async_computation | async-start | bytes 1572864 | tf_op jit(solution)/shard_map/all_to_all | solution.py:265
  38.0 19.9 %all-to-all-done.in_ref = bf16[16,16,1536]{2,1,0:T(8,128)(2,1)S(1)} async-done(((bf16[16,16,1536]{2,1,0:T(8,128)(2,1)}), bf16[16,16,1536]{2,1,0:T(8,128)(2,1)S(1)}, u32[]{:S(2)}, u32[]{:S(2)}) %all-to-all-start) | async-done | bytes 786464 | tf_op jit(solution)/shard_map/all_to_all | solution.py:265
  59.4 6.8 %all-to-all-start.1 = ((bf16[16,16,1536]{2,1,0:T(8,128)(2,1)}), bf16[16,16,1536]{2,1,0:T(8,128)(2,1)S(1)}, u32[]{:S(2)}, u32[]{:S(2)}) async-start(bf16[16,16,1536]{2,1,0:T(8,128)(2,1)} %pick.1), calls=%async_computation.1 | async-start | bytes 1572864 | tf_op jit(solution)/shard_map/all_to_all | solution.py:267
  66.3 4.2 %fusion.perm_ref.rest_1_ = bf16[1536,1536]{1,0:T(8,128)(2,1)} fusion(s32[1536]{0:T(1024)S(1)} %fusion.11), kind=kLoop, calls=%fused_computation.1 | loop fusion | flops 4718592 | bytes 4724736 | tf_op jit(solution)/shard_map/convert_element_type | solution.py:253
  70.5 16.6 %all-to-all-done.1 = bf16[16,16,1536]{2,1,0:T(8,128)(2,1)S(1)} async-done(((bf16[16,16,1536]{2,1,0:T(8,128)(2,1)}), bf16[16,16,1536]{2,1,0:T(8,128)(2,1)S(1)}, u32[]{:S(2)}, u32[]{:S(2)}) %all-to-all-start.1) | async-done | bytes 786464 | tf_op jit(solution)/shard_map/all_to_all | solution.py:267
  87.2 4.2 %head.1.h_ref = bf16[256,1536]{1,0:T(8,128)(2,1)S(1)} custom-call(bf16[256,1536]{1,0:T(8,128)(2,1)S(1)} %bitcast.7, f32[1,1536]{1,0:T(1,128)S(1)} %broadcast_in_dim.42.gain_ref.rest_0_, bf16[1536,1536]{1,0:T(8,128)(2,1)} %fusion.perm_ref.rest_1_), custom_call_target="tpu_custom_call" | custom-call | tf_op jit(solution)/shard_map/head/pallas_call | solution.py:58
  91.3 2.1 collective-permute-start.7
  95.6 24.2 %all-gather.2.cloned.1.call-done = bf16[6144,1152]{1,0:T(8,128)(2,1)} async-done(((bf16[192,1152]{1,0:T(8,128)(2,1)}), bf16[6144,1152]{1,0:T(8,128)(2,1)}) %all-gather.2.cloned.1.call-update) | async-done | bytes 14155792 | tf_op jit(solution)/shard_map/all_gather | solution.py:236
  119.7 7.8 %project.2.own_ref = bf16[4,256,1152]{2,1,0:T(8,128)(2,1)S(1)} custom-call(bf16[256,1536]{1,0:T(8,128)(2,1)S(1)} %head.1.h_ref, bf16[4,4,384,1152]{3,2,1,0:T(8,128)(2,1)} %bitcast.9), custom_call_target="tpu_custom_call" | custom-call | tf_op jit(solution)/shard_map/project/pallas_call | solution.py:75
  129.0 13.3 %attend.2 = (f32[256,1536]{1,0:T(8,128)S(1)}, bf16[256,1536]{1,0:T(8,128)(2,1)S(1)}) custom-call(bf16[256,1536]{1,0:T(8,128)(2,1)S(1)} %collective-permute-done.7.left_ref, bf16[4,256,1152]{2,1,0:T(8,128)(2,1)} %copy-done.2, bf16[4,4,384,1152]{3,2,1,0:T(8,128)(2,1)} %bitcast.10, bf16[1536,1536]{1,0:T(8,128)(2,1)} %wout_ref.3, bf16[256,1536]{1,0:T(8,128)(2,1)S(1)} %bitcast.8, ...), custom_call_target="tpu_custom_call" | custom-call | tf_op jit(solution)/shard_map/attend/pallas_call | solution.py:145
  142.3 2.2 %collective-permute-start.8 = (bf16[16,1536]{1,0:T(8,128)(2,1)S(1)}, bf16[16,1536]{1,0:T(8,128)(2,1)S(1)}, u32[]{:S(2)}, u32[]{:S(2)}) collective-permute-start(bf16[16,1536]{1,0:T(8,128)(2,1)S(1)} %get-tuple-element.27), channel_id=1, source_target_pairs={{0,1},{1,2},{2,3},{3,4},{4,5},{5,6},{6,7},{7,8},{8,9},{9,10},{10,1... | collective-permute-start | bytes 147464 | tf_op jit(solution)/shard_map/ppermute | solution.py:215
  144.4 5.5 %collective-permute-start.9 = (bf16[16,1536]{1,0:T(8,128)(2,1)S(1)}, bf16[16,1536]{1,0:T(8,128)(2,1)S(1)}, u32[]{:S(2)}, u32[]{:S(2)}) collective-permute-start(bf16[16,1536]{1,0:T(8,128)(2,1)S(1)} %get-tuple-element.26), channel_id=1, source_target_pairs={{1,0},{2,1},{3,2},{4,3},{5,4},{6,5},{7,6},{8,7},{9,8},{10,9},{11,1... | collective-permute-start | bytes 147464 | tf_op jit(solution)/shard_map/ppermute | solution.py:215
  151.7 9.6 %convolve.2 = (bf16[256,1536]{1,0:T(8,128)(2,1)S(1)}, bf16[256,1536]{1,0:T(8,128)(2,1)S(1)}) custom-call(bf16[256,1536]{1,0:T(8,128)(2,1)S(1)} %get-tuple-element.15.g_ref, bf16[16,1536]{1,0:T(8,128)(2,1)S(1)} %collective-permute-done.8.low_ref, bf16[16,1536]{1,0:T(8,128)(2,1)S(1)} %collective-permute-done.9.high_ref, ...), custom_call_target="tpu_custom_call" | custom-call | tf_op jit(solution)/shard_map/convolve/pallas_call | solution.py:203
  161.3 2.1 %collective-permute-start.10 = (bf16[256,1536]{1,0:T(8,128)(2,1)S(1)}, bf16[256,1536]{1,0:T(8,128)(2,1)S(1)}, u32[]{:S(2)}, u32[]{:S(2)}) collective-permute-start(bf16[256,1536]{1,0:T(8,128)(2,1)S(1)} %get-tuple-element.17.h_ref), channel_id=1, source_target_pairs={{0,1},{1,2},{2,3},{3,4},{4,5},{5,6},{6,7},{7,8},{8,9},{9,10},{10,1... | collective-permute-start | bytes 2359304 | tf_op jit(solution)/shard_map/ppermute | solution.py:215
  163.5 7.8 %project.3.own_ref = bf16[4,256,1152]{2,1,0:T(8,128)(2,1)S(1)} custom-call(bf16[256,1536]{1,0:T(8,128)(2,1)S(1)} %get-tuple-element.17.h_ref, bf16[4,4,384,1152]{3,2,1,0:T(8,128)(2,1)} %bitcast.11), custom_call_target="tpu_custom_call" | custom-call | tf_op jit(solution)/shard_map/project/pallas_call | solution.py:75
  172.6 4.1 %collective-permute-done.10.left_ref = bf16[256,1536]{1,0:T(8,128)(2,1)S(1)} collective-permute-done((bf16[256,1536]{1,0:T(8,128)(2,1)S(1)}, bf16[256,1536]{1,0:T(8,128)(2,1)S(1)}, u32[]{:S(2)}, u32[]{:S(2)}) %collective-permute-start.10) | collective-permute-done | bytes 786464 | tf_op jit(solution)/shard_map/ppermute | solution.py:215
  176.7 13.3 %attend.3 = (f32[256,1536]{1,0:T(8,128)S(1)}, bf16[256,1536]{1,0:T(8,128)(2,1)S(1)}) custom-call(bf16[256,1536]{1,0:T(8,128)(2,1)S(1)} %collective-permute-done.10.left_ref, bf16[4,256,1152]{2,1,0:T(8,128)(2,1)} %copy-done.1, bf16[4,4,384,1152]{3,2,1,0:T(8,128)(2,1)} %bitcast.12, bf16[1536,1536]{1,0:T(8,128)(2,1)} %wout_ref.3, ...), custom_call_target="tpu_custom_call" | custom-call | tf_op jit(solution)/shard_map/attend/pallas_call | solution.py:145
  191.9 5.8 %collective-permute-start.12 = (bf16[16,1536]{1,0:T(8,128)(2,1)S(1)}, bf16[16,1536]{1,0:T(8,128)(2,1)S(1)}, u32[]{:S(2)}, u32[]{:S(2)}) collective-permute-start(bf16[16,1536]{1,0:T(8,128)(2,1)S(1)} %get-tuple-element.24), channel_id=1, source_target_pairs={{1,0},{2,1},{3,2},{4,3},{5,4},{6,5},{7,6},{8,7},{9,8},{10,9},{11,1... | collective-permute-start | bytes 147464 | tf_op jit(solution)/shard_map/ppermute | solution.py:215
  199.4 5.3 %convolve.3 = bf16[256,1536]{1,0:T(8,128)(2,1)} custom-call(bf16[256,1536]{1,0:T(8,128)(2,1)S(1)} %get-tuple-element.19.g_ref, bf16[16,1536]{1,0:T(8,128)(2,1)S(1)} %collective-permute-done.11.low_ref, bf16[16,1536]{1,0:T(8,128)(2,1)S(1)} %collective-permute-done.12.high_ref, f32[256,1536]{1,0:T(8,128)S(1)} %get-tuple-element.20.x1_ref, ...), custom_call_target="tpu_custom_call" | custom-call | tf_op jit(solution)/shard_map/convolve/pallas_call | solution.py:203
  (56 shorter events, 17.9 us)
Async XLA Ops:
  6.5 31.5 %copy-start = (s32[16,16]{1,0:T(8,128)S(1)}, s32[16,16]{1,0:T(8,128)}, u32[]{:S(2)}) copy-start(s32[16,16]{1,0:T(8,128)} %param.9) | copy-start | bytes 3076
  6.5 59.7 %copy-start.5 = (f32[1536]{0:T(1024)S(1)}, f32[1536]{0:T(1024)}, u32[]{:S(2)}) copy-start(f32[1536]{0:T(1024)} %param.11) | copy-start | bytes 18436
  6.5 113.2 %all-gather.2.cloned.1.call-start = ((), (), s32[]{:S(2)}) async-start(), calls=%async_computation.2 | async-start | bytes 14598144 | tf_op jit(solution)/shard_map/all_gather | solution.py:236
  7.3 14.8 %collective-permute-start = (bf16[24,1152]{1,0:T(8,128)(2,1)S(1)}, bf16[24,1152]{1,0:T(8,128)(2,1)S(1)}, u32[]{:S(2)}, u32[]{:S(2)}) collective-permute-start(bf16[24,1152]{1,0:T(8,128)(2,1)S(1)} %get-tuple-element.28), channel_id=1, source_target_pairs={{0,32},{32,64},{64,96},{96,128},{128,160},{160,192},{192,224},{224... | collective-permute-start | bytes 165896 | tf_op jit(solution)/shard_map/ppermute | solution.py:233
  9.3 15.5 %collective-permute-start.1 = (bf16[24,1152]{1,0:T(8,128)(2,1)S(1)}, bf16[24,1152]{1,0:T(8,128)(2,1)S(1)}, u32[]{:S(2)}, u32[]{:S(2)}) collective-permute-start(bf16[24,1152]{1,0:T(8,128)(2,1)S(1)} %get-tuple-element.28), channel_id=1, source_target_pairs={{0,64},{32,96},{64,128},{96,160},{128,192},{160,224},{192,0},{224,... | collective-permute-start | bytes 165896 | tf_op jit(solution)/shard_map/ppermute | solution.py:233
  12.6 13.3 %collective-permute-start.2 = (bf16[24,1152]{1,0:T(8,128)(2,1)S(1)}, bf16[24,1152]{1,0:T(8,128)(2,1)S(1)}, u32[]{:S(2)}, u32[]{:S(2)}) collective-permute-start(bf16[24,1152]{1,0:T(8,128)(2,1)S(1)} %get-tuple-element.28), channel_id=1, source_target_pairs={{0,96},{32,128},{64,160},{96,192},{128,224},{160,0},{192,32},{224,... | collective-permute-start | bytes 165896 | tf_op jit(solution)/shard_map/ppermute | solution.py:233
  16.6 9.3 %collective-permute-start.3 = (bf16[24,1152]{1,0:T(8,128)(2,1)S(1)}, bf16[24,1152]{1,0:T(8,128)(2,1)S(1)}, u32[]{:S(2)}, u32[]{:S(2)}) collective-permute-start(bf16[24,1152]{1,0:T(8,128)(2,1)S(1)} %get-tuple-element.28), channel_id=1, source_target_pairs={{0,128},{32,160},{64,192},{96,224},{128,0},{160,32},{192,64},{224,... | collective-permute-start | bytes 165896 | tf_op jit(solution)/shard_map/ppermute | solution.py:233
  17.2 12.4 %collective-permute-start.4 = (bf16[24,1152]{1,0:T(8,128)(2,1)S(1)}, bf16[24,1152]{1,0:T(8,128)(2,1)S(1)}, u32[]{:S(2)}, u32[]{:S(2)}) collective-permute-start(bf16[24,1152]{1,0:T(8,128)(2,1)S(1)} %get-tuple-element.28), channel_id=1, source_target_pairs={{0,160},{32,192},{64,224},{96,0},{128,32},{160,64},{192,96},{224,1... | collective-permute-start | bytes 165896 | tf_op jit(solution)/shard_map/ppermute | solution.py:233
  22.1 7.4 %collective-permute-start.5 = (bf16[24,1152]{1,0:T(8,128)(2,1)S(1)}, bf16[24,1152]{1,0:T(8,128)(2,1)S(1)}, u32[]{:S(2)}, u32[]{:S(2)}) collective-permute-start(bf16[24,1152]{1,0:T(8,128)(2,1)S(1)} %get-tuple-element.28), channel_id=1, source_target_pairs={{0,192},{32,224},{64,0},{96,32},{128,64},{160,96},{192,128},{224,1... | collective-permute-start | bytes 165896 | tf_op jit(solution)/shard_map/ppermute | solution.py:233
  24.8 5.6 %collective-permute-start.6 = (bf16[24,1152]{1,0:T(8,128)(2,1)S(1)}, bf16[24,1152]{1,0:T(8,128)(2,1)S(1)}, u32[]{:S(2)}, u32[]{:S(2)}) collective-permute-start(bf16[24,1152]{1,0:T(8,128)(2,1)S(1)} %get-tuple-element.28), channel_id=1, source_target_pairs={{0,224},{32,0},{64,32},{96,64},{128,96},{160,128},{192,160},{224,1... | collective-permute-start | bytes 165896 | tf_op jit(solution)/shard_map/ppermute | solution.py:233
  30.4 0.8 copy-start.3
  31.2 26.7 %all-to-all-start = ((bf16[16,16,1536]{2,1,0:T(8,128)(2,1)}), bf16[16,16,1536]{2,1,0:T(8,128)(2,1)S(1)}, u32[]{:S(2)}, u32[]{:S(2)}) async-start(bf16[16,16,1536]{2,1,0:T(8,128)(2,1)} %bitcast.13), calls=%async_computation | async-start | bytes 1572864 | tf_op jit(solution)/shard_map/all_to_all | solution.py:265
  59.4 27.7 %all-to-all-start.1 = ((bf16[16,16,1536]{2,1,0:T(8,128)(2,1)}), bf16[16,16,1536]{2,1,0:T(8,128)(2,1)S(1)}, u32[]{:S(2)}, u32[]{:S(2)}) async-start(bf16[16,16,1536]{2,1,0:T(8,128)(2,1)} %pick.1), calls=%async_computation.1 | async-start | bytes 1572864 | tf_op jit(solution)/shard_map/all_to_all | solution.py:267
  66.3 27.2 %copy-start.6 = (f32[1536]{0:T(1024)S(1)}, f32[1536]{0:T(1024)}, u32[]{:S(2)}) copy-start(f32[1536]{0:T(1024)} %param.14) | copy-start | bytes 18436
  66.3 27.2 %copy-start.7 = (s32[16]{0:T(128)S(1)}, s32[16]{0:T(128)}, u32[]{:S(2)}) copy-start(s32[16]{0:T(128)} %param.10) | copy-start | bytes 196
  91.3 37.6 %collective-permute-start.7 = (bf16[256,1536]{1,0:T(8,128)(2,1)S(1)}, bf16[256,1536]{1,0:T(8,128)(2,1)S(1)}, u32[]{:S(2)}, u32[]{:S(2)}) collective-permute-start(bf16[256,1536]{1,0:T(8,128)(2,1)S(1)} %head.1.h_ref), channel_id=1, source_target_pairs={{0,1},{1,2},{2,3},{3,4},{4,5},{5,6},{6,7},{7,8},{8,9},{9,10},{10,1... | collective-permute-start | bytes 2359304 | tf_op jit(solution)/shard_map/ppermute | solution.py:215
  127.5 1.4 copy-start.2
  129.0 21.0 %copy-start.4 = (f32[31,1536]{1,0:T(8,128)S(1)}, f32[31,1536]{1,0:T(8,128)}, u32[]{:S(2)}) copy-start(f32[31,1536]{1,0:T(8,128)} %param.15) | copy-start | bytes 571396
  142.3 7.7 %collective-permute-start.8 = (bf16[16,1536]{1,0:T(8,128)(2,1)S(1)}, bf16[16,1536]{1,0:T(8,128)(2,1)S(1)}, u32[]{:S(2)}, u32[]{:S(2)}) collective-permute-start(bf16[16,1536]{1,0:T(8,128)(2,1)S(1)} %get-tuple-element.27), channel_id=1, source_target_pairs={{0,1},{1,2},{2,3},{3,4},{4,5},{5,6},{6,7},{7,8},{8,9},{9,10},{10,1... | collective-permute-start | bytes 147464 | tf_op jit(solution)/shard_map/ppermute | solution.py:215
  144.4 7.2 %collective-permute-start.9 = (bf16[16,1536]{1,0:T(8,128)(2,1)S(1)}, bf16[16,1536]{1,0:T(8,128)(2,1)S(1)}, u32[]{:S(2)}, u32[]{:S(2)}) collective-permute-start(bf16[16,1536]{1,0:T(8,128)(2,1)S(1)} %get-tuple-element.26), channel_id=1, source_target_pairs={{1,0},{2,1},{3,2},{4,3},{5,4},{6,5},{7,6},{8,7},{9,8},{10,9},{11,1... | collective-permute-start | bytes 147464 | tf_op jit(solution)/shard_map/ppermute | solution.py:215
  161.3 15.4 %collective-permute-start.10 = (bf16[256,1536]{1,0:T(8,128)(2,1)S(1)}, bf16[256,1536]{1,0:T(8,128)(2,1)S(1)}, u32[]{:S(2)}, u32[]{:S(2)}) collective-permute-start(bf16[256,1536]{1,0:T(8,128)(2,1)S(1)} %get-tuple-element.17.h_ref), channel_id=1, source_target_pairs={{0,1},{1,2},{2,3},{3,4},{4,5},{5,6},{6,7},{7,8},{8,9},{9,10},{10,1... | collective-permute-start | bytes 2359304 | tf_op jit(solution)/shard_map/ppermute | solution.py:215
  171.3 1.4 copy-start.1
  190.0 7.7 %collective-permute-start.11 = (bf16[16,1536]{1,0:T(8,128)(2,1)S(1)}, bf16[16,1536]{1,0:T(8,128)(2,1)S(1)}, u32[]{:S(2)}, u32[]{:S(2)}) collective-permute-start(bf16[16,1536]{1,0:T(8,128)(2,1)S(1)} %get-tuple-element.25), channel_id=1, source_target_pairs={{0,1},{1,2},{2,3},{3,4},{4,5},{5,6},{6,7},{7,8},{8,9},{9,10},{10,1... | collective-permute-start | bytes 147464 | tf_op jit(solution)/shard_map/ppermute | solution.py:215
  191.9 7.5 %collective-permute-start.12 = (bf16[16,1536]{1,0:T(8,128)(2,1)S(1)}, bf16[16,1536]{1,0:T(8,128)(2,1)S(1)}, u32[]{:S(2)}, u32[]{:S(2)}) collective-permute-start(bf16[16,1536]{1,0:T(8,128)(2,1)S(1)} %get-tuple-element.24), channel_id=1, source_target_pairs={{1,0},{2,1},{3,2},{4,3},{5,4},{6,5},{7,6},{8,7},{9,8},{10,9},{11,1... | collective-permute-start | bytes 147464 | tf_op jit(solution)/shard_map/ppermute | solution.py:215
Sparse Core Ops, SparseCore 0:
  31.4 88.3 all-gather.1

commit v2 on v1

v2 whole, which is shorter than its diff:
```python
import functools

import jax
import jax.numpy as jnp
from jax import lax
from jax.experimental import pallas as pl
from jax.experimental.pallas import tpu as pltpu
from jax.sharding import Mesh, PartitionSpec as P

HEAD = 64
KERNEL = 31
ITERS = 2
HALO = 16
EPS = 1e-05
DP = ("z", "yh")
SEQ = ("yl", "x", "core")
BF = jnp.bfloat16
F32 = jnp.float32
VMEM = 24 * 1024 * 1024


def params(**kw):
    return pltpu.CompilerParams(vmem_limit_bytes=VMEM, **kw)


def normed(v):
    mean = jnp.mean(v, axis=-1, keepdims=True)
    d = v - mean
    var = jnp.mean(d * d, axis=-1, keepdims=True)
    return d * lax.rsqrt(var + EPS)


def pick_kernel(row_ref, in_ref, out_ref):
    for r in range(in_ref.shape[0]):
        out_ref[r] = in_ref[row_ref[r]]


def pick(chunks, row):
    return pl.pallas_call(
        pick_kernel,
        out_shape=jax.ShapeDtypeStruct(chunks.shape, chunks.dtype),
        in_specs=[
            pl.BlockSpec(memory_space=pltpu.SMEM),
            pl.BlockSpec(memory_space=pltpu.VMEM),
        ],
        out_specs=pl.BlockSpec(memory_space=pltpu.VMEM),
        compiler_params=params(),
        name="pick",
    )(row, chunks)


def head_kernel(x_ref, gain_ref, out_ref):
    out_ref[...] = (normed(x_ref[...].astype(F32)) * gain_ref[...]).astype(BF)


def head(x, gain):
    return pl.pallas_call(
        head_kernel,
        out_shape=jax.ShapeDtypeStruct(x.shape, BF),
        compiler_params=params(),
        name="head",
    )(x, gain)


def project_kernel(h_ref, w_ref, out_ref):
    out_ref[0] = jnp.dot(h_ref[...], w_ref[0], preferred_element_type=F32).astype(BF)


def project(h, w):
    blocks, depth, cols = w.shape
    span, width = h.shape
    return pl.pallas_call(
        project_kernel,
        grid=(blocks,),
        out_shape=jax.ShapeDtypeStruct((blocks, span, cols), BF),
        in_specs=[
            pl.BlockSpec((span, width), lambda b: (0, 0)),
            pl.BlockSpec((1, depth, cols), lambda b: (b, 0, 0)),
        ],
        out_specs=pl.BlockSpec((1, span, cols), lambda b: (b, 0, 0)),
        compiler_params=params(),
        name="project",
    )(h, w)


def heads(query, keys, values, bias):
    span = query.shape[0]
    lane = lax.broadcasted_iota(jnp.int32, (span, 128), 1)
    low = lane < HEAD
    tag = jnp.where(lane == 0, 1.0, 0.0).astype(BF)
    ones = jnp.ones((2 * span, 128), BF)
    outs = []
    for at in range(0, query.shape[1], 128):
        k = jnp.concatenate([keys[:, at : at + 128], bias], axis=1)
        v = jnp.concatenate([values[:, at : at + 128], ones], axis=1)
        q = query[:, at : at + 128] * jnp.asarray(HEAD ** (-0.5), BF)
        halves = []
        for mask in (low, jnp.logical_not(low)):
            qh = jnp.concatenate([jnp.where(mask, q, jnp.zeros_like(q)), tag], axis=1)
            s = lax.dot_general(qh, k, (((1,), (1,)), ((), ())), preferred_element_type=F32)
            top = jnp.max(s, axis=-1, keepdims=True)
            e = jnp.exp(s - top).astype(BF)
            o = jnp.dot(e, v, preferred_element_type=F32)
            halves.append(o[:, :128] / o[:, 128:])
        outs.append(jnp.where(low, halves[0], halves[1]).astype(BF))
    return jnp.concatenate(outs, axis=1)


def settle(ctx, wout_ref, x_ref, gain_ref, valid_ref, x1_ref, g_ref, acc_ref):
    b = pl.program_id(0)
    part = jnp.dot(ctx, wout_ref[...], preferred_element_type=F32)

    @pl.when(b == 0)
    def _():
        acc_ref[...] = x_ref[...].astype(F32) + part

    @pl.when(b > 0)
    def _():
        acc_ref[...] += part

    @pl.when(b == pl.num_programs(0) - 1)
    def _():
        x1 = acc_ref[...]
        x1_ref[...] = x1
        g_ref[...] = (normed(x1) * gain_ref[...] * valid_ref[...]).astype(BF)


def opening_kernel(
    z_ref, left_ref, h_ref, w_ref, wout_ref, x_ref, bias_ref, gain_ref, valid_ref,
    x1_ref, g_ref, wall_ref, acc_ref, both_ref, buf_ref, in_sem, out_sem,
):
    b = pl.program_id(0)
    last = pl.num_programs(0) - 1
    slot = lax.rem(b, 2)
    span = h_ref.shape[0]
    group = wout_ref.shape[0]
    parts, _, zs, rows, _ = w_ref.shape

    def fetch(block, to):
        for part in range(parts):
            for z in range(zs):
                at = (z * parts + part) * rows
                pltpu.make_async_copy(
                    w_ref.at[part, block, lax.rem(z_ref[0] - z + zs, zs)],
                    buf_ref.at[to, pl.ds(at, rows)],
                    in_sem.at[to],
                ).start()

    def saved(block, at):
        return pltpu.make_async_copy(buf_ref.at[at], wall_ref.at[block], out_sem.at[at])

    @pl.when(b == 0)
    def _():
        fetch(0, 0)
        both_ref[pl.ds(0, span), :] = left_ref[...]
        both_ref[pl.ds(span, span), :] = h_ref[...]

    @pl.when(b > 0)
    def _():
        saved(b - 1, 1 - slot).wait()

    @pl.when(b < last)
    def _():
        fetch(b + 1, 1 - slot)

    pltpu.make_async_copy(wall_ref.at[b], buf_ref.at[slot], in_sem.at[slot]).wait()
    saved(b, slot).start()
    kv = jnp.dot(both_ref[...], buf_ref[slot, :, : 2 * group], preferred_element_type=F32).astype(BF)
    q = jnp.dot(h_ref[...], buf_ref[slot, :, 2 * group :], preferred_element_type=F32).astype(BF)
    ctx = heads(q, kv[:, :group], kv[:, group:], bias_ref[...])
    settle(ctx, wout_ref, x_ref, gain_ref, valid_ref, x1_ref, g_ref, acc_ref)

    @pl.when(b == last)
    def _():
        saved(b, slot).wait()


def whole(*shape):
    return pl.BlockSpec(shape, lambda b: (0,) * len(shape))


def opening(z, left, h, w, w_out, x, bias, gain, valid):
    parts, blocks, zs, rows, cols = w.shape
    span, width = x.shape
    group = width // blocks
    depth = parts * zs * rows
    return pl.pallas_call(
        opening_kernel,
        grid=(blocks,),
        out_shape=(
            jax.ShapeDtypeStruct((span, width), F32),
            jax.ShapeDtypeStruct((span, width), BF),
            jax.ShapeDtypeStruct((blocks, depth, cols), BF),
        ),
        in_specs=[
            pl.BlockSpec(memory_space=pltpu.SMEM),
            whole(span, width),
            whole(span, width),
            pl.BlockSpec(memory_space=pl.ANY),
            pl.BlockSpec((group, width), lambda b: (b, 0)),
            whole(span, width),
            whole(2 * span, 128),
            whole(1, width),
            whole(span, 1),
        ],
        out_specs=(whole(span, width), whole(span, width), pl.BlockSpec(memory_space=pl.ANY)),
        scratch_shapes=[
            pltpu.VMEM((span, width), F32),
            pltpu.VMEM((2 * span, width), BF),
            pltpu.VMEM((2, depth, cols), BF),
            pltpu.SemaphoreType.DMA((2,)),
            pltpu.SemaphoreType.DMA((2,)),
        ],
        compiler_params=params(),
        name="opening",
    )(z, left, h, w, w_out, x, bias, gain, valid)


def attend_kernel(
    left_ref, own_ref, w_ref, wout_ref, x_ref, bias_ref, gain_ref, valid_ref,
    x1_ref, g_ref, acc_ref,
):
    b = pl.program_id(0)
    group = wout_ref.shape[0]
    left = jnp.dot(left_ref[...], w_ref[0], preferred_element_type=F32).astype(BF)
    own = own_ref[b]
    keys = jnp.concatenate([left[:, :group], own[:, :group]], axis=0)
    values = jnp.concatenate([left[:, group:], own[:, group : 2 * group]], axis=0)
    ctx = heads(own[:, 2 * group :], keys, values, bias_ref[...])
    settle(ctx, wout_ref, x_ref, gain_ref, valid_ref, x1_ref, g_ref, acc_ref)


def attend(left, own, w, w_out, x, bias, gain, valid):
    blocks, depth, cols = w.shape
    span, width = x.shape
    group = width // blocks
    return pl.pallas_call(
        attend_kernel,
        grid=(blocks,),
        out_shape=(
            jax.ShapeDtypeStruct((span, width), F32),
            jax.ShapeDtypeStruct((span, width), BF),
        ),
        in_specs=[
            whole(span, width),
            pl.BlockSpec(memory_space=pltpu.VMEM),
            pl.BlockSpec((1, depth, 2 * group), lambda b: (b, 0, 0)),
            pl.BlockSpec((group, width), lambda b: (b, 0)),
            whole(span, width),
            whole(2 * span, 128),
            whole(1, width),
            whole(span, 1),
        ],
        out_specs=(whole(span, width), whole(span, width)),
        scratch_shapes=[pltpu.VMEM((span, width), F32)],
        compiler_params=params(),
        name="attend",
    )(left, own, w, w_out, x, bias, gain, valid)


def taps_over(pad_ref, taps, rows):
    y = jnp.zeros((rows, 128), F32)
    for r in range(8):
        hits = [(j, (j + 1) // 8) for j in range(KERNEL) if (j + 1) % 8 == r]
        deep = max(m for _, m in hits)
        moved = pad_ref[pl.ds(r, rows + 8 * deep), :]
        for j, m in hits:
            y = y + taps[j : j + 1, :] * moved[8 * m : 8 * m + rows]
    return y / (1.0 + jnp.exp(-y))


def inner_kernel(g_ref, x1_ref, taps_ref, valid_ref, gain_ref, x_ref, *rest):
    pad_ref = rest[-1]
    span, width = x1_ref.shape
    rows = pl.ds(HALO, span - 2 * HALO)
    for c in range(width // 128):
        cols = pl.ds(128 * c, 128)
        pad_ref[...] = g_ref[:, cols].astype(F32)
        silu = taps_over(pad_ref, taps_ref[:, cols], span - 2 * HALO)
        x_ref[rows, cols] = ((x1_ref[rows, cols] + silu) * valid_ref[rows, :]).astype(BF)
    if len(rest) > 1:
        rest[0][rows, :] = (normed(x_ref[rows, :].astype(F32)) * gain_ref[...]).astype(BF)


def inner(g, x1, taps, valid, gain, last):
    span, width = x1.shape
    return pl.pallas_call(
        inner_kernel,
        out_shape=(jax.ShapeDtypeStruct((span, width), BF),) * (1 if last else 2),
        scratch_shapes=[pltpu.VMEM((span, 128), F32)],
        compiler_params=params(),
        name="inner",
    )(g, x1, taps, valid, gain)


def edges_kernel(count, g_ref, low_ref, high_ref, x1_ref, taps_ref, valid_ref, gain_ref, *rest):
    ins, outs, pad_ref = rest[:count], rest[count:-1], rest[-1]
    span, width = x1_ref.shape
    x_ref = outs[0]
    for at in (0, span - HALO):
        rows = pl.ds(at, HALO)
        for c in range(width // 128):
            cols = pl.ds(128 * c, 128)
            if at == 0:
                pad_ref[pl.ds(0, HALO), :] = low_ref[:, cols].astype(F32)
                pad_ref[pl.ds(HALO, 2 * HALO), :] = g_ref[pl.ds(0, 2 * HALO), cols].astype(F32)
            else:
                pad_ref[pl.ds(0, 2 * HALO), :] = g_ref[pl.ds(span - 2 * HALO, 2 * HALO), cols].astype(F32)
                pad_ref[pl.ds(2 * HALO, HALO), :] = high_ref[:, cols].astype(F32)
            silu = taps_over(pad_ref, taps_ref[:, cols], HALO)
            x_ref[rows, cols] = ((x1_ref[rows, cols] + silu) * valid_ref[rows, :]).astype(BF)
        if count > 1:
            outs[1][rows, :] = (normed(x_ref[rows, :].astype(F32)) * gain_ref[...]).astype(BF)
    rows = pl.ds(HALO, span - 2 * HALO)
    for source, target in zip(ins, outs):
        target[rows, :] = source[rows, :]


def edges(g, low, high, x1, taps, valid, gain, inners):
    span, width = x1.shape
    count = len(inners)
    return pl.pallas_call(
        functools.partial(edges_kernel, count),
        out_shape=(jax.ShapeDtypeStruct((span, width), BF),) * count,
        scratch_shapes=[pltpu.VMEM((3 * HALO, 128), F32)],
        compiler_params=params(),
        name="edges",
    )(g, low, high, x1, taps, valid, gain, *inners)


def along(value, by):
    size = lax.axis_size(SEQ)
    pairs = [(i, i + by) for i in range(size) if 0 <= i + by < size]
    return lax.ppermute(value, SEQ, pairs)


def weight_blocks(w, frames):
    rows, cols = w.shape
    zs, xs, yls, cores = (lax.axis_size(a) for a in ("z", "x", "yl", "core"))
    deep = rows // yls
    width = cols // 3
    group = width // xs
    at = lax.axis_index("yl") * deep
    col = lax.axis_index("x") * group
    own = jnp.concatenate(
        [lax.dynamic_slice(w, (at, part * width + col), (deep, group)) for part in (1, 2, 0)],
        axis=1,
    )
    half = zs // cores
    came = {}
    for k in range(1, half + 1):
        pairs = [(cores * z, cores * ((z + k) % zs)) for z in range(zs) if k < half]
        pairs += [(cores * z + 1, cores * ((z - k) % zs) + 1) for z in range(zs)]
        came[k] = lax.ppermute(own, ("z", "core"), pairs)
    first = lax.axis_index("core") == 0
    stack = jnp.concatenate(
        [
            jnp.where(first, came[k] if k else own, came[half - k])
            for k in range(half)
        ],
        axis=0,
    )
    stack, frames = lax.optimization_barrier((stack, frames))
    full = lax.all_gather(stack, ("yh",) + SEQ, axis=0, tiled=True)
    parts = lax.axis_size("yh") * yls
    return full.reshape(parts, xs, zs, deep, 3 * group), frames


def on_device(frames, arrival, lengths, attn_gain, w_qkv, w_out, conv_gain, conv_kernel):
    span = frames.shape[1]
    width = w_out.shape[0]
    group = lax.axis_index(DP)
    place = lax.axis_index(SEQ)
    groups = lax.axis_size(DP)
    w, frames = weight_blocks(w_qkv, frames)
    row_here = lax.dynamic_index_in_dim(arrival, place, 0, keepdims=False)
    chunks = frames.reshape(groups, span // groups, width)
    chunks = lax.all_to_all(chunks, DP, split_axis=0, concat_axis=0, tiled=True)
    chunks = pick(chunks, row_here)
    chunks = lax.all_to_all(chunks, DP, split_axis=0, concat_axis=0, tiled=True)
    x = chunks.reshape(span, width)

    length = lax.dynamic_index_in_dim(lengths, group, 0, keepdims=False)
    position = place * span + jnp.arange(span)
    own_valid = position < length
    left_valid = jnp.logical_and(position - span < length, place > 0)
    key_valid = jnp.concatenate([left_valid, own_valid])
    bias = jnp.where(key_valid, 0.0, -1e30).astype(BF)
    bias = jnp.where(jnp.arange(128)[None, :] == 0, bias[:, None], jnp.zeros((), BF))
    valid = own_valid.astype(F32)[:, None]
    gain_a = attn_gain[None, :]
    gain_c = conv_gain[None, :]
    taps = jnp.pad(conv_kernel, ((0, 1), (0, 0)))

    h = head(x, gain_a)
    for step in range(ITERS):
        last = step == ITERS - 1
        left = along(h, 1)
        if step == 0:
            z = lax.axis_index("z").astype(jnp.int32)[None]
            x1, g, w = opening(z, left, h, w, w_out, x, bias, gain_c, valid)
        else:
            x1, g = attend(left, project(h, w), w, w_out, x, bias, gain_c, valid)
        low = along(g[span - HALO :], 1)
        high = along(g[:HALO], -1)
        inners = inner(g, x1, taps, valid, gain_a, last)
        out = edges(g, low, high, x1, taps, valid, gain_a, inners)
        x = out[0]
        if not last:
            h = out[1]
    return x[None]


def solution(mesh):
    fine = Mesh(mesh.devices.reshape(8, 2, 2, 4, 2), DP + SEQ)
    placed = (P(DP, SEQ, None), P(), P(), P(), P(DP, None), P(), P(), P())
    return jax.shard_map(
        on_device, mesh=fine, in_specs=placed, out_specs=P(DP, SEQ, None), check_vma=False
    )
```

time: 214 us -> 205 us (0.958)
  waiting for transfers between devices: 72.7 us -> 87.8 us
  Pallas kernels: 62.6 us -> 48 us
  starting transfers between devices: 51.7 us -> 43.6 us
  local copies, waits for them, and re-layouts: 5.1 us -> 8.95 us
  other arithmetic: 5.75 us -> 2.44 us
    ppermute x6, waiting for transfers between devices: 7.51 us -> 31.5 us  [along(): return lax.ppermute(value, SEQ, pairs)]
    all_gather x1, waiting for transfers between devices: 24.2 us -> 4.52 us  [weight_blocks(): full = lax.all_gather(stack, ('yh',) + SEQ, axis=0, tiled=True)]
    pallas_call x2 -> x1, Pallas kernels: 26.5 us -> 11.7 us  [attend(): pl.pallas_call(attend_kernel, grid=(blocks,), out_shape=(jax.ShapeDtypeSt...]
    pallas_call x2 -> x5, Pallas kernels: 14.9 us -> 29.6 us  [the longest x1 18.5 us: opening(): pl.pallas_call(opening_kernel, grid=(blocks,), out_shape=(jax.ShapeDtypeS...]
    pallas_call x2 -> x1, Pallas kernels: 15.6 us -> 4.78 us  [project(): pl.pallas_call(project_kernel, grid=(blocks,), out_shape=jax.ShapeDtypeSt...]
    ppermute x7 -> x4, starting transfers between devices: 18.5 us -> 10 us  [weight_blocks(): came[k] = lax.ppermute(own, ('z', 'core'), pairs)]
    all_to_all x2, waiting for transfers between devices: 36.5 us -> 42.4 us  [on_device(): chunks = lax.all_to_all(chunks, DP, split_axis=0, concat_axis=0, tiled=True)]
    ppermute x7 -> x4, waiting for transfers between devices: 4.44 us -> 9.34 us  [weight_blocks(): came[k] = lax.ppermute(own, ('z', 'core'), pairs)]
  transfers between devices with their start and end apart: 16 -> 13, of which waited for: 8 -> 7; matrix products, arithmetic and copies ran while one was open for 3% -> 1% of each run, Pallas kernels for 10% -> 8%
where the time goes in v2:
time: 205 us
  waiting for transfers between devices  87.8 us (43%)
  Pallas kernels  48 us (23%)
  starting transfers between devices  43.6 us (21%)
  between operations  13.7 us (7%)
  local copies, waits for them, and re-layouts  8.95 us (4%)
  other arithmetic  2.44 us (1%)
    all_to_all x2, waiting for transfers between devices, on_device(): chunks = lax.all_to_all(chunks, DP, split_axis=0, concat_axis=0, tiled=True)  42.4 us
    ppermute x6, waiting for transfers between devices, along(): return lax.ppermute(value, SEQ, pairs)  31.5 us
    ppermute x6, starting transfers between devices, along(): return lax.ppermute(value, SEQ, pairs)  19.7 us
    pallas_call x1, Pallas kernels, opening(): pl.pallas_call(opening_kernel, grid=(blocks,), out_shape=(jax.ShapeDtypeS...  18.5 us
    all_to_all x2, starting transfers between devices, on_device(): chunks = lax.all_to_all(chunks, DP, split_axis=0, concat_axis=0, tiled=True)  13.8 us
    pallas_call x1, Pallas kernels, attend(): pl.pallas_call(attend_kernel, grid=(blocks,), out_shape=(jax.ShapeDtypeSt...  11.7 us
    ppermute x4, starting transfers between devices, weight_blocks(): came[k] = lax.ppermute(own, ('z', 'core'), pairs)  10 us
    ppermute x4, waiting for transfers between devices, weight_blocks(): came[k] = lax.ppermute(own, ('z', 'core'), pairs)  9.34 us
  transfers between devices with their start and end apart: 13, of which 7 were waited for; matrix products, arithmetic and copies ran while one was open for 1% of the time, Pallas kernels for 8%

profile of v2, /device:TPU:24, one launch (start us, length us, event | category | flops | bytes accessed | tf_op | source)
XLA Modules:
  0.0 204.5 jit_solution(1397092057704997471)
XLA Ops:
  7.4 2.0 collective-permute-start.1
  9.4 5.8 %collective-permute-start.2 = (bf16[48,1152]{1,0:T(8,128)(2,1)S(1)}, bf16[48,1152]{1,0:T(8,128)(2,1)S(1)}, u32[]{:S(2)}, u32[]{:S(2)}) collective-permute-start(bf16[48,1152]{1,0:T(8,128)(2,1)S(1)} %pad_maximum_fusion.1), channel_id=1, source_target_pairs={{0,96},{32,128},{64,160},{96,192},{128,224},{160,0},{192,32},{224,... | collective-permute-start | bytes 331784 | tf_op jit(solution)/shard_map/ppermute | solution.py:354
  17.5 4.9 %collective-permute-done.2 = bf16[48,1152]{1,0:T(8,128)(2,1)S(1)} collective-permute-done((bf16[48,1152]{1,0:T(8,128)(2,1)S(1)}, bf16[48,1152]{1,0:T(8,128)(2,1)S(1)}, u32[]{:S(2)}, u32[]{:S(2)}) %collective-permute-start.2) | collective-permute-done | bytes 110624 | tf_op jit(solution)/shard_map/ppermute | solution.py:354
  22.4 4.5 %collective-permute-done.3 = bf16[48,1152]{1,0:T(8,128)(2,1)S(1)} collective-permute-done((bf16[48,1152]{1,0:T(8,128)(2,1)S(1)}, bf16[48,1152]{1,0:T(8,128)(2,1)S(1)}, u32[]{:S(2)}, u32[]{:S(2)}) %collective-permute-start.3) | collective-permute-done | bytes 110624 | tf_op jit(solution)/shard_map/ppermute | solution.py:354
  27.8 7.6 %all-to-all-start = ((bf16[16,16,1536]{2,1,0:T(8,128)(2,1)}), bf16[16,16,1536]{2,1,0:T(8,128)(2,1)S(1)}, u32[]{:S(2)}, u32[]{:S(2)}) async-start(bf16[16,16,1536]{2,1,0:T(8,128)(2,1)} %bitcast.13), calls=%async_computation | async-start | bytes 1572864 | tf_op jit(solution)/shard_map/all_to_all | solution.py:378
  35.4 21.4 %all-to-all-done.in_ref = bf16[16,16,1536]{2,1,0:T(8,128)(2,1)S(1)} async-done(((bf16[16,16,1536]{2,1,0:T(8,128)(2,1)}), bf16[16,16,1536]{2,1,0:T(8,128)(2,1)S(1)}, u32[]{:S(2)}, u32[]{:S(2)}) %all-to-all-start) | async-done | bytes 786464 | tf_op jit(solution)/shard_map/all_to_all | solution.py:378
  58.2 6.3 %all-to-all-start.1 = ((bf16[16,16,1536]{2,1,0:T(8,128)(2,1)}), bf16[16,16,1536]{2,1,0:T(8,128)(2,1)S(1)}, u32[]{:S(2)}, u32[]{:S(2)}) async-start(bf16[16,16,1536]{2,1,0:T(8,128)(2,1)} %pick.1), calls=%async_computation.1 | async-start | bytes 1572864 | tf_op jit(solution)/shard_map/all_to_all | solution.py:380
  64.5 21.0 %all-to-all-done.1 = bf16[16,16,1536]{2,1,0:T(8,128)(2,1)S(1)} async-done(((bf16[16,16,1536]{2,1,0:T(8,128)(2,1)}), bf16[16,16,1536]{2,1,0:T(8,128)(2,1)S(1)}, u32[]{:S(2)}, u32[]{:S(2)}) %all-to-all-start.1) | async-done | bytes 786464 | tf_op jit(solution)/shard_map/all_to_all | solution.py:380
  86.0 1.9 collective-permute-start.4
  90.2 22.8 %collective-permute-done.4.left_ref = bf16[256,1536]{1,0:T(8,128)(2,1)S(1)} collective-permute-done((bf16[256,1536]{1,0:T(8,128)(2,1)S(1)}, bf16[256,1536]{1,0:T(8,128)(2,1)S(1)}, u32[]{:S(2)}, u32[]{:S(2)}) %collective-permute-start.4) | collective-permute-done | bytes 786464 | tf_op jit(solution)/shard_map/ppermute | solution.py:334
  113.0 4.5 %all-gather.2.cloned.1.call-done = bf16[6144,1152]{1,0:T(8,128)(2,1)} async-done(((bf16[192,1152]{1,0:T(8,128)(2,1)}), bf16[6144,1152]{1,0:T(8,128)(2,1)}) %all-gather.2.cloned.1.call-update) | async-done | bytes 14155792 | tf_op jit(solution)/shard_map/all_gather | solution.py:364
  117.5 2.3 %copy-done.3 = bf16[1536,1536]{1,0:T(8,128)(2,1)S(1)} copy-done((bf16[1536,1536]{1,0:T(8,128)(2,1)S(1)}, bf16[1536,1536]{1,0:T(8,128)(2,1)}, u32[]{:S(2)}) %copy-start.3) | copy-done | bytes 4718616
  119.9 18.5 %opening.1 = (f32[256,1536]{1,0:T(8,128)S(1)}, bf16[256,1536]{1,0:T(8,128)(2,1)S(1)}, bf16[4,1536,1152]{2,1,0:T(8,128)(2,1)S(1)}) custom-call(s32[1]{0:T(128)} %bitcast.z_ref, bf16[256,1536]{1,0:T(8,128)(2,1)S(1)} %collective-permute-done.4.left_ref, bf16[256,1536]{1,0:T(8,128)(2,1)S(1)} %head.1.h_ref, bf16[4,4,8,48,1152]{4,3,2,1,0:T(8,128)(2,1)} %bitcast.12, ...), custom_call_target="tpu_custom_call" | custom-call | tf_op jit(solution)/shard_map/opening/pallas_call | solution.py:187
  138.4 2.2 %collective-permute-start.5 = (bf16[16,1536]{1,0:T(8,128)(2,1)S(1)}, bf16[16,1536]{1,0:T(8,128)(2,1)S(1)}, u32[]{:S(2)}, u32[]{:S(2)}) collective-permute-start(bf16[16,1536]{1,0:T(8,128)(2,1)S(1)} %get-tuple-element.33), channel_id=1, source_target_pairs={{0,1},{1,2},{2,3},{3,4},{4,5},{5,6},{6,7},{7,8},{8,9},{9,10},{10,1... | collective-permute-start | bytes 147464 | tf_op jit(solution)/shard_map/ppermute | solution.py:334
  140.5 5.7 %collective-permute-start.6 = (bf16[16,1536]{1,0:T(8,128)(2,1)S(1)}, bf16[16,1536]{1,0:T(8,128)(2,1)S(1)}, u32[]{:S(2)}, u32[]{:S(2)}) collective-permute-start(bf16[16,1536]{1,0:T(8,128)(2,1)S(1)} %get-tuple-element.32), channel_id=1, source_target_pairs={{1,0},{2,1},{3,2},{4,3},{5,4},{6,5},{7,6},{8,7},{9,8},{10,9},{11,1... | collective-permute-start | bytes 147464 | tf_op jit(solution)/shard_map/ppermute | solution.py:334
  146.3 4.8 %inner.2 = (bf16[256,1536]{1,0:T(8,128)(2,1)S(1)}, bf16[256,1536]{1,0:T(8,128)(2,1)S(1)}) custom-call(bf16[256,1536]{1,0:T(8,128)(2,1)S(1)} %get-tuple-element.18.g_ref, f32[256,1536]{1,0:T(8,128)S(1)} %get-tuple-element.19.x1_ref, f32[32,1536]{1,0:T(8,128)S(1)} %pad.4.taps_ref, f32[256,1]{1,0:T(8,128)S(1)} %fusion.valid_ref, ...), custom_call_target="tpu_custom_call" | custom-call | tf_op jit(solution)/shard_map/inner/pallas_call | solution.py:287
  152.0 2.1 %collective-permute-start.7 = (bf16[256,1536]{1,0:T(8,128)(2,1)S(1)}, bf16[256,1536]{1,0:T(8,128)(2,1)S(1)}, u32[]{:S(2)}, u32[]{:S(2)}) collective-permute-start(bf16[256,1536]{1,0:T(8,128)(2,1)S(1)} %get-tuple-element.22.h_ref), channel_id=1, source_target_pairs={{0,1},{1,2},{2,3},{3,4},{4,5},{5,6},{6,7},{7,8},{8,9},{9,10},{10,1... | collective-permute-start | bytes 2359304 | tf_op jit(solution)/shard_map/ppermute | solution.py:334
  154.1 4.8 %project.1.own_ref = bf16[4,256,1152]{2,1,0:T(8,128)(2,1)S(1)} custom-call(bf16[256,1536]{1,0:T(8,128)(2,1)S(1)} %get-tuple-element.22.h_ref, bf16[4,1536,1152]{2,1,0:T(8,128)(2,1)S(1)} %get-tuple-element.23.w_ref), custom_call_target="tpu_custom_call" | custom-call | tf_op jit(solution)/shard_map/project/pallas_call | solution.py:72
  158.9 8.7 %collective-permute-done.7.left_ref = bf16[256,1536]{1,0:T(8,128)(2,1)S(1)} collective-permute-done((bf16[256,1536]{1,0:T(8,128)(2,1)S(1)}, bf16[256,1536]{1,0:T(8,128)(2,1)S(1)}, u32[]{:S(2)}, u32[]{:S(2)}) %collective-permute-start.7) | collective-permute-done | bytes 786464 | tf_op jit(solution)/shard_map/ppermute | solution.py:334
  167.6 5.0 %copy-done.2 = bf16[4,1536,1152]{2,1,0:T(8,128)(2,1)S(1)} copy-done((bf16[4,1536,1152]{2,1,0:T(8,128)(2,1)S(1)}, bf16[4,1536,1152]{2,1,0:T(8,128)(2,1)}, u32[]{:S(2)}) %copy-start.2) | copy-done | bytes 14155800
  172.6 11.7 %attend.1 = (f32[256,1536]{1,0:T(8,128)S(1)}, bf16[256,1536]{1,0:T(8,128)(2,1)S(1)}) custom-call(bf16[256,1536]{1,0:T(8,128)(2,1)S(1)} %collective-permute-done.7.left_ref, bf16[4,256,1152]{2,1,0:T(8,128)(2,1)S(1)} %project.1.own_ref, bf16[4,1536,1152]{2,1,0:T(8,128)(2,1)S(1)} %copy-done.2, bf16[1536,1536]{1,0:T(8,128)(2,1)S(1)} %bitcast.9, ...), custom_call_target="tpu_custom_call" | custom-call | tf_op jit(solution)/shard_map/attend/pallas_call | solution.py:237
  184.3 1.9 collective-permute-start.8
  186.3 6.0 %collective-permute-start.9 = (bf16[16,1536]{1,0:T(8,128)(2,1)S(1)}, bf16[16,1536]{1,0:T(8,128)(2,1)S(1)}, u32[]{:S(2)}, u32[]{:S(2)}) collective-permute-start(bf16[16,1536]{1,0:T(8,128)(2,1)S(1)} %get-tuple-element.30), channel_id=1, source_target_pairs={{1,0},{2,1},{3,2},{4,3},{5,4},{6,5},{7,6},{8,7},{9,8},{10,9},{11,1... | collective-permute-start | bytes 147464 | tf_op jit(solution)/shard_map/ppermute | solution.py:334
  192.2 3.9 %inner.3.rest_0_ = bf16[256,1536]{1,0:T(8,128)(2,1)S(1)} custom-call(bf16[256,1536]{1,0:T(8,128)(2,1)S(1)} %get-tuple-element.25.g_ref, f32[256,1536]{1,0:T(8,128)S(1)} %get-tuple-element.26.x1_ref, f32[32,1536]{1,0:T(8,128)S(1)} %pad.4.taps_ref, f32[256,1]{1,0:T(8,128)S(1)} %fusion.valid_ref, f32[1,1536]{1,0:T(1,128)S(1)} %broadcast_in_dim.44.gain_ref), custom_call_target="tpu_custom_call" | custom-call | tf_op jit(solution)/shard_map/inner/pallas_call | solution.py:287
  (50 shorter events, 10.7 us)
Async XLA Ops:
  6.5 28.8 %copy-start = (s32[16,16]{1,0:T(8,128)S(1)}, s32[16,16]{1,0:T(8,128)}, u32[]{:S(2)}) copy-start(s32[16,16]{1,0:T(8,128)} %param.9) | copy-start | bytes 3076
  6.5 57.9 %copy-start.5 = (f32[1536]{0:T(1024)S(1)}, f32[1536]{0:T(1024)}, u32[]{:S(2)}) copy-start(f32[1536]{0:T(1024)} %param.11) | copy-start | bytes 18436
  6.5 81.4 %copy-start.6 = (f32[1536]{0:T(1024)S(1)}, f32[1536]{0:T(1024)}, u32[]{:S(2)}) copy-start(f32[1536]{0:T(1024)} %param.14) | copy-start | bytes 18436
  6.5 81.4 %copy-start.7 = (s32[16]{0:T(128)S(1)}, s32[16]{0:T(128)}, u32[]{:S(2)}) copy-start(s32[16]{0:T(128)} %param.10) | copy-start | bytes 196
  6.5 111.0 %all-gather.2.cloned.1.call-start = ((), (), s32[]{:S(2)}) async-start(), calls=%async_computation.2 | async-start | bytes 14598144 | tf_op jit(solution)/shard_map/all_gather | solution.py:364
  7.4 10.0 %collective-permute-start.1 = (bf16[48,1152]{1,0:T(8,128)(2,1)S(1)}, bf16[48,1152]{1,0:T(8,128)(2,1)S(1)}, u32[]{:S(2)}, u32[]{:S(2)}) collective-permute-start(bf16[48,1152]{1,0:T(8,128)(2,1)S(1)} %pad_maximum_fusion.1), channel_id=1, source_target_pairs={{0,32},{32,64},{64,96},{96,128},{128,160},{160,192},{192,224},{224... | collective-permute-start | bytes 331784 | tf_op jit(solution)/shard_map/ppermute | solution.py:354
  9.4 12.9 %collective-permute-start.2 = (bf16[48,1152]{1,0:T(8,128)(2,1)S(1)}, bf16[48,1152]{1,0:T(8,128)(2,1)S(1)}, u32[]{:S(2)}, u32[]{:S(2)}) collective-permute-start(bf16[48,1152]{1,0:T(8,128)(2,1)S(1)} %pad_maximum_fusion.1), channel_id=1, source_target_pairs={{0,96},{32,128},{64,160},{96,192},{128,224},{160,0},{192,32},{224,... | collective-permute-start | bytes 331784 | tf_op jit(solution)/shard_map/ppermute | solution.py:354
  15.3 7.1 %collective-permute-start = (bf16[48,1152]{1,0:T(8,128)(2,1)S(1)}, bf16[48,1152]{1,0:T(8,128)(2,1)S(1)}, u32[]{:S(2)}, u32[]{:S(2)}) collective-permute-start(bf16[48,1152]{1,0:T(8,128)(2,1)S(1)} %pad_maximum_fusion.1), channel_id=1, source_target_pairs={{1,129},{33,161},{65,193},{97,225},{129,1},{161,33},{193,65},{225,... | collective-permute-start | bytes 331784 | tf_op jit(solution)/shard_map/ppermute | solution.py:354
  15.9 11.0 %collective-permute-start.3 = (bf16[48,1152]{1,0:T(8,128)(2,1)S(1)}, bf16[48,1152]{1,0:T(8,128)(2,1)S(1)}, u32[]{:S(2)}, u32[]{:S(2)}) collective-permute-start(bf16[48,1152]{1,0:T(8,128)(2,1)S(1)} %pad_maximum_fusion.1), channel_id=1, source_target_pairs={{0,64},{32,96},{64,128},{96,160},{128,192},{160,224},{192,0},{224,... | collective-permute-start | bytes 331784 | tf_op jit(solution)/shard_map/ppermute | solution.py:354
  27.8 29.0 %all-to-all-start = ((bf16[16,16,1536]{2,1,0:T(8,128)(2,1)}), bf16[16,16,1536]{2,1,0:T(8,128)(2,1)S(1)}, u32[]{:S(2)}, u32[]{:S(2)}) async-start(bf16[16,16,1536]{2,1,0:T(8,128)(2,1)} %bitcast.13), calls=%async_computation | async-start | bytes 1572864 | tf_op jit(solution)/shard_map/all_to_all | solution.py:378
  58.2 27.3 %all-to-all-start.1 = ((bf16[16,16,1536]{2,1,0:T(8,128)(2,1)}), bf16[16,16,1536]{2,1,0:T(8,128)(2,1)S(1)}, u32[]{:S(2)}, u32[]{:S(2)}) async-start(bf16[16,16,1536]{2,1,0:T(8,128)(2,1)} %pick.1), calls=%async_computation.1 | async-start | bytes 1572864 | tf_op jit(solution)/shard_map/all_to_all | solution.py:380
  86.0 27.0 %collective-permute-start.4 = (bf16[256,1536]{1,0:T(8,128)(2,1)S(1)}, bf16[256,1536]{1,0:T(8,128)(2,1)S(1)}, u32[]{:S(2)}, u32[]{:S(2)}) collective-permute-start(bf16[256,1536]{1,0:T(8,128)(2,1)S(1)} %head.1.h_ref), channel_id=1, source_target_pairs={{0,1},{1,2},{2,3},{3,4},{4,5},{5,6},{6,7},{7,8},{8,9},{9,10},{10,1... | collective-permute-start | bytes 2359304 | tf_op jit(solution)/shard_map/ppermute | solution.py:334
  117.5 2.3 %copy-start.3 = (bf16[1536,1536]{1,0:T(8,128)(2,1)S(1)}, bf16[1536,1536]{1,0:T(8,128)(2,1)}, u32[]{:S(2)}) copy-start(bf16[1536,1536]{1,0:T(8,128)(2,1)} %wout_ref.3) | copy-start | bytes 14155780
  119.9 26.4 %copy-start.4 = (f32[31,1536]{1,0:T(8,128)S(1)}, f32[31,1536]{1,0:T(8,128)}, u32[]{:S(2)}) copy-start(f32[31,1536]{1,0:T(8,128)} %param.15) | copy-start | bytes 571396
  138.3 20.6 %copy-start.1 = (bf16[4,1536,1152]{2,1,0:T(8,128)(2,1)}, bf16[4,1536,1152]{2,1,0:T(8,128)(2,1)S(1)}, u32[]{:S(2)}) copy-start(bf16[4,1536,1152]{2,1,0:T(8,128)(2,1)S(1)} %get-tuple-element.23.w_ref) | copy-start | bytes 42467332
  138.4 12.7 %collective-permute-start.5 = (bf16[16,1536]{1,0:T(8,128)(2,1)S(1)}, bf16[16,1536]{1,0:T(8,128)(2,1)S(1)}, u32[]{:S(2)}, u32[]{:S(2)}) collective-permute-start(bf16[16,1536]{1,0:T(8,128)(2,1)S(1)} %get-tuple-element.33), channel_id=1, source_target_pairs={{0,1},{1,2},{2,3},{3,4},{4,5},{5,6},{6,7},{7,8},{8,9},{9,10},{10,1... | collective-permute-start | bytes 147464 | tf_op jit(solution)/shard_map/ppermute | solution.py:334
  140.5 10.6 %collective-permute-start.6 = (bf16[16,1536]{1,0:T(8,128)(2,1)S(1)}, bf16[16,1536]{1,0:T(8,128)(2,1)S(1)}, u32[]{:S(2)}, u32[]{:S(2)}) collective-permute-start(bf16[16,1536]{1,0:T(8,128)(2,1)S(1)} %get-tuple-element.32), channel_id=1, source_target_pairs={{1,0},{2,1},{3,2},{4,3},{5,4},{6,5},{7,6},{8,7},{9,8},{10,9},{11,1... | collective-permute-start | bytes 147464 | tf_op jit(solution)/shard_map/ppermute | solution.py:334
  151.1 16.5 %slice-start = ((s8[4718592]{0:T(1024)(128)(4,1)}), s8[4194304]{0:T(1024)(128)(4,1)S(1)}, s32[]{:S(2)}) async-start(s8[4718592]{0:T(1024)(128)(4,1)} %bitcast.8), calls=%async_computation.3 | async-start | bytes 8388608
  152.0 15.6 %collective-permute-start.7 = (bf16[256,1536]{1,0:T(8,128)(2,1)S(1)}, bf16[256,1536]{1,0:T(8,128)(2,1)S(1)}, u32[]{:S(2)}, u32[]{:S(2)}) collective-permute-start(bf16[256,1536]{1,0:T(8,128)(2,1)S(1)} %get-tuple-element.22.h_ref), channel_id=1, source_target_pairs={{0,1},{1,2},{2,3},{3,4},{4,5},{5,6},{6,7},{7,8},{8,9},{9,10},{10,1... | collective-permute-start | bytes 2359304 | tf_op jit(solution)/shard_map/ppermute | solution.py:334
  154.1 13.5 %slice-start.1 = ((s8[4718592]{0:T(1024)(128)(4,1)}), s8[524288]{0:T(1024)(128)(4,1)S(1)}, s32[]{:S(2)}) async-start(s8[4718592]{0:T(1024)(128)(4,1)} %bitcast.8), calls=%async_computation.4 | async-start | bytes 1048576
  167.6 5.0 %copy-start.2 = (bf16[4,1536,1152]{2,1,0:T(8,128)(2,1)S(1)}, bf16[4,1536,1152]{2,1,0:T(8,128)(2,1)}, u32[]{:S(2)}) copy-start(bf16[4,1536,1152]{2,1,0:T(8,128)(2,1)} %copy-done.1) | copy-start | bytes 42467332
  184.3 11.8 %collective-permute-start.8 = (bf16[16,1536]{1,0:T(8,128)(2,1)S(1)}, bf16[16,1536]{1,0:T(8,128)(2,1)S(1)}, u32[]{:S(2)}, u32[]{:S(2)}) collective-permute-start(bf16[16,1536]{1,0:T(8,128)(2,1)S(1)} %get-tuple-element.31), channel_id=1, source_target_pairs={{0,1},{1,2},{2,3},{3,4},{4,5},{5,6},{6,7},{7,8},{8,9},{9,10},{10,1... | collective-permute-start | bytes 147464 | tf_op jit(solution)/shard_map/ppermute | solution.py:334
  186.3 9.9 %collective-permute-start.9 = (bf16[16,1536]{1,0:T(8,128)(2,1)S(1)}, bf16[16,1536]{1,0:T(8,128)(2,1)S(1)}, u32[]{:S(2)}, u32[]{:S(2)}) collective-permute-start(bf16[16,1536]{1,0:T(8,128)(2,1)S(1)} %get-tuple-element.30), channel_id=1, source_target_pairs={{1,0},{2,1},{3,2},{4,3},{5,4},{6,5},{7,6},{8,7},{9,8},{10,9},{11,1... | collective-permute-start | bytes 147464 | tf_op jit(solution)/shard_map/ppermute | solution.py:334
Sparse Core Ops, SparseCore 0:
  27.9 89.5 all-gather.1

commit v3 on v2

--- a/solution.py
+++ b/solution.py
@@ -23,6 +23,14 @@
     return pltpu.CompilerParams(vmem_limit_bytes=VMEM, **kw)
 
 
+def in_vmem(v):
+    return pltpu.with_memory_space_constraint(v, pltpu.VMEM)
+
+
+def in_hbm(v):
+    return pltpu.with_memory_space_constraint(v, pltpu.HBM)
+
+
 def normed(v):
     mean = jnp.mean(v, axis=-1, keepdims=True)
     d = v - mean
@@ -63,24 +71,18 @@
 
 
 def project_kernel(h_ref, w_ref, out_ref):
-    out_ref[0] = jnp.dot(h_ref[...], w_ref[0], preferred_element_type=F32).astype(BF)
+    for b in range(w_ref.shape[0]):
+        out_ref[b] = jnp.dot(h_ref[...], w_ref[b], preferred_element_type=F32).astype(BF)
 
 
 def project(h, w):
-    blocks, depth, cols = w.shape
-    span, width = h.shape
+    blocks, _, cols = w.shape
     return pl.pallas_call(
         project_kernel,
-        grid=(blocks,),
-        out_shape=jax.ShapeDtypeStruct((blocks, span, cols), BF),
-        in_specs=[
-            pl.BlockSpec((span, width), lambda b: (0, 0)),
-            pl.BlockSpec((1, depth, cols), lambda b: (b, 0, 0)),
-        ],
-        out_specs=pl.BlockSpec((1, span, cols), lambda b: (b, 0, 0)),
+        out_shape=pltpu.VMEM((blocks, h.shape[0], cols), BF),
         compiler_params=params(),
         name="project",
-    )(h, w)
+    )(h, in_vmem(w))
 
 
 def heads(query, keys, values, bias):
@@ -127,52 +129,39 @@
 
 def opening_kernel(
     z_ref, left_ref, h_ref, w_ref, wout_ref, x_ref, bias_ref, gain_ref, valid_ref,
-    x1_ref, g_ref, wall_ref, acc_ref, both_ref, buf_ref, in_sem, out_sem,
+    x1_ref, g_ref, wall_ref, acc_ref, both_ref, sem,
 ):
     b = pl.program_id(0)
     last = pl.num_programs(0) - 1
-    slot = lax.rem(b, 2)
     span = h_ref.shape[0]
     group = wout_ref.shape[0]
     parts, _, zs, rows, _ = w_ref.shape
 
-    def fetch(block, to):
+    def fetch(block):
         for part in range(parts):
             for z in range(zs):
                 at = (z * parts + part) * rows
                 pltpu.make_async_copy(
                     w_ref.at[part, block, lax.rem(z_ref[0] - z + zs, zs)],
-                    buf_ref.at[to, pl.ds(at, rows)],
-                    in_sem.at[to],
+                    wall_ref.at[block, pl.ds(at, rows)],
+                    sem.at[block],
                 ).start()
-
-    def saved(block, at):
-        return pltpu.make_async_copy(buf_ref.at[at], wall_ref.at[block], out_sem.at[at])
 
     @pl.when(b == 0)
     def _():
-        fetch(0, 0)
+        fetch(0)
         both_ref[pl.ds(0, span), :] = left_ref[...]
         both_ref[pl.ds(span, span), :] = h_ref[...]
 
-    @pl.when(b > 0)
-    def _():
-        saved(b - 1, 1 - slot).wait()
-
     @pl.when(b < last)
     def _():
-        fetch(b + 1, 1 - slot)
-
-    pltpu.make_async_copy(wall_ref.at[b], buf_ref.at[slot], in_sem.at[slot]).wait()
-    saved(b, slot).start()
-    kv = jnp.dot(both_ref[...], buf_ref[slot, :, : 2 * group], preferred_element_type=F32).astype(BF)
-    q = jnp.dot(h_ref[...], buf_ref[slot, :, 2 * group :], preferred_element_type=F32).astype(BF)
+        fetch(b + 1)
+
+    pltpu.make_async_copy(wall_ref.at[b], wall_ref.at[b], sem.at[b]).wait()
+    kv = jnp.dot(both_ref[...], wall_ref[b, :, : 2 * group], preferred_element_type=F32).astype(BF)
+    q = jnp.dot(h_ref[...], wall_ref[b, :, 2 * group :], preferred_element_type=F32).astype(BF)
     ctx = heads(q, kv[:, :group], kv[:, group:], bias_ref[...])
     settle(ctx, wout_ref, x_ref, gain_ref, valid_ref, x1_ref, g_ref, acc_ref)
-
-    @pl.when(b == last)
-    def _():
-        saved(b, slot).wait()
 
 
 def whole(*shape):
@@ -190,7 +179,7 @@
         out_shape=(
             jax.ShapeDtypeStruct((span, width), F32),
             jax.ShapeDtypeStruct((span, width), BF),
-            jax.ShapeDtypeStruct((blocks, depth, cols), BF),
+            pltpu.VMEM((blocks, depth, cols), BF),
         ),
         in_specs=[
             pl.BlockSpec(memory_space=pltpu.SMEM),
@@ -203,17 +192,15 @@
             whole(1, width),
             whole(span, 1),
         ],
-        out_specs=(whole(span, width), whole(span, width), pl.BlockSpec(memory_space=pl.ANY)),
+        out_specs=(whole(span, width), whole(span, width), pl.BlockSpec(memory_space=pltpu.VMEM)),
         scratch_shapes=[
             pltpu.VMEM((span, width), F32),
             pltpu.VMEM((2 * span, width), BF),
-            pltpu.VMEM((2, depth, cols), BF),
-            pltpu.SemaphoreType.DMA((2,)),
-            pltpu.SemaphoreType.DMA((2,)),
+            pltpu.SemaphoreType.DMA((blocks,)),
         ],
         compiler_params=params(),
         name="opening",
-    )(z, left, h, w, w_out, x, bias, gain, valid)
+    )(z, left, h, w, in_hbm(w_out), x, bias, gain, valid)
 
 
 def attend_kernel(
@@ -222,7 +209,7 @@
 ):
     b = pl.program_id(0)
     group = wout_ref.shape[0]
-    left = jnp.dot(left_ref[...], w_ref[0], preferred_element_type=F32).astype(BF)
+    left = jnp.dot(left_ref[...], w_ref[b, :, : 2 * group], preferred_element_type=F32).astype(BF)
     own = own_ref[b]
     keys = jnp.concatenate([left[:, :group], own[:, :group]], axis=0)
     values = jnp.concatenate([left[:, group:], own[:, group : 2 * group]], axis=0)
@@ -231,7 +218,7 @@
 
 
 def attend(left, own, w, w_out, x, bias, gain, valid):
-    blocks, depth, cols = w.shape
+    blocks = w.shape[0]
     span, width = x.shape
     group = width // blocks
     return pl.pallas_call(
@@ -244,7 +231,7 @@
         in_specs=[
             whole(span, width),
             pl.BlockSpec(memory_space=pltpu.VMEM),
-            pl.BlockSpec((1, depth, 2 * group), lambda b: (b, 0, 0)),
+            pl.BlockSpec(memory_space=pltpu.VMEM),
             pl.BlockSpec((group, width), lambda b: (b, 0)),
             whole(span, width),
             whole(2 * span, 128),
@@ -255,7 +242,7 @@
         scratch_shapes=[pltpu.VMEM((span, width), F32)],
         compiler_params=params(),
         name="attend",
-    )(left, own, w, w_out, x, bias, gain, valid)
+    )(left, in_vmem(own), in_vmem(w), in_hbm(w_out), x, bias, gain, valid)
 
 
 def taps_over(pad_ref, taps, rows):

time: 205 us -> 198 us (0.966)
  local copies, waits for them, and re-layouts: 8.95 us -> 1.5 us
    unnamed x20 -> x10, local copies, waits for them, and re-layouts: 7.4 us -> 0.02 us
where the time goes in v3:
time: 198 us; the launch traced here: 197 us
  waiting for transfers between devices  88.6 us (45%)
  Pallas kernels  47.8 us (24%)
  starting transfers between devices  43.5 us (22%)
  between operations  13.7 us (7%)
  other arithmetic  2.19 us (1%)
    all_to_all x2, waiting for transfers between devices, on_device(): chunks = lax.all_to_all(chunks, DP, split_axis=0, concat_axis=0, tiled=True)  42.4 us
    ppermute x6, waiting for transfers between devices, along(): return lax.ppermute(value, SEQ, pairs)  32.4 us
    ppermute x6, starting transfers between devices, along(): return lax.ppermute(value, SEQ, pairs)  19.6 us
    pallas_call x1, Pallas kernels, opening(): pl.pallas_call(opening_kernel, grid=(blocks,), out_shape=(jax.ShapeDtypeS...  18.1 us
    all_to_all x2, starting transfers between devices, on_device(): chunks = lax.all_to_all(chunks, DP, split_axis=0, concat_axis=0, tiled=True)  13.8 us
    pallas_call x1, Pallas kernels, attend(): pl.pallas_call(attend_kernel, grid=(blocks,), out_shape=(jax.ShapeDtypeSt...  12.4 us
    ppermute x4, starting transfers between devices, weight_blocks(): came[k] = lax.ppermute(own, ('z', 'core'), pairs)  10 us
    ppermute x4, waiting for transfers between devices, weight_blocks(): came[k] = lax.ppermute(own, ('z', 'core'), pairs)  9.34 us
  transfers between devices with their start and end apart: 13, of which 7 were waited for; matrix products, arithmetic and copies ran while one was open for 1% of the time, Pallas kernels for 8%

profile of v3, /device:TPU:24, one launch (start us, length us, event | category | flops | bytes accessed | tf_op | source)
XLA Modules:
  0.0 197.3 jit_solution(6331934361367711769)
XLA Ops:
  7.4 2.0 %collective-permute-start.1 = (bf16[48,1152]{1,0:T(8,128)(2,1)S(1)}, bf16[48,1152]{1,0:T(8,128)(2,1)S(1)}, u32[]{:S(2)}, u32[]{:S(2)}) collective-permute-start(bf16[48,1152]{1,0:T(8,128)(2,1)S(1)} %pad_maximum_fusion.1), channel_id=1, source_target_pairs={{0,32},{32,64},{64,96},{96,128},{128,160},{160,192},{192,224},{224... | collective-permute-start | bytes 331784 | tf_op jit(solution)/shard_map/ppermute | solution.py:341
  9.4 5.8 %collective-permute-start.2 = (bf16[48,1152]{1,0:T(8,128)(2,1)S(1)}, bf16[48,1152]{1,0:T(8,128)(2,1)S(1)}, u32[]{:S(2)}, u32[]{:S(2)}) collective-permute-start(bf16[48,1152]{1,0:T(8,128)(2,1)S(1)} %pad_maximum_fusion.1), channel_id=1, source_target_pairs={{0,96},{32,128},{64,160},{96,192},{128,224},{160,0},{192,32},{224,... | collective-permute-start | bytes 331784 | tf_op jit(solution)/shard_map/ppermute | solution.py:341
  15.9 1.5 collective-permute-start.3
  17.5 4.9 %collective-permute-done.2 = bf16[48,1152]{1,0:T(8,128)(2,1)S(1)} collective-permute-done((bf16[48,1152]{1,0:T(8,128)(2,1)S(1)}, bf16[48,1152]{1,0:T(8,128)(2,1)S(1)}, u32[]{:S(2)}, u32[]{:S(2)}) %collective-permute-start.2) | collective-permute-done | bytes 110624 | tf_op jit(solution)/shard_map/ppermute | solution.py:341
  22.4 4.5 %collective-permute-done.3 = bf16[48,1152]{1,0:T(8,128)(2,1)S(1)} collective-permute-done((bf16[48,1152]{1,0:T(8,128)(2,1)S(1)}, bf16[48,1152]{1,0:T(8,128)(2,1)S(1)}, u32[]{:S(2)}, u32[]{:S(2)}) %collective-permute-start.3) | collective-permute-done | bytes 110624 | tf_op jit(solution)/shard_map/ppermute | solution.py:341
  27.8 7.6 %all-to-all-start = ((bf16[16,16,1536]{2,1,0:T(8,128)(2,1)}), bf16[16,16,1536]{2,1,0:T(8,128)(2,1)S(1)}, u32[]{:S(2)}, u32[]{:S(2)}) async-start(bf16[16,16,1536]{2,1,0:T(8,128)(2,1)} %bitcast.11), calls=%async_computation | async-start | bytes 1572864 | tf_op jit(solution)/shard_map/all_to_all | solution.py:365
  35.3 21.4 %all-to-all-done.in_ref = bf16[16,16,1536]{2,1,0:T(8,128)(2,1)S(1)} async-done(((bf16[16,16,1536]{2,1,0:T(8,128)(2,1)}), bf16[16,16,1536]{2,1,0:T(8,128)(2,1)S(1)}, u32[]{:S(2)}, u32[]{:S(2)}) %all-to-all-start) | async-done | bytes 786464 | tf_op jit(solution)/shard_map/all_to_all | solution.py:365
  58.2 6.3 %all-to-all-start.1 = ((bf16[16,16,1536]{2,1,0:T(8,128)(2,1)}), bf16[16,16,1536]{2,1,0:T(8,128)(2,1)S(1)}, u32[]{:S(2)}, u32[]{:S(2)}) async-start(bf16[16,16,1536]{2,1,0:T(8,128)(2,1)} %pick.1), calls=%async_computation.1 | async-start | bytes 1572864 | tf_op jit(solution)/shard_map/all_to_all | solution.py:367
  64.5 21.0 %all-to-all-done.1 = bf16[16,16,1536]{2,1,0:T(8,128)(2,1)S(1)} async-done(((bf16[16,16,1536]{2,1,0:T(8,128)(2,1)}), bf16[16,16,1536]{2,1,0:T(8,128)(2,1)S(1)}, u32[]{:S(2)}, u32[]{:S(2)}) %all-to-all-start.1) | async-done | bytes 786464 | tf_op jit(solution)/shard_map/all_to_all | solution.py:367
  86.0 1.9 collective-permute-start.4
  89.9 23.1 %collective-permute-done.4.left_ref = bf16[256,1536]{1,0:T(8,128)(2,1)S(1)} collective-permute-done((bf16[256,1536]{1,0:T(8,128)(2,1)S(1)}, bf16[256,1536]{1,0:T(8,128)(2,1)S(1)}, u32[]{:S(2)}, u32[]{:S(2)}) %collective-permute-start.4) | collective-permute-done | bytes 786464 | tf_op jit(solution)/shard_map/ppermute | solution.py:321
  113.0 4.5 %all-gather.2.cloned.1.call-done = bf16[6144,1152]{1,0:T(8,128)(2,1)} async-done(((bf16[192,1152]{1,0:T(8,128)(2,1)}), bf16[6144,1152]{1,0:T(8,128)(2,1)}) %all-gather.2.cloned.1.call-update) | async-done | bytes 14155792 | tf_op jit(solution)/shard_map/all_gather | solution.py:351
  117.5 18.1 %opening.1 = (f32[256,1536]{1,0:T(8,128)S(1)}, bf16[256,1536]{1,0:T(8,128)(2,1)S(1)}, bf16[4,1536,1152]{2,1,0:T(8,128)(2,1)S(1)}) custom-call(s32[1]{0:T(128)} %bitcast.z_ref, bf16[256,1536]{1,0:T(8,128)(2,1)S(1)} %collective-permute-done.4.left_ref, bf16[256,1536]{1,0:T(8,128)(2,1)S(1)} %head.1.h_ref, bf16[4,4,8,48,1152]{4,3,2,1,0:T(8,128)(2,1)} %bitcast.10, ...), custom_call_target="tpu_custom_call" | custom-call | tf_op jit(solution)/shard_map/opening/pallas_call | solution.py:176
  135.6 2.2 %collective-permute-start.5 = (bf16[16,1536]{1,0:T(8,128)(2,1)S(1)}, bf16[16,1536]{1,0:T(8,128)(2,1)S(1)}, u32[]{:S(2)}, u32[]{:S(2)}) collective-permute-start(bf16[16,1536]{1,0:T(8,128)(2,1)S(1)} %get-tuple-element.33), channel_id=1, source_target_pairs={{0,1},{1,2},{2,3},{3,4},{4,5},{5,6},{6,7},{7,8},{8,9},{9,10},{10,1... | collective-permute-start | bytes 147464 | tf_op jit(solution)/shard_map/ppermute | solution.py:321
  137.8 5.7 %collective-permute-start.6 = (bf16[16,1536]{1,0:T(8,128)(2,1)S(1)}, bf16[16,1536]{1,0:T(8,128)(2,1)S(1)}, u32[]{:S(2)}, u32[]{:S(2)}) collective-permute-start(bf16[16,1536]{1,0:T(8,128)(2,1)S(1)} %get-tuple-element.32), channel_id=1, source_target_pairs={{1,0},{2,1},{3,2},{4,3},{5,4},{6,5},{7,6},{8,7},{9,8},{10,9},{11,1... | collective-permute-start | bytes 147464 | tf_op jit(solution)/shard_map/ppermute | solution.py:321
  143.5 4.8 %inner.2 = (bf16[256,1536]{1,0:T(8,128)(2,1)S(1)}, bf16[256,1536]{1,0:T(8,128)(2,1)S(1)}) custom-call(bf16[256,1536]{1,0:T(8,128)(2,1)S(1)} %get-tuple-element.18.g_ref, f32[256,1536]{1,0:T(8,128)S(1)} %get-tuple-element.19.x1_ref, f32[32,1536]{1,0:T(8,128)S(1)} %pad.4.taps_ref, f32[256,1]{1,0:T(8,128)S(1)} %fusion.valid_ref, ...), custom_call_target="tpu_custom_call" | custom-call | tf_op jit(solution)/shard_map/inner/pallas_call | solution.py:274
  149.3 1.9 collective-permute-start.7
  151.2 4.2 %project.1.own_ref = bf16[4,256,1152]{2,1,0:T(8,128)(2,1)S(1)} custom-call(bf16[256,1536]{1,0:T(8,128)(2,1)S(1)} %get-tuple-element.22.h_ref, bf16[4,1536,1152]{2,1,0:T(8,128)(2,1)S(1)} %get-tuple-element.23.w_ref), custom_call_target="tpu_custom_call" | custom-call | tf_op jit(solution)/shard_map/project/pallas_call | solution.py:80
  155.4 9.2 %collective-permute-done.7.left_ref = bf16[256,1536]{1,0:T(8,128)(2,1)S(1)} collective-permute-done((bf16[256,1536]{1,0:T(8,128)(2,1)S(1)}, bf16[256,1536]{1,0:T(8,128)(2,1)S(1)}, u32[]{:S(2)}, u32[]{:S(2)}) %collective-permute-start.7) | collective-permute-done | bytes 786464 | tf_op jit(solution)/shard_map/ppermute | solution.py:321
  164.7 12.4 %attend.1 = (f32[256,1536]{1,0:T(8,128)S(1)}, bf16[256,1536]{1,0:T(8,128)(2,1)S(1)}) custom-call(bf16[256,1536]{1,0:T(8,128)(2,1)S(1)} %collective-permute-done.7.left_ref, bf16[4,256,1152]{2,1,0:T(8,128)(2,1)S(1)} %project.1.own_ref, bf16[4,1536,1152]{2,1,0:T(8,128)(2,1)S(1)} %get-tuple-element.23.w_ref, bf16[1536,1536]{1,0:T(8,128)(2,1)} %wout_ref.3, ...), custom_call_target="tpu_custom_call" | custom-call | tf_op jit(solution)/shard_map/attend/pallas_call | solution.py:224
  177.1 1.9 collective-permute-start.8
  179.0 6.0 %collective-permute-start.9 = (bf16[16,1536]{1,0:T(8,128)(2,1)S(1)}, bf16[16,1536]{1,0:T(8,128)(2,1)S(1)}, u32[]{:S(2)}, u32[]{:S(2)}) collective-permute-start(bf16[16,1536]{1,0:T(8,128)(2,1)S(1)} %get-tuple-element.30), channel_id=1, source_target_pairs={{1,0},{2,1},{3,2},{4,3},{5,4},{6,5},{7,6},{8,7},{9,8},{10,9},{11,1... | collective-permute-start | bytes 147464 | tf_op jit(solution)/shard_map/ppermute | solution.py:321
  185.0 3.8 %inner.3.rest_0_ = bf16[256,1536]{1,0:T(8,128)(2,1)S(1)} custom-call(bf16[256,1536]{1,0:T(8,128)(2,1)S(1)} %get-tuple-element.25.g_ref, f32[256,1536]{1,0:T(8,128)S(1)} %get-tuple-element.26.x1_ref, f32[32,1536]{1,0:T(8,128)S(1)} %pad.4.taps_ref, f32[256,1]{1,0:T(8,128)S(1)} %fusion.valid_ref, f32[1,1536]{1,0:T(1,128)S(1)} %broadcast_in_dim.44.gain_ref), custom_call_target="tpu_custom_call" | custom-call | tf_op jit(solution)/shard_map/inner/pallas_call | solution.py:274
  188.9 1.5 edges.3
  (39 shorter events, 7.3 us)
Async XLA Ops:
  6.5 28.8 %copy-start = (s32[16,16]{1,0:T(8,128)S(1)}, s32[16,16]{1,0:T(8,128)}, u32[]{:S(2)}) copy-start(s32[16,16]{1,0:T(8,128)} %param.9) | copy-start | bytes 3076
  6.5 57.9 %copy-start.2 = (f32[1536]{0:T(1024)S(1)}, f32[1536]{0:T(1024)}, u32[]{:S(2)}) copy-start(f32[1536]{0:T(1024)} %param.11) | copy-start | bytes 18436
  6.5 81.4 %copy-start.3 = (f32[1536]{0:T(1024)S(1)}, f32[1536]{0:T(1024)}, u32[]{:S(2)}) copy-start(f32[1536]{0:T(1024)} %param.14) | copy-start | bytes 18436
  6.5 81.4 %copy-start.4 = (s32[16]{0:T(128)S(1)}, s32[16]{0:T(128)}, u32[]{:S(2)}) copy-start(s32[16]{0:T(128)} %param.10) | copy-start | bytes 196
  6.5 111.0 %all-gather.2.cloned.1.call-start = ((), (), s32[]{:S(2)}) async-start(), calls=%async_computation.2 | async-start | bytes 14598144 | tf_op jit(solution)/shard_map/all_gather | solution.py:351
  7.4 10.0 %collective-permute-start.1 = (bf16[48,1152]{1,0:T(8,128)(2,1)S(1)}, bf16[48,1152]{1,0:T(8,128)(2,1)S(1)}, u32[]{:S(2)}, u32[]{:S(2)}) collective-permute-start(bf16[48,1152]{1,0:T(8,128)(2,1)S(1)} %pad_maximum_fusion.1), channel_id=1, source_target_pairs={{0,32},{32,64},{64,96},{96,128},{128,160},{160,192},{192,224},{224... | collective-permute-start | bytes 331784 | tf_op jit(solution)/shard_map/ppermute | solution.py:341
  9.4 12.9 %collective-permute-start.2 = (bf16[48,1152]{1,0:T(8,128)(2,1)S(1)}, bf16[48,1152]{1,0:T(8,128)(2,1)S(1)}, u32[]{:S(2)}, u32[]{:S(2)}) collective-permute-start(bf16[48,1152]{1,0:T(8,128)(2,1)S(1)} %pad_maximum_fusion.1), channel_id=1, source_target_pairs={{0,96},{32,128},{64,160},{96,192},{128,224},{160,0},{192,32},{224,... | collective-permute-start | bytes 331784 | tf_op jit(solution)/shard_map/ppermute | solution.py:341
  15.3 7.1 %collective-permute-start = (bf16[48,1152]{1,0:T(8,128)(2,1)S(1)}, bf16[48,1152]{1,0:T(8,128)(2,1)S(1)}, u32[]{:S(2)}, u32[]{:S(2)}) collective-permute-start(bf16[48,1152]{1,0:T(8,128)(2,1)S(1)} %pad_maximum_fusion.1), channel_id=1, source_target_pairs={{1,129},{33,161},{65,193},{97,225},{129,1},{161,33},{193,65},{225,... | collective-permute-start | bytes 331784 | tf_op jit(solution)/shard_map/ppermute | solution.py:341
  15.9 11.0 %collective-permute-start.3 = (bf16[48,1152]{1,0:T(8,128)(2,1)S(1)}, bf16[48,1152]{1,0:T(8,128)(2,1)S(1)}, u32[]{:S(2)}, u32[]{:S(2)}) collective-permute-start(bf16[48,1152]{1,0:T(8,128)(2,1)S(1)} %pad_maximum_fusion.1), channel_id=1, source_target_pairs={{0,64},{32,96},{64,128},{96,160},{128,192},{160,224},{192,0},{224,... | collective-permute-start | bytes 331784 | tf_op jit(solution)/shard_map/ppermute | solution.py:341
  27.8 29.0 %all-to-all-start = ((bf16[16,16,1536]{2,1,0:T(8,128)(2,1)}), bf16[16,16,1536]{2,1,0:T(8,128)(2,1)S(1)}, u32[]{:S(2)}, u32[]{:S(2)}) async-start(bf16[16,16,1536]{2,1,0:T(8,128)(2,1)} %bitcast.11), calls=%async_computation | async-start | bytes 1572864 | tf_op jit(solution)/shard_map/all_to_all | solution.py:365
  58.2 27.3 %all-to-all-start.1 = ((bf16[16,16,1536]{2,1,0:T(8,128)(2,1)}), bf16[16,16,1536]{2,1,0:T(8,128)(2,1)S(1)}, u32[]{:S(2)}, u32[]{:S(2)}) async-start(bf16[16,16,1536]{2,1,0:T(8,128)(2,1)} %pick.1), calls=%async_computation.1 | async-start | bytes 1572864 | tf_op jit(solution)/shard_map/all_to_all | solution.py:367
  86.0 27.0 %collective-permute-start.4 = (bf16[256,1536]{1,0:T(8,128)(2,1)S(1)}, bf16[256,1536]{1,0:T(8,128)(2,1)S(1)}, u32[]{:S(2)}, u32[]{:S(2)}) collective-permute-start(bf16[256,1536]{1,0:T(8,128)(2,1)S(1)} %head.1.h_ref), channel_id=1, source_target_pairs={{0,1},{1,2},{2,3},{3,4},{4,5},{5,6},{6,7},{7,8},{8,9},{9,10},{10,1... | collective-permute-start | bytes 2359304 | tf_op jit(solution)/shard_map/ppermute | solution.py:321
  117.5 26.0 %copy-start.1 = (f32[31,1536]{1,0:T(8,128)S(1)}, f32[31,1536]{1,0:T(8,128)}, u32[]{:S(2)}) copy-start(f32[31,1536]{1,0:T(8,128)} %param.15) | copy-start | bytes 571396
  135.6 12.7 %collective-permute-start.5 = (bf16[16,1536]{1,0:T(8,128)(2,1)S(1)}, bf16[16,1536]{1,0:T(8,128)(2,1)S(1)}, u32[]{:S(2)}, u32[]{:S(2)}) collective-permute-start(bf16[16,1536]{1,0:T(8,128)(2,1)S(1)} %get-tuple-element.33), channel_id=1, source_target_pairs={{0,1},{1,2},{2,3},{3,4},{4,5},{5,6},{6,7},{7,8},{8,9},{9,10},{10,1... | collective-permute-start | bytes 147464 | tf_op jit(solution)/shard_map/ppermute | solution.py:321
  137.8 10.5 %collective-permute-start.6 = (bf16[16,1536]{1,0:T(8,128)(2,1)S(1)}, bf16[16,1536]{1,0:T(8,128)(2,1)S(1)}, u32[]{:S(2)}, u32[]{:S(2)}) collective-permute-start(bf16[16,1536]{1,0:T(8,128)(2,1)S(1)} %get-tuple-element.32), channel_id=1, source_target_pairs={{1,0},{2,1},{3,2},{4,3},{5,4},{6,5},{7,6},{8,7},{9,8},{10,9},{11,1... | collective-permute-start | bytes 147464 | tf_op jit(solution)/shard_map/ppermute | solution.py:321
  149.3 15.4 %collective-permute-start.7 = (bf16[256,1536]{1,0:T(8,128)(2,1)S(1)}, bf16[256,1536]{1,0:T(8,128)(2,1)S(1)}, u32[]{:S(2)}, u32[]{:S(2)}) collective-permute-start(bf16[256,1536]{1,0:T(8,128)(2,1)S(1)} %get-tuple-element.22.h_ref), channel_id=1, source_target_pairs={{0,1},{1,2},{2,3},{3,4},{4,5},{5,6},{6,7},{7,8},{8,9},{9,10},{10,1... | collective-permute-start | bytes 2359304 | tf_op jit(solution)/shard_map/ppermute | solution.py:321
  177.1 11.7 %collective-permute-start.8 = (bf16[16,1536]{1,0:T(8,128)(2,1)S(1)}, bf16[16,1536]{1,0:T(8,128)(2,1)S(1)}, u32[]{:S(2)}, u32[]{:S(2)}) collective-permute-start(bf16[16,1536]{1,0:T(8,128)(2,1)S(1)} %get-tuple-element.31), channel_id=1, source_target_pairs={{0,1},{1,2},{2,3},{3,4},{4,5},{5,6},{6,7},{7,8},{8,9},{9,10},{10,1... | collective-permute-start | bytes 147464 | tf_op jit(solution)/shard_map/ppermute | solution.py:321
  179.0 9.8 %collective-permute-start.9 = (bf16[16,1536]{1,0:T(8,128)(2,1)S(1)}, bf16[16,1536]{1,0:T(8,128)(2,1)S(1)}, u32[]{:S(2)}, u32[]{:S(2)}) collective-permute-start(bf16[16,1536]{1,0:T(8,128)(2,1)S(1)} %get-tuple-element.30), channel_id=1, source_target_pairs={{1,0},{2,1},{3,2},{4,3},{5,4},{6,5},{7,6},{8,7},{9,8},{10,9},{11,1... | collective-permute-start | bytes 147464 | tf_op jit(solution)/shard_map/ppermute | solution.py:321
Sparse Core Ops, SparseCore 0:
  27.9 89.5 all-gather.1

commit v4 on v3

--- a/solution.py
+++ b/solution.py
@@ -70,19 +70,98 @@
     )(x, gain)
 
 
-def project_kernel(h_ref, w_ref, out_ref):
+def rows_of(h, w, wq, b):
+    extra = wq.shape[1] // w.shape[0]
+    main = jnp.dot(h, w[b], preferred_element_type=F32).astype(BF)
+    rest = jnp.dot(h, wq[:, pl.ds(b * extra, extra)], preferred_element_type=F32).astype(BF)
+    return main, rest
+
+
+def project_kernel(h_ref, w_ref, wq_ref, out_ref):
+    cols = w_ref.shape[2]
     for b in range(w_ref.shape[0]):
-        out_ref[b] = jnp.dot(h_ref[...], w_ref[b], preferred_element_type=F32).astype(BF)
-
-
-def project(h, w):
+        main, rest = rows_of(h_ref[...], w_ref, wq_ref, b)
+        out_ref[b, :, :cols] = main
+        out_ref[b, :, cols:] = rest
+
+
+def project(h, w, wq):
     blocks, _, cols = w.shape
     return pl.pallas_call(
         project_kernel,
-        out_shape=pltpu.VMEM((blocks, h.shape[0], cols), BF),
+        out_shape=pltpu.VMEM((blocks, h.shape[0], cols + wq.shape[1] // blocks), BF),
         compiler_params=params(),
         name="project",
-    )(h, in_vmem(w))
+    )(h, in_vmem(w), in_vmem(wq))
+
+
+def opening_kernel(at_ref, h_ref, w_ref, mine_ref, other_ref, wall_ref, wq_ref, out_ref, sem):
+    parts, blocks, zs, rows, cols = w_ref.shape
+    half = mine_ref.shape[1]
+    extra = wq_ref.shape[1] // blocks
+    z, y, core = at_ref[0], at_ref[1], at_ref[2]
+
+    def fetch(block):
+        for part in range(parts):
+            for to in range(zs):
+                pltpu.make_async_copy(
+                    w_ref.at[part, block, lax.rem(z - to + zs, zs)],
+                    wall_ref.at[block, pl.ds((to * parts + part) * rows, rows)],
+                    sem.at[block],
+                ).start()
+
+    def fetch_rest():
+        for source, lane in ((mine_ref, core), (other_ref, 1 - core)):
+            for step in range(parts):
+                for slot in range(half):
+                    to = lax.rem(z - (lane * half + slot) + zs, zs)
+                    part = lax.rem(y + step, parts)
+                    row = pl.multiple_of((to * parts + part) * rows, rows)
+                    pltpu.make_async_copy(
+                        source.at[step, slot], wq_ref.at[pl.ds(row, rows)], sem.at[blocks]
+                    ).start()
+
+    fetch(0)
+    fetch_rest()
+    fetch(1)
+    for b in range(blocks):
+        if b + 2 < blocks:
+            fetch(b + 2)
+        pltpu.make_async_copy(wall_ref.at[b], wall_ref.at[b], sem.at[b]).wait()
+        out_ref[b, :, :cols] = jnp.dot(
+            h_ref[...], wall_ref[b], preferred_element_type=F32
+        ).astype(BF)
+        if b == 0:
+            pltpu.make_async_copy(wq_ref, wq_ref, sem.at[blocks]).wait()
+        out_ref[b, :, cols:] = jnp.dot(
+            h_ref[...], wq_ref[:, pl.ds(b * extra, extra)], preferred_element_type=F32
+        ).astype(BF)
+
+
+def opening(at, h, w, mine, other):
+    parts, blocks, zs, rows, cols = w.shape
+    depth = parts * zs * rows
+    rest = mine.shape[-1]
+    anywhere = pl.BlockSpec(memory_space=pl.ANY)
+    return pl.pallas_call(
+        opening_kernel,
+        out_shape=(
+            pltpu.VMEM((blocks, depth, cols), BF),
+            pltpu.VMEM((depth, rest), BF),
+            pltpu.VMEM((blocks, h.shape[0], cols + rest // blocks), BF),
+        ),
+        in_specs=[
+            pl.BlockSpec(memory_space=pltpu.SMEM),
+            pl.BlockSpec(memory_space=pltpu.VMEM),
+            anywhere,
+            anywhere,
+            anywhere,
+        ],
+        out_specs=(pl.BlockSpec(memory_space=pltpu.VMEM),) * 3,
+        scratch_shapes=[pltpu.SemaphoreType.DMA((blocks + 1,))],
+        compiler_params=params(),
+        name="opening",
+    )(at, h, w, mine, other)
 
 
 def heads(query, keys, values, bias):
@@ -127,80 +206,8 @@
         g_ref[...] = (normed(x1) * gain_ref[...] * valid_ref[...]).astype(BF)
 
 
-def opening_kernel(
-    z_ref, left_ref, h_ref, w_ref, wout_ref, x_ref, bias_ref, gain_ref, valid_ref,
-    x1_ref, g_ref, wall_ref, acc_ref, both_ref, sem,
-):
-    b = pl.program_id(0)
-    last = pl.num_programs(0) - 1
-    span = h_ref.shape[0]
-    group = wout_ref.shape[0]
-    parts, _, zs, rows, _ = w_ref.shape
-
-    def fetch(block):
-        for part in range(parts):
-            for z in range(zs):
-                at = (z * parts + part) * rows
-                pltpu.make_async_copy(
-                    w_ref.at[part, block, lax.rem(z_ref[0] - z + zs, zs)],
-                    wall_ref.at[block, pl.ds(at, rows)],
-                    sem.at[block],
-                ).start()
-
-    @pl.when(b == 0)
-    def _():
-        fetch(0)
-        both_ref[pl.ds(0, span), :] = left_ref[...]
-        both_ref[pl.ds(span, span), :] = h_ref[...]
-
-    @pl.when(b < last)
-    def _():
-        fetch(b + 1)
-
-    pltpu.make_async_copy(wall_ref.at[b], wall_ref.at[b], sem.at[b]).wait()
-    kv = jnp.dot(both_ref[...], wall_ref[b, :, : 2 * group], preferred_element_type=F32).astype(BF)
-    q = jnp.dot(h_ref[...], wall_ref[b, :, 2 * group :], preferred_element_type=F32).astype(BF)
-    ctx = heads(q, kv[:, :group], kv[:, group:], bias_ref[...])
-    settle(ctx, wout_ref, x_ref, gain_ref, valid_ref, x1_ref, g_ref, acc_ref)
-
-
 def whole(*shape):
     return pl.BlockSpec(shape, lambda b: (0,) * len(shape))
-
-
-def opening(z, left, h, w, w_out, x, bias, gain, valid):
-    parts, blocks, zs, rows, cols = w.shape
-    span, width = x.shape
-    group = width // blocks
-    depth = parts * zs * rows
-    return pl.pallas_call(
-        opening_kernel,
-        grid=(blocks,),
-        out_shape=(
-            jax.ShapeDtypeStruct((span, width), F32),
-            jax.ShapeDtypeStruct((span, width), BF),
-            pltpu.VMEM((blocks, depth, cols), BF),
-        ),
-        in_specs=[
-            pl.BlockSpec(memory_space=pltpu.SMEM),
-            whole(span, width),
-            whole(span, width),
-            pl.BlockSpec(memory_space=pl.ANY),
-            pl.BlockSpec((group, width), lambda b: (b, 0)),
-            whole(span, width),
-            whole(2 * span, 128),
-            whole(1, width),
-            whole(span, 1),
-        ],
-        out_specs=(whole(span, width), whole(span, width), pl.BlockSpec(memory_space=pltpu.VMEM)),
-        scratch_shapes=[
-            pltpu.VMEM((span, width), F32),
-            pltpu.VMEM((2 * span, width), BF),
-            pltpu.SemaphoreType.DMA((blocks,)),
-        ],
-        compiler_params=params(),
-        name="opening",
-    )(z, left, h, w, in_hbm(w_out), x, bias, gain, valid)
 
 
 def attend_kernel(
@@ -321,36 +328,91 @@
     return lax.ppermute(value, SEQ, pairs)
 
 
+def carve_kernel(group, at_ref, w_ref, out_ref):
+    width = w_ref.shape[1] // 3
+    start = pl.multiple_of(at_ref[1] * group, 128)
+    out_ref[:, :group] = w_ref[:, pl.ds(width + start, group)]
+    out_ref[:, group : 2 * group] = w_ref[:, pl.ds(2 * width + start, group)]
+    out_ref[:, 2 * group : 2 * group + 128] = w_ref[:, pl.ds(start, 128)]
+    to = 2 * group + 128
+    for x in range(width // group):
+        out_ref[:, to : to + group - 128] = w_ref[:, x * group + 128 : (x + 1) * group]
+        to += group - 128
+
+
+def carve(at, w, deep, group):
+    width = w.shape[1] // 3
+    size = 2 * group + 128 + (width // group) * (group - 128)
+    return pl.pallas_call(
+        functools.partial(carve_kernel, group),
+        grid_spec=pltpu.PrefetchScalarGridSpec(
+            num_scalar_prefetch=1,
+            grid=(1,),
+            in_specs=[pl.BlockSpec((deep, w.shape[1]), lambda i, at: (at[0], 0))],
+            out_specs=pl.BlockSpec((deep, size), lambda i, at: (0, 0)),
+        ),
+        out_shape=jax.ShapeDtypeStruct((deep, size), w.dtype),
+        compiler_params=params(),
+        name="carve",
+    )(at, in_hbm(w))
+
+
+def line_up_kernel(core_ref, *refs):
+    came, (near_ref, far_ref) = refs[:-2], refs[-2:]
+    half = len(came) - 1
+    deep = came[0].shape[0]
+    cut = near_ref.shape[1]
+    for lane in range(2):
+
+        @pl.when(core_ref[0] == lane)
+        def _():
+            for k in range(half):
+                piece = came[half - k] if lane else came[k]
+                near_ref[pl.ds(k * deep, deep), :] = piece[:, :cut]
+                far_ref[pl.ds(k * deep, deep), :] = piece[:, cut:]
+
+
+def line_up(core, came, cut):
+    deep, size = came[0].shape
+    rows = deep * (len(came) - 1)
+    space = pl.BlockSpec(memory_space=pltpu.VMEM)
+    return pl.pallas_call(
+        line_up_kernel,
+        out_shape=(
+            jax.ShapeDtypeStruct((rows, cut), BF),
+            jax.ShapeDtypeStruct((rows, size - cut), BF),
+        ),
+        in_specs=[pl.BlockSpec(memory_space=pltpu.SMEM)] + [space] * len(came),
+        out_specs=(space, space),
+        compiler_params=params(),
+        name="line_up",
+    )(core, *came)
+
+
 def weight_blocks(w, frames):
     rows, cols = w.shape
-    zs, xs, yls, cores = (lax.axis_size(a) for a in ("z", "x", "yl", "core"))
+    zs, xs, yhs, yls, cores = (lax.axis_size(a) for a in ("z", "x", "yh", "yl", "core"))
     deep = rows // yls
-    width = cols // 3
-    group = width // xs
-    at = lax.axis_index("yl") * deep
-    col = lax.axis_index("x") * group
-    own = jnp.concatenate(
-        [lax.dynamic_slice(w, (at, part * width + col), (deep, group)) for part in (1, 2, 0)],
-        axis=1,
-    )
+    group = cols // 3 // xs
+    cut = 2 * group + 128
+    at = jnp.stack([lax.axis_index("yl"), lax.axis_index("x")]).astype(jnp.int32)
+    own = carve(at, w, deep, group)
     half = zs // cores
-    came = {}
+    came = []
     for k in range(1, half + 1):
         pairs = [(cores * z, cores * ((z + k) % zs)) for z in range(zs) if k < half]
         pairs += [(cores * z + 1, cores * ((z - k) % zs) + 1) for z in range(zs)]
-        came[k] = lax.ppermute(own, ("z", "core"), pairs)
-    first = lax.axis_index("core") == 0
-    stack = jnp.concatenate(
-        [
-            jnp.where(first, came[k] if k else own, came[half - k])
-            for k in range(half)
-        ],
-        axis=0,
-    )
-    stack, frames = lax.optimization_barrier((stack, frames))
-    full = lax.all_gather(stack, ("yh",) + SEQ, axis=0, tiled=True)
-    parts = lax.axis_size("yh") * yls
-    return full.reshape(parts, xs, zs, deep, 3 * group), frames
+        came.append(lax.ppermute(own, ("z", "core"), pairs))
+    near, far = line_up(lax.axis_index("core").astype(jnp.int32)[None], [own] + came, cut)
+    near, far, frames = lax.optimization_barrier((near, far, frames))
+    parts = yhs * yls
+    turned = [far] + [
+        lax.ppermute(far, ("yh", "yl"), [(i, (i - k) % parts) for i in range(parts)])
+        for k in range(1, parts)
+    ]
+    full = lax.all_gather(near, ("yh",) + SEQ, axis=0, tiled=True)
+    turned = jnp.stack(turned).reshape(parts, half, deep, -1)
+    return full.reshape(parts, xs, zs, deep, cut), turned, frames
 
 
 def on_device(frames, arrival, lengths, attn_gain, w_qkv, w_out, conv_gain, conv_kernel):
@@ -359,11 +421,13 @@
     group = lax.axis_index(DP)
     place = lax.axis_index(SEQ)
     groups = lax.axis_size(DP)
-    w, frames = weight_blocks(w_qkv, frames)
+    w, mine, frames = weight_blocks(w_qkv, frames)
     row_here = lax.dynamic_index_in_dim(arrival, place, 0, keepdims=False)
     chunks = frames.reshape(groups, span // groups, width)
     chunks = lax.all_to_all(chunks, DP, split_axis=0, concat_axis=0, tiled=True)
     chunks = pick(chunks, row_here)
+    chunks, mine = lax.optimization_barrier((chunks, mine))
+    other = lax.ppermute(mine, "core", [(0, 1), (1, 0)])
     chunks = lax.all_to_all(chunks, DP, split_axis=0, concat_axis=0, tiled=True)
     x = chunks.reshape(span, width)
 
@@ -384,10 +448,11 @@
         last = step == ITERS - 1
         left = along(h, 1)
         if step == 0:
-            z = lax.axis_index("z").astype(jnp.int32)[None]
-            x1, g, w = opening(z, left, h, w, w_out, x, bias, gain_c, valid)
+            at = [lax.axis_index("z"), lax.axis_index(("yh", "yl")), lax.axis_index("core")]
+            w, wq, own = opening(jnp.stack(at).astype(jnp.int32), h, w, mine, other)
         else:
-            x1, g = attend(left, project(h, w), w, w_out, x, bias, gain_c, valid)
+            own = project(h, w, wq)
+        x1, g = attend(left, own, w, w_out, x, bias, gain_c, valid)
         low = along(g[span - HALO :], 1)
         high = along(g[:HALO], -1)
         inners = inner(g, x1, taps, valid, gain_a, last)

time: 198 us -> 208 us (1.051)
  Pallas kernels: 47.8 us -> 53.5 us
  starting transfers between devices: 43.5 us -> 48.6 us
    ppermute x4 -> x8, waiting for transfers between devices: 9.34 us -> 44.2 us  [the longest x3 29.6 us: weight_blocks(): lax.ppermute(far, ('yh', 'yl'), [(i, (i - k) % parts) for i in range(part...]
    ppermute x6, waiting for transfers between devices: 32.4 us -> 7.49 us  [along(): return lax.ppermute(value, SEQ, pairs)]
    all_to_all x2, waiting for transfers between devices: 42.4 us -> 19.1 us  [on_device(): chunks = lax.all_to_all(chunks, DP, split_axis=0, concat_axis=0, tiled=True)]
    pallas_call x1 -> x2, Pallas kernels: 12.4 us -> 25.1 us  [attend(): pl.pallas_call(attend_kernel, grid=(blocks,), out_shape=(jax.ShapeDtypeSt...]
    all_gather x1, waiting for transfers between devices: 4.52 us -> 16.6 us  [weight_blocks(): full = lax.all_gather(near, ('yh',) + SEQ, axis=0, tiled=True)]
    pallas_call x1 -> x3, Pallas kernels: 18.1 us -> 11 us  [the longest x1 8.62 us: opening(): pl.pallas_call(opening_kernel, out_shape=(pltpu.VMEM((blocks, depth, cols...]
    ppermute x4 -> x8, starting transfers between devices: 10 us -> 13.5 us  [the longest x4 9.96 us: weight_blocks(): came.append(lax.ppermute(own, ('z', 'core'), pairs))]
    all_to_all x2, starting transfers between devices: 13.8 us -> 17.1 us  [on_device(): chunks = lax.all_to_all(chunks, DP, split_axis=0, concat_axis=0, tiled=True)]
  transfers between devices with their start and end apart: 13 -> 17, of which waited for: 7 -> 8; matrix products, arithmetic and copies ran while one was open for 1% -> 2% of each run, Pallas kernels for 8% -> 11%
where the time goes in v4:
time: 208 us
  waiting for transfers between devices  87.5 us (42%)
  Pallas kernels  53.5 us (26%)
  starting transfers between devices  48.6 us (23%)
  between operations  13.7 us (7%)
  other arithmetic  2.9 us (1%)
    ppermute x3, waiting for transfers between devices, weight_blocks(): lax.ppermute(far, ('yh', 'yl'), [(i, (i - k) % parts) for i in range(part...  29.6 us
    pallas_call x2, Pallas kernels, attend(): pl.pallas_call(attend_kernel, grid=(blocks,), out_shape=(jax.ShapeDtypeSt...  25.1 us
    all_to_all x2, waiting for transfers between devices, on_device(): chunks = lax.all_to_all(chunks, DP, split_axis=0, concat_axis=0, tiled=True)  19.1 us
    ppermute x6, starting transfers between devices, along(): return lax.ppermute(value, SEQ, pairs)  18 us
    all_to_all x2, starting transfers between devices, on_device(): chunks = lax.all_to_all(chunks, DP, split_axis=0, concat_axis=0, tiled=True)  17.1 us
    all_gather x1, waiting for transfers between devices, weight_blocks(): full = lax.all_gather(near, ('yh',) + SEQ, axis=0, tiled=True)  16.6 us
    ppermute x4, waiting for transfers between devices, weight_blocks(): came.append(lax.ppermute(own, ('z', 'core'), pairs))  14.7 us
    ppermute x4, starting transfers between devices, weight_blocks(): came.append(lax.ppermute(own, ('z', 'core'), pairs))  9.96 us
  transfers between devices with their start and end apart: 17, of which 8 were waited for; matrix products, arithmetic and copies ran while one was open for 2% of the time, Pallas kernels for 11%

profile of v4, /device:TPU:24, one launch (start us, length us, event | category | flops | bytes accessed | tf_op | source)
XLA Modules:
  0.0 207.7 jit_solution(3980087249801778747)
XLA Ops:
  8.2 2.0 collective-permute-start
  10.2 3.3 %collective-permute-start.1 = (bf16[48,1920]{1,0:T(8,128)(2,1)S(1)}, bf16[48,1920]{1,0:T(8,128)(2,1)S(1)}, u32[]{:S(2)}, u32[]{:S(2)}) collective-permute-start(bf16[48,1920]{1,0:T(8,128)(2,1)S(1)} %carve.1.refs_0_), channel_id=1, source_target_pairs={{0,64},{32,96},{64,128},{96,160},{128,192},{160,224},{192,0},{224,... | collective-permute-start | bytes 552968 | tf_op jit(solution)/shard_map/ppermute | solution.py:405
  13.5 4.0 %collective-permute-start.2 = (bf16[48,1920]{1,0:T(8,128)(2,1)S(1)}, bf16[48,1920]{1,0:T(8,128)(2,1)S(1)}, u32[]{:S(2)}, u32[]{:S(2)}) collective-permute-start(bf16[48,1920]{1,0:T(8,128)(2,1)S(1)} %carve.1.refs_0_), channel_id=1, source_target_pairs={{0,96},{32,128},{64,160},{96,192},{128,224},{160,0},{192,32},{224,... | collective-permute-start | bytes 552968 | tf_op jit(solution)/shard_map/ppermute | solution.py:405
  18.2 3.4 %collective-permute-done.1.refs_2_ = bf16[48,1920]{1,0:T(8,128)(2,1)S(1)} collective-permute-done((bf16[48,1920]{1,0:T(8,128)(2,1)S(1)}, bf16[48,1920]{1,0:T(8,128)(2,1)S(1)}, u32[]{:S(2)}, u32[]{:S(2)}) %collective-permute-start.1) | collective-permute-done | bytes 184352 | tf_op jit(solution)/shard_map/ppermute | solution.py:405
  21.6 11.2 %collective-permute-done.2.refs_3_ = bf16[48,1920]{1,0:T(8,128)(2,1)S(1)} collective-permute-done((bf16[48,1920]{1,0:T(8,128)(2,1)S(1)}, bf16[48,1920]{1,0:T(8,128)(2,1)S(1)}, u32[]{:S(2)}, u32[]{:S(2)}) %collective-permute-start.2) | collective-permute-done | bytes 184352 | tf_op jit(solution)/shard_map/ppermute | solution.py:405
  33.7 7.5 %all-to-all-start = ((bf16[16,16,1536]{2,1,0:T(8,128)(2,1)}), bf16[16,16,1536]{2,1,0:T(8,128)(2,1)S(1)}, u32[]{:S(2)}, u32[]{:S(2)}) async-start(bf16[16,16,1536]{2,1,0:T(8,128)(2,1)} %bitcast.4), calls=%async_computation | async-start | bytes 1572864 | tf_op jit(solution)/shard_map/all_to_all | solution.py:427
  42.7 2.0 collective-permute-start.6
  44.7 19.3 %collective-permute-done.4 = bf16[192,1024]{1,0:T(8,128)(2,1)S(1)} collective-permute-done((bf16[192,1024]{1,0:T(8,128)(2,1)S(1)}, bf16[192,1024]{1,0:T(8,128)(2,1)S(1)}, u32[]{:S(2)}, u32[]{:S(2)}) %collective-permute-start.4) | collective-permute-done | bytes 393248 | tf_op jit(solution)/shard_map/ppermute | solution.py:410
  63.9 8.7 %collective-permute-done.5 = bf16[192,1024]{1,0:T(8,128)(2,1)S(1)} collective-permute-done((bf16[192,1024]{1,0:T(8,128)(2,1)S(1)}, bf16[192,1024]{1,0:T(8,128)(2,1)S(1)}, u32[]{:S(2)}, u32[]{:S(2)}) %collective-permute-start.5) | collective-permute-done | bytes 393248 | tf_op jit(solution)/shard_map/ppermute | solution.py:410
  77.8 9.6 %all-to-all-start.1 = ((bf16[16,16,1536]{2,1,0:T(8,128)(2,1)}), bf16[16,16,1536]{2,1,0:T(8,128)(2,1)S(1)}, u32[]{:S(2)}, u32[]{:S(2)}) async-start(bf16[16,16,1536]{2,1,0:T(8,128)(2,1)} %pick.1), calls=%async_computation.1 | async-start | bytes 1572864 | tf_op jit(solution)/shard_map/all_to_all | solution.py:431
  88.1 19.1 %all-to-all-done.1 = bf16[16,16,1536]{2,1,0:T(8,128)(2,1)S(1)} async-done(((bf16[16,16,1536]{2,1,0:T(8,128)(2,1)}), bf16[16,16,1536]{2,1,0:T(8,128)(2,1)S(1)}, u32[]{:S(2)}, u32[]{:S(2)}) %all-to-all-start.1) | async-done | bytes 786464 | tf_op jit(solution)/shard_map/all_to_all | solution.py:431
  107.8 2.1 %collective-permute-start.7 = (bf16[256,1536]{1,0:T(8,128)(2,1)S(1)}, bf16[256,1536]{1,0:T(8,128)(2,1)}, u32[]{:S(2)}, u32[]{:S(2)}) collective-permute-start(bf16[256,1536]{1,0:T(8,128)(2,1)S(1)} %head.1.h_ref), channel_id=1, source_target_pairs={{0,1},{1,2},{2,3},{3,4},{4,5},{5,6},{6,7},{7,8},{8,9},{9,10},{10,1... | collective-permute-start | bytes 2359304 | tf_op jit(solution)/shard_map/ppermute | solution.py:328
  111.5 16.6 %all-gather.2.cloned.1.call-done = bf16[6144,896]{1,0:T(8,128)(2,1)} async-done(((bf16[192,896]{1,0:T(8,128)(2,1)}), bf16[6144,896]{1,0:T(8,128)(2,1)}) %all-gather.2.cloned.1.call-update) | async-done | bytes 11010064 | tf_op jit(solution)/shard_map/all_gather | solution.py:413
  128.1 8.6 %opening.1 = (bf16[4,1536,896]{2,1,0:T(8,128)(2,1)S(1)}, bf16[1536,1024]{1,0:T(8,128)(2,1)S(1)}, bf16[4,256,1152]{2,1,0:T(8,128)(2,1)S(1)}) custom-call(s32[3]{0:T(128)S(1)} %pad_add_fusion.1.at_ref, bf16[256,1536]{1,0:T(8,128)(2,1)S(1)} %head.1.h_ref, bf16[4,4,8,48,896]{4,3,2,1,0:T(8,128)(2,1)} %bitcast.19, ...), custom_call_target="tpu_custom_call" | custom-call | tf_op jit(solution)/shard_map/opening/pallas_call | solution.py:146
  136.7 12.7 %attend.2 = (f32[256,1536]{1,0:T(8,128)S(1)}, bf16[256,1536]{1,0:T(8,128)(2,1)S(1)}) custom-call(bf16[256,1536]{1,0:T(8,128)(2,1)} %collective-permute-done.7.left_ref, bf16[4,256,1152]{2,1,0:T(8,128)(2,1)S(1)} %get-tuple-element.30.own_ref, bf16[4,1536,896]{2,1,0:T(8,128)(2,1)S(1)} %get-tuple-element.31.w_ref, bf16[1536,1536]{1,0:T(8,128)(2,1)} %wout_ref.3, ...), custom_call_target="tpu_custom_call" | custom-call | tf_op jit(solution)/shard_map/attend/pallas_call | solution.py:231
  151.4 2.6 %collective-permute-start.9 = (bf16[16,1536]{1,0:T(8,128)(2,1)S(1)}, bf16[16,1536]{1,0:T(8,128)(2,1)S(1)}, u32[]{:S(2)}, u32[]{:S(2)}) collective-permute-start(bf16[16,1536]{1,0:T(8,128)(2,1)S(1)} %get-tuple-element.44), channel_id=1, source_target_pairs={{0,1},{1,2},{2,3},{3,4},{4,5},{5,6},{6,7},{7,8},{8,9},{9,10},{10,1... | collective-permute-start | bytes 147464 | tf_op jit(solution)/shard_map/ppermute | solution.py:328
  154.1 4.8 %inner.2 = (bf16[256,1536]{1,0:T(8,128)(2,1)S(1)}, bf16[256,1536]{1,0:T(8,128)(2,1)S(1)}) custom-call(bf16[256,1536]{1,0:T(8,128)(2,1)S(1)} %get-tuple-element.32.g_ref, f32[256,1536]{1,0:T(8,128)S(1)} %get-tuple-element.33.x1_ref, f32[32,1536]{1,0:T(8,128)S(1)} %pad.4.taps_ref, f32[256,1]{1,0:T(8,128)S(1)} %fusion.valid_ref, ...), custom_call_target="tpu_custom_call" | custom-call | tf_op jit(solution)/shard_map/inner/pallas_call | solution.py:281
  159.9 3.7 %collective-permute-start.11 = (bf16[256,1536]{1,0:T(8,128)(2,1)S(1)}, bf16[256,1536]{1,0:T(8,128)(2,1)S(1)}, u32[]{:S(2)}, u32[]{:S(2)}) collective-permute-start(bf16[256,1536]{1,0:T(8,128)(2,1)S(1)} %get-tuple-element.36.h_ref), channel_id=1, source_target_pairs={{0,1},{1,2},{2,3},{3,4},{4,5},{5,6},{6,7},{7,8},{8,9},{9,10},{10,1... | collective-permute-start | bytes 2359304 | tf_op jit(solution)/shard_map/ppermute | solution.py:328
  163.5 4.3 %project.1.own_ref = bf16[4,256,1152]{2,1,0:T(8,128)(2,1)S(1)} custom-call(bf16[256,1536]{1,0:T(8,128)(2,1)S(1)} %get-tuple-element.36.h_ref, bf16[4,1536,896]{2,1,0:T(8,128)(2,1)S(1)} %get-tuple-element.31.w_ref, bf16[1536,1024]{1,0:T(8,128)(2,1)S(1)} %get-tuple-element.37.wq_ref), custom_call_target="tpu_custom_call" | custom-call | tf_op jit(solution)/shard_map/project/pallas_call | solution.py:90
  167.8 7.5 %collective-permute-done.11.left_ref = bf16[256,1536]{1,0:T(8,128)(2,1)S(1)} collective-permute-done((bf16[256,1536]{1,0:T(8,128)(2,1)S(1)}, bf16[256,1536]{1,0:T(8,128)(2,1)S(1)}, u32[]{:S(2)}, u32[]{:S(2)}) %collective-permute-start.11) | collective-permute-done | bytes 786464 | tf_op jit(solution)/shard_map/ppermute | solution.py:328
  175.3 12.4 %attend.3 = (f32[256,1536]{1,0:T(8,128)S(1)}, bf16[256,1536]{1,0:T(8,128)(2,1)S(1)}) custom-call(bf16[256,1536]{1,0:T(8,128)(2,1)S(1)} %collective-permute-done.11.left_ref, bf16[4,256,1152]{2,1,0:T(8,128)(2,1)S(1)} %project.1.own_ref, bf16[4,1536,896]{2,1,0:T(8,128)(2,1)S(1)} %get-tuple-element.31.w_ref, bf16[1536,1536]{1,0:T(8,128)(2,1)} %wout_ref.3, ...), custom_call_target="tpu_custom_call" | custom-call | tf_op jit(solution)/shard_map/attend/pallas_call | solution.py:231
  187.7 1.9 collective-permute-start.12
  189.6 5.8 %collective-permute-start.13 = (bf16[16,1536]{1,0:T(8,128)(2,1)S(1)}, bf16[16,1536]{1,0:T(8,128)(2,1)S(1)}, u32[]{:S(2)}, u32[]{:S(2)}) collective-permute-start(bf16[16,1536]{1,0:T(8,128)(2,1)S(1)} %get-tuple-element.41), channel_id=1, source_target_pairs={{1,0},{2,1},{3,2},{4,3},{5,4},{6,5},{7,6},{8,7},{9,8},{10,9},{11,1... | collective-permute-start | bytes 147464 | tf_op jit(solution)/shard_map/ppermute | solution.py:328
  195.4 3.9 %inner.3.rest_0_ = bf16[256,1536]{1,0:T(8,128)(2,1)S(1)} custom-call(bf16[256,1536]{1,0:T(8,128)(2,1)S(1)} %get-tuple-element.39.g_ref, f32[256,1536]{1,0:T(8,128)S(1)} %get-tuple-element.40.x1_ref, f32[32,1536]{1,0:T(8,128)S(1)} %pad.4.taps_ref, f32[256,1]{1,0:T(8,128)S(1)} %fusion.valid_ref, f32[1,1536]{1,0:T(1,128)S(1)} %broadcast_in_dim.44.gain_ref), custom_call_target="tpu_custom_call" | custom-call | tf_op jit(solution)/shard_map/inner/pallas_call | solution.py:281
  (52 shorter events, 16.9 us)
Async XLA Ops:
  6.5 38.1 %copy-start = (s32[16,16]{1,0:T(8,128)S(1)}, s32[16,16]{1,0:T(8,128)}, u32[]{:S(2)}) copy-start(s32[16,16]{1,0:T(8,128)} %param.9) | copy-start | bytes 3076
  6.5 121.6 %all-gather.2.cloned.1.call-start = ((), (), s32[]{:S(2)}) async-start(), calls=%async_computation.2 | async-start | bytes 11354112 | tf_op jit(solution)/shard_map/all_gather | solution.py:413
  8.2 10.0 %collective-permute-start = (bf16[48,1920]{1,0:T(8,128)(2,1)S(1)}, bf16[48,1920]{1,0:T(8,128)(2,1)S(1)}, u32[]{:S(2)}, u32[]{:S(2)}) collective-permute-start(bf16[48,1920]{1,0:T(8,128)(2,1)S(1)} %carve.1.refs_0_), channel_id=1, source_target_pairs={{0,32},{32,64},{64,96},{96,128},{128,160},{160,192},{192,224},{224... | collective-permute-start | bytes 552968 | tf_op jit(solution)/shard_map/ppermute | solution.py:405
  10.2 11.4 %collective-permute-start.1 = (bf16[48,1920]{1,0:T(8,128)(2,1)S(1)}, bf16[48,1920]{1,0:T(8,128)(2,1)S(1)}, u32[]{:S(2)}, u32[]{:S(2)}) collective-permute-start(bf16[48,1920]{1,0:T(8,128)(2,1)S(1)} %carve.1.refs_0_), channel_id=1, source_target_pairs={{0,64},{32,96},{64,128},{96,160},{128,192},{160,224},{192,0},{224,... | collective-permute-start | bytes 552968 | tf_op jit(solution)/shard_map/ppermute | solution.py:405
  13.5 19.4 %collective-permute-start.2 = (bf16[48,1920]{1,0:T(8,128)(2,1)S(1)}, bf16[48,1920]{1,0:T(8,128)(2,1)S(1)}, u32[]{:S(2)}, u32[]{:S(2)}) collective-permute-start(bf16[48,1920]{1,0:T(8,128)(2,1)S(1)} %carve.1.refs_0_), channel_id=1, source_target_pairs={{0,96},{32,128},{64,160},{96,192},{128,224},{160,0},{192,32},{224,... | collective-permute-start | bytes 552968 | tf_op jit(solution)/shard_map/ppermute | solution.py:405
  17.5 15.3 %collective-permute-start.3 = (bf16[48,1920]{1,0:T(8,128)(2,1)S(1)}, bf16[48,1920]{1,0:T(8,128)(2,1)S(1)}, u32[]{:S(2)}, u32[]{:S(2)}) collective-permute-start(bf16[48,1920]{1,0:T(8,128)(2,1)S(1)} %carve.1.refs_0_), channel_id=1, source_target_pairs={{1,129},{33,161},{65,193},{97,225},{129,1},{161,33},{193,65},{225,... | collective-permute-start | bytes 552968 | tf_op jit(solution)/shard_map/ppermute | solution.py:405
  33.7 42.7 %all-to-all-start = ((bf16[16,16,1536]{2,1,0:T(8,128)(2,1)}), bf16[16,16,1536]{2,1,0:T(8,128)(2,1)S(1)}, u32[]{:S(2)}, u32[]{:S(2)}) async-start(bf16[16,16,1536]{2,1,0:T(8,128)(2,1)} %bitcast.4), calls=%async_computation | async-start | bytes 1572864 | tf_op jit(solution)/shard_map/all_to_all | solution.py:427
  41.1 22.8 %collective-permute-start.4 = (bf16[192,1024]{1,0:T(8,128)(2,1)S(1)}, bf16[192,1024]{1,0:T(8,128)(2,1)S(1)}, u32[]{:S(2)}, u32[]{:S(2)}) collective-permute-start(bf16[192,1024]{1,0:T(8,128)(2,1)S(1)} %get-tuple-element.26), channel_id=1, source_target_pairs={{0,24},{8,0},{16,8},{24,16},{1,25},{9,1},{17,9},{25,17},{2,26},{10... | collective-permute-start | bytes 1179656 | tf_op jit(solution)/shard_map/ppermute | solution.py:410
  41.9 30.8 %collective-permute-start.5 = (bf16[192,1024]{1,0:T(8,128)(2,1)S(1)}, bf16[192,1024]{1,0:T(8,128)(2,1)S(1)}, u32[]{:S(2)}, u32[]{:S(2)}) collective-permute-start(bf16[192,1024]{1,0:T(8,128)(2,1)S(1)} %get-tuple-element.26), channel_id=1, source_target_pairs={{0,16},{8,24},{16,0},{24,8},{1,17},{9,25},{17,1},{25,9},{2,18},{10... | collective-permute-start | bytes 1179656 | tf_op jit(solution)/shard_map/ppermute | solution.py:410
  42.7 31.6 %collective-permute-start.6 = (bf16[192,1024]{1,0:T(8,128)(2,1)S(1)}, bf16[192,1024]{1,0:T(8,128)(2,1)S(1)}, u32[]{:S(2)}, u32[]{:S(2)}) collective-permute-start(bf16[192,1024]{1,0:T(8,128)(2,1)S(1)} %get-tuple-element.26), channel_id=1, source_target_pairs={{0,8},{8,16},{16,24},{24,0},{1,9},{9,17},{17,25},{25,1},{2,10},{10... | collective-permute-start | bytes 1179656 | tf_op jit(solution)/shard_map/ppermute | solution.py:410
  72.6 1.6 copy-start.1
  74.2 0.7 copy-start.2
  76.3 11.2 %copy-start.4 = (f32[1536]{0:T(1024)S(1)}, f32[1536]{0:T(1024)}, u32[]{:S(2)}) copy-start(f32[1536]{0:T(1024)} %param.11) | copy-start | bytes 18436
  76.3 11.2 %copy-start.5 = (f32[1536]{0:T(1024)S(1)}, f32[1536]{0:T(1024)}, u32[]{:S(2)}) copy-start(f32[1536]{0:T(1024)} %param.14) | copy-start | bytes 18436
  76.3 11.2 %copy-start.6 = (s32[16]{0:T(128)S(1)}, s32[16]{0:T(128)}, u32[]{:S(2)}) copy-start(s32[16]{0:T(128)} %param.10) | copy-start | bytes 196
  77.8 29.5 %all-to-all-start.1 = ((bf16[16,16,1536]{2,1,0:T(8,128)(2,1)}), bf16[16,16,1536]{2,1,0:T(8,128)(2,1)S(1)}, u32[]{:S(2)}, u32[]{:S(2)}) async-start(bf16[16,16,1536]{2,1,0:T(8,128)(2,1)} %pick.1), calls=%async_computation.1 | async-start | bytes 1572864 | tf_op jit(solution)/shard_map/all_to_all | solution.py:431
  87.4 24.0 %collective-permute-start.8 = (bf16[4,4,48,1024]{3,2,1,0:T(8,128)(2,1)S(1)}, bf16[4,4,48,1024]{3,2,1,0:T(8,128)(2,1)}, u32[]{:S(2)}, u32[]{:S(2)}) collective-permute-start(bf16[4,4,48,1024]{3,2,1,0:T(8,128)(2,1)S(1)} %pad_maximum_fusion.mine_ref), channel_id=1, source_target_pairs={{0,1},{1,0},{2,3},{3,2},{4,5},{5,4},{6,7},{7,6},{8,9},{9,8},{10,11... | collective-permute-start | bytes 4718600 | tf_op jit(solution)/shard_map/ppermute | solution.py:430
  107.8 28.9 %collective-permute-start.7 = (bf16[256,1536]{1,0:T(8,128)(2,1)S(1)}, bf16[256,1536]{1,0:T(8,128)(2,1)}, u32[]{:S(2)}, u32[]{:S(2)}) collective-permute-start(bf16[256,1536]{1,0:T(8,128)(2,1)S(1)} %head.1.h_ref), channel_id=1, source_target_pairs={{0,1},{1,2},{2,3},{3,4},{4,5},{5,6},{6,7},{7,8},{8,9},{9,10},{10,1... | collective-permute-start | bytes 2359304 | tf_op jit(solution)/shard_map/ppermute | solution.py:328
  136.7 17.3 %copy-start.3 = (f32[31,1536]{1,0:T(8,128)S(1)}, f32[31,1536]{1,0:T(8,128)}, u32[]{:S(2)}) copy-start(f32[31,1536]{1,0:T(8,128)} %param.15) | copy-start | bytes 571396
  149.5 9.5 %collective-permute-start.10 = (bf16[16,1536]{1,0:T(8,128)(2,1)S(1)}, bf16[16,1536]{1,0:T(8,128)(2,1)S(1)}, u32[]{:S(2)}, u32[]{:S(2)}) collective-permute-start(bf16[16,1536]{1,0:T(8,128)(2,1)S(1)} %get-tuple-element.43), channel_id=1, source_target_pairs={{1,0},{2,1},{3,2},{4,3},{5,4},{6,5},{7,6},{8,7},{9,8},{10,9},{11,1... | collective-permute-start | bytes 147464 | tf_op jit(solution)/shard_map/ppermute | solution.py:328
  151.4 7.5 %collective-permute-start.9 = (bf16[16,1536]{1,0:T(8,128)(2,1)S(1)}, bf16[16,1536]{1,0:T(8,128)(2,1)S(1)}, u32[]{:S(2)}, u32[]{:S(2)}) collective-permute-start(bf16[16,1536]{1,0:T(8,128)(2,1)S(1)} %get-tuple-element.44), channel_id=1, source_target_pairs={{0,1},{1,2},{2,3},{3,4},{4,5},{5,6},{6,7},{7,8},{8,9},{9,10},{10,1... | collective-permute-start | bytes 147464 | tf_op jit(solution)/shard_map/ppermute | solution.py:328
  159.9 15.4 %collective-permute-start.11 = (bf16[256,1536]{1,0:T(8,128)(2,1)S(1)}, bf16[256,1536]{1,0:T(8,128)(2,1)S(1)}, u32[]{:S(2)}, u32[]{:S(2)}) collective-permute-start(bf16[256,1536]{1,0:T(8,128)(2,1)S(1)} %get-tuple-element.36.h_ref), channel_id=1, source_target_pairs={{0,1},{1,2},{2,3},{3,4},{4,5},{5,6},{6,7},{7,8},{8,9},{9,10},{10,1... | collective-permute-start | bytes 2359304 | tf_op jit(solution)/shard_map/ppermute | solution.py:328
  187.7 11.6 %collective-permute-start.12 = (bf16[16,1536]{1,0:T(8,128)(2,1)S(1)}, bf16[16,1536]{1,0:T(8,128)(2,1)S(1)}, u32[]{:S(2)}, u32[]{:S(2)}) collective-permute-start(bf16[16,1536]{1,0:T(8,128)(2,1)S(1)} %get-tuple-element.42), channel_id=1, source_target_pairs={{0,1},{1,2},{2,3},{3,4},{4,5},{5,6},{6,7},{7,8},{8,9},{9,10},{10,1... | collective-permute-start | bytes 147464 | tf_op jit(solution)/shard_map/ppermute | solution.py:328
  189.6 9.7 %collective-permute-start.13 = (bf16[16,1536]{1,0:T(8,128)(2,1)S(1)}, bf16[16,1536]{1,0:T(8,128)(2,1)S(1)}, u32[]{:S(2)}, u32[]{:S(2)}) collective-permute-start(bf16[16,1536]{1,0:T(8,128)(2,1)S(1)} %get-tuple-element.41), channel_id=1, source_target_pairs={{1,0},{2,1},{3,2},{4,3},{5,4},{6,5},{7,6},{8,7},{9,8},{10,9},{11,1... | collective-permute-start | bytes 147464 | tf_op jit(solution)/shard_map/ppermute | solution.py:328
Sparse Core Ops, SparseCore 0:
  33.8 94.2 all-gather.1

commit v5 on v3

--- a/solution.py
+++ b/solution.py
@@ -108,41 +108,36 @@
     return jnp.concatenate(outs, axis=1)
 
 
-def settle(ctx, wout_ref, x_ref, gain_ref, valid_ref, x1_ref, g_ref, acc_ref):
+def settle(ctx, wout_ref, x_ref, gain_ref, valid_ref, x1_ref, g_ref, ctx_ref):
     b = pl.program_id(0)
-    part = jnp.dot(ctx, wout_ref[...], preferred_element_type=F32)
-
-    @pl.when(b == 0)
-    def _():
-        acc_ref[...] = x_ref[...].astype(F32) + part
-
-    @pl.when(b > 0)
-    def _():
-        acc_ref[...] += part
+    group = ctx.shape[1]
+    ctx_ref[:, pl.ds(pl.multiple_of(b * group, group), group)] = ctx
 
     @pl.when(b == pl.num_programs(0) - 1)
     def _():
-        x1 = acc_ref[...]
+        x1 = x_ref[...].astype(F32) + jnp.dot(
+            ctx_ref[...], wout_ref[...], preferred_element_type=F32
+        )
         x1_ref[...] = x1
         g_ref[...] = (normed(x1) * gain_ref[...] * valid_ref[...]).astype(BF)
 
 
 def opening_kernel(
     z_ref, left_ref, h_ref, w_ref, wout_ref, x_ref, bias_ref, gain_ref, valid_ref,
-    x1_ref, g_ref, wall_ref, acc_ref, both_ref, sem,
+    x1_ref, g_ref, wall_ref, ctx_ref, both_ref, sem,
 ):
     b = pl.program_id(0)
     last = pl.num_programs(0) - 1
     span = h_ref.shape[0]
-    group = wout_ref.shape[0]
-    parts, _, zs, rows, _ = w_ref.shape
+    group = wout_ref.shape[0] // w_ref.shape[0]
+    _, parts, zs, rows, _ = w_ref.shape
 
     def fetch(block):
         for part in range(parts):
             for z in range(zs):
                 at = (z * parts + part) * rows
                 pltpu.make_async_copy(
-                    w_ref.at[part, block, lax.rem(z_ref[0] - z + zs, zs)],
+                    w_ref.at[block, part, lax.rem(z_ref[0] - z + zs, zs)],
                     wall_ref.at[block, pl.ds(at, rows)],
                     sem.at[block],
                 ).start()
@@ -161,7 +156,7 @@
     kv = jnp.dot(both_ref[...], wall_ref[b, :, : 2 * group], preferred_element_type=F32).astype(BF)
     q = jnp.dot(h_ref[...], wall_ref[b, :, 2 * group :], preferred_element_type=F32).astype(BF)
     ctx = heads(q, kv[:, :group], kv[:, group:], bias_ref[...])
-    settle(ctx, wout_ref, x_ref, gain_ref, valid_ref, x1_ref, g_ref, acc_ref)
+    settle(ctx, wout_ref, x_ref, gain_ref, valid_ref, x1_ref, g_ref, ctx_ref)
 
 
 def whole(*shape):
@@ -169,7 +164,7 @@
 
 
 def opening(z, left, h, w, w_out, x, bias, gain, valid):
-    parts, blocks, zs, rows, cols = w.shape
+    blocks, parts, zs, rows, cols = w.shape
     span, width = x.shape
     group = width // blocks
     depth = parts * zs * rows
@@ -186,7 +181,7 @@
             whole(span, width),
             whole(span, width),
             pl.BlockSpec(memory_space=pl.ANY),
-            pl.BlockSpec((group, width), lambda b: (b, 0)),
+            whole(width, width),
             whole(span, width),
             whole(2 * span, 128),
             whole(1, width),
@@ -194,7 +189,7 @@
         ],
         out_specs=(whole(span, width), whole(span, width), pl.BlockSpec(memory_space=pltpu.VMEM)),
         scratch_shapes=[
-            pltpu.VMEM((span, width), F32),
+            pltpu.VMEM((span, width), BF),
             pltpu.VMEM((2 * span, width), BF),
             pltpu.SemaphoreType.DMA((blocks,)),
         ],
@@ -204,20 +199,28 @@
 
 
 def attend_kernel(
-    left_ref, own_ref, w_ref, wout_ref, x_ref, bias_ref, gain_ref, valid_ref,
-    x1_ref, g_ref, acc_ref,
+    inner_ref, edge_ref, own_ref, w_ref, wout_ref, x_ref, bias_ref, gain_ref, valid_ref,
+    x1_ref, g_ref, ctx_ref, left_ref,
 ):
     b = pl.program_id(0)
-    group = wout_ref.shape[0]
+    group = wout_ref.shape[0] // w_ref.shape[0]
+    span = left_ref.shape[0]
+
+    @pl.when(b == 0)
+    def _():
+        left_ref[pl.ds(0, HALO), :] = edge_ref[pl.ds(0, HALO), :]
+        left_ref[pl.ds(HALO, span - 2 * HALO), :] = inner_ref[...]
+        left_ref[pl.ds(span - HALO, HALO), :] = edge_ref[pl.ds(HALO, HALO), :]
+
     left = jnp.dot(left_ref[...], w_ref[b, :, : 2 * group], preferred_element_type=F32).astype(BF)
     own = own_ref[b]
     keys = jnp.concatenate([left[:, :group], own[:, :group]], axis=0)
     values = jnp.concatenate([left[:, group:], own[:, group : 2 * group]], axis=0)
     ctx = heads(own[:, 2 * group :], keys, values, bias_ref[...])
-    settle(ctx, wout_ref, x_ref, gain_ref, valid_ref, x1_ref, g_ref, acc_ref)
-
-
-def attend(left, own, w, w_out, x, bias, gain, valid):
+    settle(ctx, wout_ref, x_ref, gain_ref, valid_ref, x1_ref, g_ref, ctx_ref)
+
+
+def attend(left_inner, left_edge, own, w, w_out, x, bias, gain, valid):
     blocks = w.shape[0]
     span, width = x.shape
     group = width // blocks
@@ -229,20 +232,21 @@
             jax.ShapeDtypeStruct((span, width), BF),
         ),
         in_specs=[
-            whole(span, width),
+            whole(span - 2 * HALO, width),
+            whole(2 * HALO, width),
             pl.BlockSpec(memory_space=pltpu.VMEM),
             pl.BlockSpec(memory_space=pltpu.VMEM),
-            pl.BlockSpec((group, width), lambda b: (b, 0)),
+            whole(width, width),
             whole(span, width),
             whole(2 * span, 128),
             whole(1, width),
             whole(span, 1),
         ],
         out_specs=(whole(span, width), whole(span, width)),
-        scratch_shapes=[pltpu.VMEM((span, width), F32)],
+        scratch_shapes=[pltpu.VMEM((span, width), BF), pltpu.VMEM((span, width), BF)],
         compiler_params=params(),
         name="attend",
-    )(left, in_vmem(own), in_vmem(w), in_hbm(w_out), x, bias, gain, valid)
+    )(left_inner, left_edge, in_vmem(own), in_vmem(w), in_hbm(w_out), x, bias, gain, valid)
 
 
 def taps_over(pad_ref, taps, rows):
@@ -264,16 +268,17 @@
         cols = pl.ds(128 * c, 128)
         pad_ref[...] = g_ref[:, cols].astype(F32)
         silu = taps_over(pad_ref, taps_ref[:, cols], span - 2 * HALO)
-        x_ref[rows, cols] = ((x1_ref[rows, cols] + silu) * valid_ref[rows, :]).astype(BF)
+        x_ref[:, cols] = ((x1_ref[rows, cols] + silu) * valid_ref[rows, :]).astype(BF)
     if len(rest) > 1:
-        rest[0][rows, :] = (normed(x_ref[rows, :].astype(F32)) * gain_ref[...]).astype(BF)
+        rest[0][...] = (normed(x_ref[...].astype(F32)) * gain_ref[...]).astype(BF)
 
 
 def inner(g, x1, taps, valid, gain, last):
     span, width = x1.shape
+    out = jax.ShapeDtypeStruct((span - 2 * HALO, width), BF)
     return pl.pallas_call(
         inner_kernel,
-        out_shape=(jax.ShapeDtypeStruct((span, width), BF),) * (1 if last else 2),
+        out_shape=(out,) * (1 if last else 2),
         scratch_shapes=[pltpu.VMEM((span, 128), F32)],
         compiler_params=params(),
         name="inner",
@@ -282,6 +287,8 @@
 
 def edges_kernel(count, g_ref, low_ref, high_ref, x1_ref, taps_ref, valid_ref, gain_ref, *rest):
     ins, outs, pad_ref = rest[:count], rest[count:-1], rest[-1]
+    if count > 1:
+        outs, edge_ref = outs[:-1], outs[-1]
     span, width = x1_ref.shape
     x_ref = outs[0]
     for at in (0, span - HALO):
@@ -297,10 +304,12 @@
             silu = taps_over(pad_ref, taps_ref[:, cols], HALO)
             x_ref[rows, cols] = ((x1_ref[rows, cols] + silu) * valid_ref[rows, :]).astype(BF)
         if count > 1:
-            outs[1][rows, :] = (normed(x_ref[rows, :].astype(F32)) * gain_ref[...]).astype(BF)
+            h = (normed(x_ref[rows, :].astype(F32)) * gain_ref[...]).astype(BF)
+            outs[1][rows, :] = h
+            edge_ref[pl.ds(HALO if at else 0, HALO), :] = h
     rows = pl.ds(HALO, span - 2 * HALO)
     for source, target in zip(ins, outs):
-        target[rows, :] = source[rows, :]
+        target[rows, :] = source[...]
 
 
 def edges(g, low, high, x1, taps, valid, gain, inners):
@@ -308,7 +317,8 @@
     count = len(inners)
     return pl.pallas_call(
         functools.partial(edges_kernel, count),
-        out_shape=(jax.ShapeDtypeStruct((span, width), BF),) * count,
+        out_shape=(jax.ShapeDtypeStruct((span, width), BF),) * count
+        + (jax.ShapeDtypeStruct((2 * HALO, width), BF),) * (count - 1),
         scratch_shapes=[pltpu.VMEM((3 * HALO, 128), F32)],
         compiler_params=params(),
         name="edges",
@@ -348,9 +358,9 @@
         axis=0,
     )
     stack, frames = lax.optimization_barrier((stack, frames))
-    full = lax.all_gather(stack, ("yh",) + SEQ, axis=0, tiled=True)
+    full = lax.all_gather(stack, ("x", "yh", "yl", "core"), axis=0, tiled=True)
     parts = lax.axis_size("yh") * yls
-    return full.reshape(parts, xs, zs, deep, 3 * group), frames
+    return full.reshape(xs, parts, zs, deep, 3 * group), frames
 
 
 def on_device(frames, arrival, lengths, attn_gain, w_qkv, w_out, conv_gain, conv_kernel):
@@ -382,19 +392,26 @@
     h = head(x, gain_a)
     for step in range(ITERS):
         last = step == ITERS - 1
-        left = along(h, 1)
         if step == 0:
+            left = along(h, 1)
             z = lax.axis_index("z").astype(jnp.int32)[None]
             x1, g, w = opening(z, left, h, w, w_out, x, bias, gain_c, valid)
         else:
-            x1, g = attend(left, project(h, w), w, w_out, x, bias, gain_c, valid)
+            left_edge = along(edge, 1)
+            x1, g = attend(
+                left_inner, left_edge, project(h, w), w, w_out, x, bias, gain_c, valid
+            )
         low = along(g[span - HALO :], 1)
         high = along(g[:HALO], -1)
         inners = inner(g, x1, taps, valid, gain_a, last)
+        if not last:
+            h_inner, low, high = lax.optimization_barrier((inners[1], low, high))
+            inners = (inners[0], h_inner)
+            left_inner = along(h_inner, 1)
         out = edges(g, low, high, x1, taps, valid, gain_a, inners)
         x = out[0]
         if not last:
-            h = out[1]
+            h, edge = out[1:]
     return x[None]
 
 

time: 198 us -> 195 us (0.985)
  waiting for transfers between devices: 88.6 us -> 86.6 us
    ppermute x6 -> x7, waiting for transfers between devices: 32.4 us -> 30.4 us  [along(): return lax.ppermute(value, SEQ, pairs)]
    ppermute x6 -> x7, starting transfers between devices: 19.6 us -> 18.2 us  [along(): return lax.ppermute(value, SEQ, pairs)]
  transfers between devices with their start and end apart: 13 -> 14, of which waited for: 7 -> 8; matrix products, arithmetic and copies ran while one was open for 1% -> 1% of each run, Pallas kernels for 8% -> 8%
where the time goes in v5:
time: 195 us; the launch traced here: 194 us
  waiting for transfers between devices  86.6 us (44%)
  Pallas kernels  47.9 us (25%)
  starting transfers between devices  42 us (22%)
  between operations  13.7 us (7%)
  other arithmetic  2.34 us (1%)
    all_to_all x2, waiting for transfers between devices, on_device(): chunks = lax.all_to_all(chunks, DP, split_axis=0, concat_axis=0, tiled=True)  42.4 us
    ppermute x7, waiting for transfers between devices, along(): return lax.ppermute(value, SEQ, pairs)  30.4 us
    ppermute x7, starting transfers between devices, along(): return lax.ppermute(value, SEQ, pairs)  18.2 us
    pallas_call x1, Pallas kernels, opening(): pl.pallas_call(opening_kernel, grid=(blocks,), out_shape=(jax.ShapeDtypeS...  18.1 us
    all_to_all x2, starting transfers between devices, on_device(): chunks = lax.all_to_all(chunks, DP, split_axis=0, concat_axis=0, tiled=True)  13.8 us
    pallas_call x1, Pallas kernels, attend(): pl.pallas_call(attend_kernel, grid=(blocks,), out_shape=(jax.ShapeDtypeSt...  12.5 us
    ppermute x4, starting transfers between devices, weight_blocks(): came[k] = lax.ppermute(own, ('z', 'core'), pairs)  10 us
    ppermute x4, waiting for transfers between devices, weight_blocks(): came[k] = lax.ppermute(own, ('z', 'core'), pairs)  9.34 us
  transfers between devices with their start and end apart: 14, of which 8 were waited for; matrix products, arithmetic and copies ran while one was open for 1% of the time, Pallas kernels for 8%

profile of v5, /device:TPU:24, one launch (start us, length us, event | category | flops | bytes accessed | tf_op | source)
XLA Modules:
  0.0 194.2 jit_solution(4204732223356790023)
XLA Ops:
  7.4 2.0 %collective-permute-start.1 = (bf16[48,1152]{1,0:T(8,128)(2,1)S(1)}, bf16[48,1152]{1,0:T(8,128)(2,1)S(1)}, u32[]{:S(2)}, u32[]{:S(2)}) collective-permute-start(bf16[48,1152]{1,0:T(8,128)(2,1)S(1)} %pad_maximum_fusion.1), channel_id=1, source_target_pairs={{0,32},{32,64},{64,96},{96,128},{128,160},{160,192},{192,224},{224... | collective-permute-start | bytes 331784 | tf_op jit(solution)/shard_map/ppermute | solution.py:351
  9.4 5.8 %collective-permute-start.2 = (bf16[48,1152]{1,0:T(8,128)(2,1)S(1)}, bf16[48,1152]{1,0:T(8,128)(2,1)S(1)}, u32[]{:S(2)}, u32[]{:S(2)}) collective-permute-start(bf16[48,1152]{1,0:T(8,128)(2,1)S(1)} %pad_maximum_fusion.1), channel_id=1, source_target_pairs={{0,96},{32,128},{64,160},{96,192},{128,224},{160,0},{192,32},{224,... | collective-permute-start | bytes 331784 | tf_op jit(solution)/shard_map/ppermute | solution.py:351
  15.9 1.5 collective-permute-start.3
  17.5 4.9 %collective-permute-done.2 = bf16[48,1152]{1,0:T(8,128)(2,1)S(1)} collective-permute-done((bf16[48,1152]{1,0:T(8,128)(2,1)S(1)}, bf16[48,1152]{1,0:T(8,128)(2,1)S(1)}, u32[]{:S(2)}, u32[]{:S(2)}) %collective-permute-start.2) | collective-permute-done | bytes 110624 | tf_op jit(solution)/shard_map/ppermute | solution.py:351
  22.4 4.5 %collective-permute-done.3 = bf16[48,1152]{1,0:T(8,128)(2,1)S(1)} collective-permute-done((bf16[48,1152]{1,0:T(8,128)(2,1)S(1)}, bf16[48,1152]{1,0:T(8,128)(2,1)S(1)}, u32[]{:S(2)}, u32[]{:S(2)}) %collective-permute-start.3) | collective-permute-done | bytes 110624 | tf_op jit(solution)/shard_map/ppermute | solution.py:351
  27.7 7.6 %all-to-all-start = ((bf16[16,16,1536]{2,1,0:T(8,128)(2,1)}), bf16[16,16,1536]{2,1,0:T(8,128)(2,1)S(1)}, u32[]{:S(2)}, u32[]{:S(2)}) async-start(bf16[16,16,1536]{2,1,0:T(8,128)(2,1)} %bitcast.11), calls=%async_computation | async-start | bytes 1572864 | tf_op jit(solution)/shard_map/all_to_all | solution.py:375
  35.3 21.4 %all-to-all-done.in_ref = bf16[16,16,1536]{2,1,0:T(8,128)(2,1)S(1)} async-done(((bf16[16,16,1536]{2,1,0:T(8,128)(2,1)}), bf16[16,16,1536]{2,1,0:T(8,128)(2,1)S(1)}, u32[]{:S(2)}, u32[]{:S(2)}) %all-to-all-start) | async-done | bytes 786464 | tf_op jit(solution)/shard_map/all_to_all | solution.py:375
  58.2 6.3 %all-to-all-start.1 = ((bf16[16,16,1536]{2,1,0:T(8,128)(2,1)}), bf16[16,16,1536]{2,1,0:T(8,128)(2,1)S(1)}, u32[]{:S(2)}, u32[]{:S(2)}) async-start(bf16[16,16,1536]{2,1,0:T(8,128)(2,1)} %pick.1), calls=%async_computation.1 | async-start | bytes 1572864 | tf_op jit(solution)/shard_map/all_to_all | solution.py:377
  64.5 21.0 %all-to-all-done.1 = bf16[16,16,1536]{2,1,0:T(8,128)(2,1)S(1)} async-done(((bf16[16,16,1536]{2,1,0:T(8,128)(2,1)}), bf16[16,16,1536]{2,1,0:T(8,128)(2,1)S(1)}, u32[]{:S(2)}, u32[]{:S(2)}) %all-to-all-start.1) | async-done | bytes 786464 | tf_op jit(solution)/shard_map/all_to_all | solution.py:377
  86.0 1.9 collective-permute-start.4
  90.0 23.0 %collective-permute-done.4.left_ref = bf16[256,1536]{1,0:T(8,128)(2,1)S(1)} collective-permute-done((bf16[256,1536]{1,0:T(8,128)(2,1)S(1)}, bf16[256,1536]{1,0:T(8,128)(2,1)S(1)}, u32[]{:S(2)}, u32[]{:S(2)}) %collective-permute-start.4) | collective-permute-done | bytes 786464 | tf_op jit(solution)/shard_map/ppermute | solution.py:331
  113.0 4.5 %all-gather.2.cloned.1.call-done = bf16[6144,1152]{1,0:T(8,128)(2,1)} async-done(((bf16[192,1152]{1,0:T(8,128)(2,1)}), bf16[6144,1152]{1,0:T(8,128)(2,1)}) %all-gather.2.cloned.1.call-update) | async-done | bytes 14155792 | tf_op jit(solution)/shard_map/all_gather | solution.py:361
  117.5 18.1 %opening.1 = (f32[256,1536]{1,0:T(8,128)S(1)}, bf16[256,1536]{1,0:T(8,128)(2,1)S(1)}, bf16[4,1536,1152]{2,1,0:T(8,128)(2,1)S(1)}) custom-call(s32[1]{0:T(128)} %bitcast.z_ref, bf16[256,1536]{1,0:T(8,128)(2,1)S(1)} %collective-permute-done.4.left_ref, bf16[256,1536]{1,0:T(8,128)(2,1)S(1)} %head.1.h_ref, bf16[4,4,8,48,1152]{4,3,2,1,0:T(8,128)(2,1)} %bitcast.10, ...), custom_call_target="tpu_custom_call" | custom-call | tf_op jit(solution)/shard_map/opening/pallas_call | solution.py:171
  135.7 2.2 %collective-permute-start.5 = (bf16[16,1536]{1,0:T(8,128)(2,1)S(1)}, bf16[16,1536]{1,0:T(8,128)(2,1)S(1)}, u32[]{:S(2)}, u32[]{:S(2)}) collective-permute-start(bf16[16,1536]{1,0:T(8,128)(2,1)S(1)} %get-tuple-element.41), channel_id=1, source_target_pairs={{0,1},{1,2},{2,3},{3,4},{4,5},{5,6},{6,7},{7,8},{8,9},{9,10},{10,1... | collective-permute-start | bytes 147464 | tf_op jit(solution)/shard_map/ppermute | solution.py:331
  137.8 5.7 %collective-permute-start.6 = (bf16[16,1536]{1,0:T(8,128)(2,1)S(1)}, bf16[16,1536]{1,0:T(8,128)(2,1)S(1)}, u32[]{:S(2)}, u32[]{:S(2)}) collective-permute-start(bf16[16,1536]{1,0:T(8,128)(2,1)S(1)} %get-tuple-element.40), channel_id=1, source_target_pairs={{1,0},{2,1},{3,2},{4,3},{5,4},{6,5},{7,6},{8,7},{9,8},{10,9},{11,1... | collective-permute-start | bytes 147464 | tf_op jit(solution)/shard_map/ppermute | solution.py:331
  143.6 4.8 %inner.2 = (bf16[224,1536]{1,0:T(8,128)(2,1)S(1)}, bf16[224,1536]{1,0:T(8,128)(2,1)S(1)}) custom-call(bf16[256,1536]{1,0:T(8,128)(2,1)S(1)} %get-tuple-element.22.g_ref, f32[256,1536]{1,0:T(8,128)S(1)} %get-tuple-element.23.x1_ref, f32[32,1536]{1,0:T(8,128)S(1)} %pad.4.taps_ref, f32[256,1]{1,0:T(8,128)S(1)} %fusion.valid_ref, ...), custom_call_target="tpu_custom_call" | custom-call | tf_op jit(solution)/shard_map/inner/pallas_call | solution.py:279
  148.4 1.9 collective-permute-start.7
  151.2 1.9 collective-permute-start.8
  153.2 4.2 %project.1.own_ref = bf16[4,256,1152]{2,1,0:T(8,128)(2,1)S(1)} custom-call(bf16[256,1536]{1,0:T(8,128)(2,1)S(1)} %get-tuple-element.30.h_ref, bf16[4,1536,1152]{2,1,0:T(8,128)(2,1)S(1)} %get-tuple-element.31.w_ref), custom_call_target="tpu_custom_call" | custom-call | tf_op jit(solution)/shard_map/project/pallas_call | solution.py:80
  157.4 6.4 %collective-permute-done.8.edge_ref = bf16[32,1536]{1,0:T(8,128)(2,1)S(1)} collective-permute-done((bf16[32,1536]{1,0:T(8,128)(2,1)S(1)}, bf16[32,1536]{1,0:T(8,128)(2,1)S(1)}, u32[]{:S(2)}, u32[]{:S(2)}) %collective-permute-start.8) | collective-permute-done | bytes 98336 | tf_op jit(solution)/shard_map/ppermute | solution.py:331
  163.8 12.5 %attend.1 = (f32[256,1536]{1,0:T(8,128)S(1)}, bf16[256,1536]{1,0:T(8,128)(2,1)S(1)}) custom-call(bf16[224,1536]{1,0:T(8,128)(2,1)S(1)} %collective-permute-done.7.inner_ref, bf16[32,1536]{1,0:T(8,128)(2,1)S(1)} %collective-permute-done.8.edge_ref, bf16[4,256,1152]{2,1,0:T(8,128)(2,1)S(1)} %project.1.own_ref, ...), custom_call_target="tpu_custom_call" | custom-call | tf_op jit(solution)/shard_map/attend/pallas_call | solution.py:227
  176.3 1.9 collective-permute-start.10
  178.3 2.6 %collective-permute-start.9 = (bf16[16,1536]{1,0:T(8,128)(2,1)S(1)}, bf16[16,1536]{1,0:T(8,128)(2,1)S(1)}, u32[]{:S(2)}, u32[]{:S(2)}) collective-permute-start(bf16[16,1536]{1,0:T(8,128)(2,1)S(1)} %get-tuple-element.39), channel_id=1, source_target_pairs={{0,1},{1,2},{2,3},{3,4},{4,5},{5,6},{6,7},{7,8},{8,9},{9,10},{10,1... | collective-permute-start | bytes 147464 | tf_op jit(solution)/shard_map/ppermute | solution.py:331
  180.9 3.8 %inner.3.rest_0_ = bf16[224,1536]{1,0:T(8,128)(2,1)S(1)} custom-call(bf16[256,1536]{1,0:T(8,128)(2,1)S(1)} %get-tuple-element.33.g_ref, f32[256,1536]{1,0:T(8,128)S(1)} %get-tuple-element.34.x1_ref, f32[32,1536]{1,0:T(8,128)S(1)} %pad.4.taps_ref, f32[256,1]{1,0:T(8,128)S(1)} %fusion.valid_ref, f32[1,1536]{1,0:T(1,128)S(1)} %broadcast_in_dim.44.gain_ref), custom_call_target="tpu_custom_call" | custom-call | tf_op jit(solution)/shard_map/inner/pallas_call | solution.py:279
  (41 shorter events, 10.1 us)
Async XLA Ops:
  6.5 28.8 %copy-start = (s32[16,16]{1,0:T(8,128)S(1)}, s32[16,16]{1,0:T(8,128)}, u32[]{:S(2)}) copy-start(s32[16,16]{1,0:T(8,128)} %param.9) | copy-start | bytes 3076
  6.5 57.9 %copy-start.2 = (f32[1536]{0:T(1024)S(1)}, f32[1536]{0:T(1024)}, u32[]{:S(2)}) copy-start(f32[1536]{0:T(1024)} %param.11) | copy-start | bytes 18436
  6.5 81.4 %copy-start.3 = (f32[1536]{0:T(1024)S(1)}, f32[1536]{0:T(1024)}, u32[]{:S(2)}) copy-start(f32[1536]{0:T(1024)} %param.14) | copy-start | bytes 18436
  6.5 81.4 %copy-start.4 = (s32[16]{0:T(128)S(1)}, s32[16]{0:T(128)}, u32[]{:S(2)}) copy-start(s32[16]{0:T(128)} %param.10) | copy-start | bytes 196
  6.5 111.0 %all-gather.2.cloned.1.call-start = ((), (), s32[]{:S(2)}) async-start(), calls=%async_computation.2 | async-start | bytes 14598144 | tf_op jit(solution)/shard_map/all_gather | solution.py:361
  7.4 10.0 %collective-permute-start.1 = (bf16[48,1152]{1,0:T(8,128)(2,1)S(1)}, bf16[48,1152]{1,0:T(8,128)(2,1)S(1)}, u32[]{:S(2)}, u32[]{:S(2)}) collective-permute-start(bf16[48,1152]{1,0:T(8,128)(2,1)S(1)} %pad_maximum_fusion.1), channel_id=1, source_target_pairs={{0,32},{32,64},{64,96},{96,128},{128,160},{160,192},{192,224},{224... | collective-permute-start | bytes 331784 | tf_op jit(solution)/shard_map/ppermute | solution.py:351
  9.4 12.9 %collective-permute-start.2 = (bf16[48,1152]{1,0:T(8,128)(2,1)S(1)}, bf16[48,1152]{1,0:T(8,128)(2,1)S(1)}, u32[]{:S(2)}, u32[]{:S(2)}) collective-permute-start(bf16[48,1152]{1,0:T(8,128)(2,1)S(1)} %pad_maximum_fusion.1), channel_id=1, source_target_pairs={{0,96},{32,128},{64,160},{96,192},{128,224},{160,0},{192,32},{224,... | collective-permute-start | bytes 331784 | tf_op jit(solution)/shard_map/ppermute | solution.py:351
  15.3 7.1 %collective-permute-start = (bf16[48,1152]{1,0:T(8,128)(2,1)S(1)}, bf16[48,1152]{1,0:T(8,128)(2,1)S(1)}, u32[]{:S(2)}, u32[]{:S(2)}) collective-permute-start(bf16[48,1152]{1,0:T(8,128)(2,1)S(1)} %pad_maximum_fusion.1), channel_id=1, source_target_pairs={{1,129},{33,161},{65,193},{97,225},{129,1},{161,33},{193,65},{225,... | collective-permute-start | bytes 331784 | tf_op jit(solution)/shard_map/ppermute | solution.py:351
  15.9 11.0 %collective-permute-start.3 = (bf16[48,1152]{1,0:T(8,128)(2,1)S(1)}, bf16[48,1152]{1,0:T(8,128)(2,1)S(1)}, u32[]{:S(2)}, u32[]{:S(2)}) collective-permute-start(bf16[48,1152]{1,0:T(8,128)(2,1)S(1)} %pad_maximum_fusion.1), channel_id=1, source_target_pairs={{0,64},{32,96},{64,128},{96,160},{128,192},{160,224},{192,0},{224,... | collective-permute-start | bytes 331784 | tf_op jit(solution)/shard_map/ppermute | solution.py:351
  27.7 29.0 %all-to-all-start = ((bf16[16,16,1536]{2,1,0:T(8,128)(2,1)}), bf16[16,16,1536]{2,1,0:T(8,128)(2,1)S(1)}, u32[]{:S(2)}, u32[]{:S(2)}) async-start(bf16[16,16,1536]{2,1,0:T(8,128)(2,1)} %bitcast.11), calls=%async_computation | async-start | bytes 1572864 | tf_op jit(solution)/shard_map/all_to_all | solution.py:375
  58.2 27.3 %all-to-all-start.1 = ((bf16[16,16,1536]{2,1,0:T(8,128)(2,1)}), bf16[16,16,1536]{2,1,0:T(8,128)(2,1)S(1)}, u32[]{:S(2)}, u32[]{:S(2)}) async-start(bf16[16,16,1536]{2,1,0:T(8,128)(2,1)} %pick.1), calls=%async_computation.1 | async-start | bytes 1572864 | tf_op jit(solution)/shard_map/all_to_all | solution.py:377
  86.0 27.0 %collective-permute-start.4 = (bf16[256,1536]{1,0:T(8,128)(2,1)S(1)}, bf16[256,1536]{1,0:T(8,128)(2,1)S(1)}, u32[]{:S(2)}, u32[]{:S(2)}) collective-permute-start(bf16[256,1536]{1,0:T(8,128)(2,1)S(1)} %head.1.h_ref), channel_id=1, source_target_pairs={{0,1},{1,2},{2,3},{3,4},{4,5},{5,6},{6,7},{7,8},{8,9},{9,10},{10,1... | collective-permute-start | bytes 2359304 | tf_op jit(solution)/shard_map/ppermute | solution.py:331
  117.5 26.0 %copy-start.1 = (f32[31,1536]{1,0:T(8,128)S(1)}, f32[31,1536]{1,0:T(8,128)}, u32[]{:S(2)}) copy-start(f32[31,1536]{1,0:T(8,128)} %param.15) | copy-start | bytes 571396
  135.7 12.7 %collective-permute-start.5 = (bf16[16,1536]{1,0:T(8,128)(2,1)S(1)}, bf16[16,1536]{1,0:T(8,128)(2,1)S(1)}, u32[]{:S(2)}, u32[]{:S(2)}) collective-permute-start(bf16[16,1536]{1,0:T(8,128)(2,1)S(1)} %get-tuple-element.41), channel_id=1, source_target_pairs={{0,1},{1,2},{2,3},{3,4},{4,5},{5,6},{6,7},{7,8},{8,9},{9,10},{10,1... | collective-permute-start | bytes 147464 | tf_op jit(solution)/shard_map/ppermute | solution.py:331
  137.8 10.5 %collective-permute-start.6 = (bf16[16,1536]{1,0:T(8,128)(2,1)S(1)}, bf16[16,1536]{1,0:T(8,128)(2,1)S(1)}, u32[]{:S(2)}, u32[]{:S(2)}) collective-permute-start(bf16[16,1536]{1,0:T(8,128)(2,1)S(1)} %get-tuple-element.40), channel_id=1, source_target_pairs={{1,0},{2,1},{3,2},{4,3},{5,4},{6,5},{7,6},{8,7},{9,8},{10,9},{11,1... | collective-permute-start | bytes 147464 | tf_op jit(solution)/shard_map/ppermute | solution.py:331
  148.4 15.4 %collective-permute-start.7 = (bf16[224,1536]{1,0:T(8,128)(2,1)S(1)}, bf16[224,1536]{1,0:T(8,128)(2,1)S(1)}, u32[]{:S(2)}, u32[]{:S(2)}) collective-permute-start(bf16[224,1536]{1,0:T(8,128)(2,1)S(1)} %get-tuple-element.25.rest_1_), channel_id=1, source_target_pairs={{0,1},{1,2},{2,3},{3,4},{4,5},{5,6},{6,7},{7,8},{8,9},{9,10},{10,1... | collective-permute-start | bytes 2064392 | tf_op jit(solution)/shard_map/ppermute | solution.py:331
  151.2 12.6 %collective-permute-start.8 = (bf16[32,1536]{1,0:T(8,128)(2,1)S(1)}, bf16[32,1536]{1,0:T(8,128)(2,1)S(1)}, u32[]{:S(2)}, u32[]{:S(2)}) collective-permute-start(bf16[32,1536]{1,0:T(8,128)(2,1)S(1)} %get-tuple-element.29), channel_id=1, source_target_pairs={{0,1},{1,2},{2,3},{3,4},{4,5},{5,6},{6,7},{7,8},{8,9},{9,10},{10,1... | collective-permute-start | bytes 294920 | tf_op jit(solution)/shard_map/ppermute | solution.py:331
  176.3 8.4 %collective-permute-start.10 = (bf16[16,1536]{1,0:T(8,128)(2,1)S(1)}, bf16[16,1536]{1,0:T(8,128)(2,1)S(1)}, u32[]{:S(2)}, u32[]{:S(2)}) collective-permute-start(bf16[16,1536]{1,0:T(8,128)(2,1)S(1)} %get-tuple-element.38), channel_id=1, source_target_pairs={{1,0},{2,1},{3,2},{4,3},{5,4},{6,5},{7,6},{8,7},{9,8},{10,9},{11,1... | collective-permute-start | bytes 147464 | tf_op jit(solution)/shard_map/ppermute | solution.py:331
  178.3 7.5 %collective-permute-start.9 = (bf16[16,1536]{1,0:T(8,128)(2,1)S(1)}, bf16[16,1536]{1,0:T(8,128)(2,1)S(1)}, u32[]{:S(2)}, u32[]{:S(2)}) collective-permute-start(bf16[16,1536]{1,0:T(8,128)(2,1)S(1)} %get-tuple-element.39), channel_id=1, source_target_pairs={{0,1},{1,2},{2,3},{3,4},{4,5},{5,6},{6,7},{7,8},{8,9},{9,10},{10,1... | collective-permute-start | bytes 147464 | tf_op jit(solution)/shard_map/ppermute | solution.py:331
Sparse Core Ops, SparseCore 0:
  27.9 89.5 all-gather.1
